TPU v7x, 32 devices: a whole 2x2x4 slice. The times are simulated.
32 devices in a mesh: dp: 8 (over y, x, core), mp: 4 (over z).
Axes of the slice: x: 2, y: 2, z: 4, core: 2. Of those that a mesh axis runs over, the one named last changes fastest.
Arguments:
- tokens: bfloat16 [320, 48, 1024], P('mp', 'dp'), may hold values from -6 to 6
- counts: int32 [48], P('dp'), may hold values from 1 to 256, as said below
- norm_gains: float32 [2, 1024], replicated, may hold values from 0.1 to 1.9
- norm_shifts: float32 [2, 1024], replicated, may hold values from -1 to 1
- qkv_weight: bfloat16 [3, 1024, 1024], P(None, 'dp', 'mp'), may hold values from -0.1875 to 0.1875
- qkv_bias: float32 [2, 1024], P(None, 'mp'), may hold values from -1.5 to 1.5
- proj_weight: bfloat16 [1024, 1024], P('mp', 'dp'), may hold values from -2 to 2
- out_biases: float32 [2, 1024], replicated, may hold values from -1.5 to 1.5
- up_weight: bfloat16 [1024, 4096], P('dp', 'mp'), may hold values from -0.1875 to 0.1875
- up_bias: float32 [4096], P('mp'), may hold values from -1.5 to 1.5
- down_weight: bfloat16 [4096, 1024], P('mp', 'dp'), may hold values from -0.09375 to 0.09375
- cotangent: bfloat16 [320, 48, 1024], P('mp', 'dp'), may hold values from -6 to 6
Outputs:
- block_out: bfloat16 [320, 48, 1024], P('mp', 'dp')
- input_grad: bfloat16 [320, 48, 1024], P('mp', 'dp')
- gains_grad: float32 [2, 1024], replicated
- shifts_grad: float32 [2, 1024], replicated
- qkv_grad: float32 [3, 1024, 1024], P(None, 'dp', 'mp')
- bias_grad: float32 [2, 1024], P(None, 'mp')
- proj_grad: float32 [1024, 1024], P('mp', 'dp')
- outbias_grad: float32 [2, 1024], replicated
- up_grad: float32 [1024, 4096], P('dp', 'mp')
- upbias_grad: float32 [4096], P('mp')
- down_grad: float32 [4096, 1024], P('mp', 'dp')
Inputs may be any that keep to these rules, and one draw needn't show every extreme that they name: `counts`: in each aligned block of 6 images one image has exactly 256 kept tokens.
All inputs are finite; a program needn't handle non-finite values.
Results may differ from a plain program's by a relative error of at most 0.012.
The roundings to bfloat16 on the way count: a program that leaves them out, or rounds other values in their place, can miss the bound.
Values may be sent and summed in bfloat16 or wider, within the bound.
No kernel may reach another device: no remote copies, remote signals or barrier semaphores. Data moves between devices by JAX's collectives and lax.ppermute only.
A program may use at most 128 MiB of HBM per device.

v0:
```python
import jax
import jax.numpy as jnp
from jax import lax
from jax.sharding import PartitionSpec as P

HEAD = 64
BUF = 64


epsilon = 1e-06
masked_score = -1e30


def layer_norm(values, scales, shifts):
    average = jnp.mean(values, axis=-1, keepdims=True)
    centred = values - average
    spread = jnp.mean(centred * centred, axis=-1, keepdims=True)
    return centred * lax.rsqrt(spread + epsilon) * scales + shifts


def gelu_slope(inputs):
    normal_cdf = 0.5 * (1.0 + lax.erf(inputs * 0.7071067811865476))
    density = jnp.exp(-0.5 * inputs * inputs) * 0.3989422804014327
    return normal_cdf + inputs * density


def image_block():
    return 2


def attend(qkv_low, valid_all):
    slot_count, images, per_dev = (qkv_low.shape[1], qkv_low.shape[2], qkv_low.shape[3])
    heads_here = per_dev // HEAD
    image_pair = image_block()
    factor = HEAD ** (-0.5)

    def one_block(block_index, buffers):
        mixed_buf, sums_buf = buffers
        offset = block_index * image_pair
        block_qkv = lax.dynamic_slice_in_dim(qkv_low, offset, image_pair, 2).reshape(
            3, slot_count, image_pair, heads_here, HEAD
        )
        allowed = lax.dynamic_slice_in_dim(valid_all, offset, image_pair, 1)
        scores = (
            jnp.einsum(
                "qbhe,kbhe->bhqk", block_qkv[0], block_qkv[1], preferred_element_type=jnp.float32
            )
            * factor
        )
        scores = jnp.where(jnp.transpose(allowed)[:, None, None, :], scores, masked_score)
        highest = jnp.max(scores, axis=-1, keepdims=True)
        powers = jnp.exp(scores - highest)
        totals = jnp.sum(powers, axis=-1, keepdims=True)
        weights = (powers / totals).astype(jnp.bfloat16)
        mixture = jnp.einsum(
            "bhqk,kbhe->qbhe", weights, block_qkv[2], preferred_element_type=jnp.float32
        )
        mixture = mixture.astype(jnp.bfloat16).reshape(slot_count, image_pair, per_dev)
        mixed_buf = lax.dynamic_update_slice_in_dim(mixed_buf, mixture, offset, 1)
        sums_buf = lax.dynamic_update_slice_in_dim(
            sums_buf, (highest + jnp.log(totals))[..., 0], offset, 0
        )
        return (mixed_buf, sums_buf)

    initial = (
        jnp.zeros((slot_count, images, per_dev), jnp.bfloat16),
        jnp.zeros((images, heads_here, slot_count), jnp.float32),
    )
    return lax.fori_loop(0, images // image_pair, one_block, initial)


def attend_back(qkv_low, logsums, grad_mixture, valid_all):
    slot_count, images, per_dev = (qkv_low.shape[1], qkv_low.shape[2], qkv_low.shape[3])
    heads_here = per_dev // HEAD
    image_pair = image_block()
    factor = HEAD ** (-0.5)

    def one_block(block_index, grad_buf):
        offset = block_index * image_pair
        block_qkv = lax.dynamic_slice_in_dim(qkv_low, offset, image_pair, 2).reshape(
            3, slot_count, image_pair, heads_here, HEAD
        )
        allowed = lax.dynamic_slice_in_dim(valid_all, offset, image_pair, 1)
        block_grad = lax.dynamic_slice_in_dim(grad_mixture, offset, image_pair, 1).reshape(
            slot_count, image_pair, heads_here, HEAD
        )
        block_sums = lax.dynamic_slice_in_dim(logsums, offset, image_pair, 0)
        scores = (
            jnp.einsum(
                "qbhe,kbhe->bhqk", block_qkv[0], block_qkv[1], preferred_element_type=jnp.float32
            )
            * factor
        )
        scores = jnp.where(jnp.transpose(allowed)[:, None, None, :], scores, masked_score)
        weights = jnp.exp(scores - block_sums[..., None])
        grad_probs = jnp.einsum(
            "qbhe,kbhe->bhqk", block_grad, block_qkv[2], preferred_element_type=jnp.float32
        )
        row_dot = jnp.sum(weights * grad_probs, axis=-1, keepdims=True)
        grad_scores = (weights * (grad_probs - row_dot)).astype(jnp.bfloat16)
        grad_query = (
            jnp.einsum(
                "bhqk,kbhe->qbhe", grad_scores, block_qkv[1], preferred_element_type=jnp.float32
            )
            * factor
        )
        grad_key = (
            jnp.einsum(
                "bhqk,qbhe->kbhe", grad_scores, block_qkv[0], preferred_element_type=jnp.float32
            )
            * factor
        )
        grad_value = jnp.einsum(
            "bhqk,qbhe->kbhe",
            weights.astype(jnp.bfloat16),
            block_grad,
            preferred_element_type=jnp.float32,
        )
        stacked = (
            jnp.stack([grad_query, grad_key, grad_value])
            .astype(jnp.bfloat16)
            .reshape(3, slot_count, image_pair, per_dev)
        )
        return lax.dynamic_update_slice_in_dim(grad_buf, stacked, offset, 2)

    initial = jnp.zeros((3, slot_count, images, per_dev), jnp.bfloat16)
    return lax.fori_loop(0, images // image_pair, one_block, initial)


def local(
    tokens,
    counts,
    norm_gains,
    norm_shifts,
    qkv_weight,
    qkv_bias,
    proj_weight,
    out_biases,
    up_weight,
    up_bias,
    down_weight,
    cotangent,
):
    local_slots, images, model_width = tokens.shape
    group_size = lax.axis_size("mp")
    slot_count = local_slots * group_size
    mp_index = lax.axis_index("mp")
    row_offset = mp_index * local_slots
    slot_ids = jnp.arange(slot_count, dtype=jnp.int32)
    valid_all = slot_ids[:, None] < BUF + counts[None, :]
    keep_mine = lax.dynamic_slice_in_dim(valid_all, row_offset, local_slots, 0).astype(jnp.float32)[
        :, :, None
    ]
    qkv_full, proj_full, up_full, down_full = (
        lax.all_gather(qkv_weight, "dp", axis=1, tiled=True),
        lax.all_gather(proj_weight, "dp", axis=1, tiled=True),
        lax.all_gather(up_weight, "dp", axis=0, tiled=True),
        lax.all_gather(down_weight, "dp", axis=1, tiled=True),
    )
    per_dev = qkv_full.shape[2]
    hidden_dev = up_full.shape[1]
    inputs32 = tokens.astype(jnp.float32)
    normed_one, norm_one_back = jax.vjp(layer_norm, inputs32, norm_gains[0], norm_shifts[0])
    normed_all = lax.all_gather(normed_one.astype(jnp.bfloat16), "mp", axis=0, tiled=True)
    projected = jnp.einsum(
        "sbd,tde->tsbe", normed_all, qkv_full, preferred_element_type=jnp.float32
    )
    bias_rows = jnp.stack([qkv_bias[0], jnp.zeros_like(qkv_bias[0]), qkv_bias[1]])
    qkv_low = (projected + bias_rows[:, None, None, :]).astype(jnp.bfloat16)
    mixture, logsums = attend(qkv_low, valid_all)
    rows_in = mixture
    attended = lax.psum_scatter(
        jnp.einsum("sbe,ed->sbd", rows_in, proj_full, preferred_element_type=jnp.float32),
        "mp",
        scatter_dimension=0,
        tiled=True,
    )
    hidden = inputs32 + attended + out_biases[0]
    normed_two, norm_two_back = jax.vjp(layer_norm, hidden, norm_gains[1], norm_shifts[1])
    mlp_in = lax.all_gather(normed_two.astype(jnp.bfloat16), "mp", axis=0, tiled=True)
    up_pre = (
        jnp.einsum("sbd,df->sbf", mlp_in, up_full, preferred_element_type=jnp.float32) + up_bias
    )
    up_act = jax.nn.gelu(up_pre, approximate=False).astype(jnp.bfloat16)
    rows_in = up_act
    branch = lax.psum_scatter(
        jnp.einsum("sbf,fd->sbd", rows_in, down_full, preferred_element_type=jnp.float32).astype(
            jnp.bfloat16
        ),
        "mp",
        scatter_dimension=0,
        tiled=True,
    ).astype(jnp.float32)
    block_out = ((hidden + branch + out_biases[1]) * keep_mine).astype(jnp.bfloat16)
    grad_out = cotangent.astype(jnp.float32) * keep_mine
    grad_branch = lax.all_gather(grad_out.astype(jnp.bfloat16), "mp", axis=0, tiled=True)
    qkv_full, proj_full, up_full, down_full = (
        lax.all_gather(qkv_weight, "dp", axis=1, tiled=True),
        lax.all_gather(proj_weight, "dp", axis=1, tiled=True),
        lax.all_gather(up_weight, "dp", axis=0, tiled=True),
        lax.all_gather(down_weight, "dp", axis=1, tiled=True),
    )
    down_grad = jnp.einsum("sbf,sbd->fd", up_act, grad_branch, preferred_element_type=jnp.float32)
    grad_act = jnp.einsum("sbd,fd->sbf", grad_branch, down_full, preferred_element_type=jnp.float32)
    grad_pre = (grad_act * gelu_slope(up_pre)).astype(jnp.bfloat16)
    up_grad = jnp.einsum("sbd,sbf->df", mlp_in, grad_pre, preferred_element_type=jnp.float32)
    upbias_part = jnp.sum(grad_pre, axis=(0, 1), dtype=jnp.float32)
    rows_in = grad_pre
    grad_norm_two = lax.psum_scatter(
        jnp.einsum("sbf,df->sbd", rows_in, up_full, preferred_element_type=jnp.float32),
        "mp",
        scatter_dimension=0,
        tiled=True,
    )
    grad_hidden_part, gain_two, shift_two = norm_two_back(grad_norm_two)
    grad_hidden = grad_out + grad_hidden_part
    grad_attended = lax.all_gather(grad_hidden.astype(jnp.bfloat16), "mp", axis=0, tiled=True)
    proj_grad = jnp.einsum(
        "sbe,sbd->ed", mixture, grad_attended, preferred_element_type=jnp.float32
    )
    grad_mixture = jnp.einsum(
        "sbd,ed->sbe", grad_attended, proj_full, preferred_element_type=jnp.float32
    ).astype(jnp.bfloat16)
    grad_qkv = attend_back(qkv_low, logsums, grad_mixture, valid_all)
    qkv_grad = jnp.einsum("sbd,tsbe->tde", normed_all, grad_qkv, preferred_element_type=jnp.float32)
    bias_part = jnp.stack(
        [
            jnp.sum(grad_qkv[0], axis=(0, 1), dtype=jnp.float32),
            jnp.sum(grad_qkv[2], axis=(0, 1), dtype=jnp.float32),
        ]
    )
    rows_in = grad_qkv
    grad_norm_one = lax.psum_scatter(
        jnp.einsum("tsbe,tde->sbd", rows_in, qkv_full, preferred_element_type=jnp.float32),
        "mp",
        scatter_dimension=0,
        tiled=True,
    )
    grad_input_part, gain_one, shift_one = norm_one_back(grad_norm_one)
    input_grad = (grad_hidden + grad_input_part).astype(jnp.bfloat16)
    qkv_owned, proj_owned, up_owned, down_owned = (
        lax.psum_scatter(qkv_grad, "dp", scatter_dimension=1, tiled=True),
        lax.psum_scatter(proj_grad, "dp", scatter_dimension=1, tiled=True),
        lax.psum_scatter(up_grad, "dp", scatter_dimension=0, tiled=True),
        lax.psum_scatter(down_grad, "dp", scatter_dimension=1, tiled=True),
    )
    bias_wide = lax.dynamic_update_slice_in_dim(
        jnp.zeros((2, per_dev * group_size), jnp.float32), bias_part, mp_index * per_dev, 1
    )
    upbias_wide = lax.dynamic_update_slice_in_dim(
        jnp.zeros((hidden_dev * group_size,), jnp.float32), upbias_part, mp_index * hidden_dev, 0
    )
    gain_rows = jnp.stack([gain_one, gain_two])
    shift_rows = jnp.stack([shift_one, shift_two])
    outbias_rows = jnp.stack([jnp.sum(grad_hidden, axis=(0, 1)), jnp.sum(grad_out, axis=(0, 1))])
    gains_grad, shifts_grad, outbias_grad, bias_sum, upbias_sum = lax.psum(
        (gain_rows, shift_rows, outbias_rows, bias_wide, upbias_wide), ("dp", "mp")
    )
    bias_grad = lax.dynamic_slice_in_dim(bias_sum, mp_index * per_dev, per_dev, 1)
    upbias_grad = lax.dynamic_slice_in_dim(upbias_sum, mp_index * hidden_dev, hidden_dev, 0)
    return (
        block_out,
        input_grad,
        gains_grad,
        shifts_grad,
        qkv_owned,
        bias_grad,
        proj_owned,
        outbias_grad,
        up_owned,
        upbias_grad,
        down_owned,
    )


def solution(mesh):
    return jax.shard_map(
        local,
        mesh=mesh,
        in_specs=(
            P("mp", "dp", None),
            P("dp"),
            P(),
            P(),
            P(None, "dp", "mp"),
            P(None, "mp"),
            P("mp", "dp"),
            P(),
            P("dp", "mp"),
            P("mp"),
            P("mp", "dp"),
            P("mp", "dp", None),
        ),
        out_specs=(
            P("mp", "dp", None),
            P("mp", "dp", None),
            P(),
            P(),
            P(None, "dp", "mp"),
            P(None, "mp"),
            P("mp", "dp"),
            P(),
            P("dp", "mp"),
            P("mp"),
            P("mp", "dp"),
        ),
        check_vma=False,
    )
```

profile of v0, /device:TPU:0, one launch (start us, length us, event | category | flops | bytes accessed | tf_op | source)
XLA Modules:
  0.0 1210.8 jit_solution(12188046485732918140)
XLA Ops:
  13.8 2.6 fusion.46
  16.6 13.0 %all_gather.30 = bf16[256,1024]{1,0:T(8,128)(2,1)} all-gather(bf16[256,128]{1,0:T(8,128)(2,1)S(1)} %copy-done.19), channel_id=1, replica_groups=mesh['dp'=8,'mp'=4] {'dp'}, dimensions={1}, use_global_device_ids=true | all-gather | bytes 589824 | tf_op jit(solution)/shard_map/all_gather | solution.py:156
  29.7 9.3 all-gather.10.cloned.1.call-done
  39.1 78.6 %all-gather.8.cloned.1.call-done = bf16[320,6,1024]{2,0,1:T(8,128)(2,1)} async-done(((bf16[80,6,1024]{2,0,1:T(8,128)(2,1)}), bf16[320,6,1024]{2,0,1:T(8,128)(2,1)}) %all-gather.8.cloned.1.call-update) | async-done | bytes 3932176 | tf_op jit(solution)/shard_map/all_gather | solution.py:164
  117.7 7.4 fusion.32
  125.1 4.4 copy.27
  131.3 14.5 %while.28 = (s32[]{:T(128)}, bf16[320,6,256]{0,2,1:T(8,128)(2,1)}, f32[6,4,320]{2,1,0:T(4,128)}, bf16[3,320,6,256]{1,3,2,0:T(8,128)(2,1)S(1)}, pred[320,6]{0,1:T...) while((s32[]{:T(128)}, bf16[320,6,256]{0,2,1:T(8,128)(2,1)}, ...), condition=%wide.region_5.6_spmd, body=%wide.region_2.5_spmd.sunk | while | flops 219706880 | bytes 13915467 | solution.py:69
  145.8 5.7 fusion.64
  153.5 133.0 %reduce-scatter.9.cloned.1.call-done = f32[80,6,1024]{2,0,1:T(8,128)} async-done(((f32[320,6,1024]{2,0,1:T(8,128)}), f32[80,6,1024]{2,0,1:T(8,128)}) %reduce-scatter.9.cloned.1.call-update) | async-done | bytes 1966096 | tf_op jit(solution)/shard_map/reduce_scatter | solution.py:172
  286.5 2.1 fusion.72
  289.9 2.0 add_convert_fusion.2
  292.7 2.4 fusion.52
  295.4 21.3 %all-gather.14.cloned.1.call-done = bf16[1024,1024]{1,0:T(8,128)(2,1)} async-done(((bf16[128,1024]{1,0:T(8,128)(2,1)}), bf16[1024,1024]{1,0:T(8,128)(2,1)}) %all-gather.14.cloned.1.call-update) | async-done | bytes 2097168 | tf_op jit(solution)/shard_map/all_gather | solution.py:157
  316.7 78.5 %all-gather.12.cloned.1.call-done = bf16[320,6,1024]{2,0,1:T(8,128)(2,1)} async-done(((bf16[80,6,1024]{2,0,1:T(8,128)(2,1)}), bf16[320,6,1024]{2,0,1:T(8,128)(2,1)}) %all-gather.12.cloned.1.call-update) | async-done | bytes 3932176 | tf_op jit(solution)/shard_map/all_gather | solution.py:180
  395.1 13.3 %fusion.54 = (u8[320,1024]{1,0:T(8,128)(4,1)}, u8[320,1024]{1,0:T(8,128)(4,1)}, f32[320,6,1024]{2,0,1:T(8,128)}) fusion(f32[1024]{0:T(1024)} %param.25, bf16[320,6,1024]{2,0,1:T(8,128)(2,1)} %all-gather.12.cloned.1.call-done, bf16[1024,1024]{1,0:T(8,128)(2,1)} %all-gather.14.cloned.1.call-done), kind=kOutput, calls=%fused_computation.108 | convolution fusion | flops 4053401600 | bytes 14553088 | tf_op jit(solution)/shard_map/sbd,df->sbf/dot_general | solution.py:182
  408.4 15.2 %all-gather.16.cloned.1.call-done = bf16[1024,1024]{1,0:T(8,128)(2,1)} async-done(((bf16[1024,128]{1,0:T(8,128)(2,1)}), bf16[1024,1024]{1,0:T(8,128)(2,1)}) %all-gather.16.cloned.1.call-update) | async-done | bytes 2097168 | tf_op jit(solution)/shard_map/all_gather | solution.py:158
  423.7 78.6 %all-gather.18.cloned.1.call-done = bf16[320,6,1024]{2,0,1:T(8,128)(2,1)} async-done(((bf16[80,6,1024]{2,0,1:T(8,128)(2,1)}), bf16[320,6,1024]{2,0,1:T(8,128)(2,1)}) %all-gather.18.cloned.1.call-update) | async-done | bytes 3932176 | tf_op jit(solution)/shard_map/all_gather | solution.py:196
  502.3 10.9 convert_reduce_fusion
  513.2 2.0 copy-done.36
  515.2 6.5 fusion.41
  521.7 11.2 reduce-scatter.11.cloned.1.call-start
  533.0 19.6 %fusion.15 = bf16[320,6,1024]{2,0,1:T(8,128)(2,1)S(1)} fusion(f32[320,6,1024]{2,0,1:T(8,128)} %get-tuple-element.304, f32[1024]{0:T(1024)} %param.25, u8[320,1024]{1,0:T(8,128)(4,1)} %get-tuple-element.241, u8[320,1024]{1,0:T(8,128)(4,1)} %get-tuple-element.240), kind=kLoop, calls=%fused_computation.36 | loop fusion | flops 139591680 | bytes 12455936 | tf_op jit(solution)/shard_map/convert_element_type | solution.py:184
  552.6 1.9 copy-done.8
  554.4 5.7 convolution_convert_fusion
  560.2 96.4 %reduce-scatter.13.cloned.1.call-done = f32[80,6,1024]{2,0,1:T(8,128)} async-done(((f32[320,6,1024]{2,0,1:T(8,128)}), f32[80,6,1024]{2,0,1:T(8,128)}) %reduce-scatter.13.cloned.1.call-update) | async-done | bytes 1966096 | tf_op jit(solution)/shard_map/reduce_scatter | solution.py:209
  656.7 3.5 multiply_reduce_fusion.1
  660.8 71.5 %reduce-scatter.11.cloned.1.call-done = bf16[80,6,1024]{2,0,1:T(8,128)(2,1)} async-done(((bf16[320,6,1024]{2,0,1:T(8,128)(2,1)}), bf16[80,6,1024]{2,0,1:T(8,128)(2,1)}) %reduce-scatter.11.cloned.1.call-update) | async-done | bytes 983056 | tf_op jit(solution)/shard_map/reduce_scatter | solution.py:186
  732.2 4.3 fusion.71
  737.9 2.0 fusion.66
  740.0 76.9 %all-gather.20.cloned.1.call-done = bf16[320,6,1024]{2,0,1:T(8,128)(2,1)} async-done(((bf16[80,6,1024]{2,0,1:T(8,128)(2,1)}), bf16[320,6,1024]{2,0,1:T(8,128)(2,1)}) %all-gather.20.cloned.1.call-update) | async-done | bytes 3932176 | tf_op jit(solution)/shard_map/all_gather | solution.py:217
  816.8 4.4 convolution_convert_fusion.1
  821.2 2.3 broadcast_in_dim.102
  823.5 36.8 %while.29 = (s32[]{:T(128)}, bf16[3,320,6,256]{1,3,2,0:T(8,128)(2,1)}, bf16[3,320,6,256]{1,3,2,0:T(8,128)(2,1)S(1)}, pred[320,6]{0,1:T(8,128)(4,1)S(1)}, f32[6,4...) while((s32[]{:T(128)}, ...), condition=%wide.region_15.16_spmd, body=%wide.region_13.0_spmd.sunk | while | flops 535426560 | bytes 56954056 | solution.py:127
  825.3 1.7 constant_dynamic-slice_fusion.14
  860.3 8.4 fusion.55
  868.8 7.7 convolution_bitcast_fusion
  876.8 10.4 convolution_bitcast_fusion.2
  887.3 10.3 convolution_bitcast_fusion.1
  900.9 4.8 convolution_bitcast_fusion.3
  905.8 7.9 reduce-scatter.17.cloned.1.call-done
  913.7 1.9 copy.34
  915.6 136.6 %reduce-scatter.15.cloned.1.call-done = f32[80,6,1024]{2,0,1:T(8,128)} async-done(((f32[320,6,1024]{2,0,1:T(8,128)}), f32[80,6,1024]{2,0,1:T(8,128)}) %reduce-scatter.15.cloned.1.call-update) | async-done | bytes 1966096 | tf_op jit(solution)/shard_map/reduce_scatter | solution.py:233
  1052.2 2.2 fusion.70
  1055.5 42.1 %all-reduce = (f32[2,1024]{1,0:T(2,128)}, f32[2,1024]{1,0:T(2,128)}, f32[2,1024]{1,0:T(2,128)S(1)}, f32[2,1024]{1,0:T(2,128)}, f32[4096]{0:T(1024)S(1)}) all-reduce(f32[2,1024]{1,0:T(2,128)S(1)} %get-tuple-element.307, f32[2,1024]{1,0:T(2,128)S(1)} %get-tuple-element.308, ...), channel_id=1, replica_groups=mesh['dp'=8,'mp'=4] {'dp','mp'}, use_global_device_ids=true, to_apply=%region_21.0 | all-reduce | flops 12288 | bytes 98304 | tf_op jit(solution)/shard_map/psum | solution.py:256
  1098.8 3.4 add_convert_fusion.1
  1102.2 6.5 reduce-scatter.21.cloned.1.call-done
  1108.8 55.1 %reduce-scatter.23.cloned.1.call-done = f32[1024,128]{1,0:T(8,128)} async-done(((f32[1024,1024]{1,0:T(8,128)}), f32[1024,128]{1,0:T(8,128)}) %reduce-scatter.23.cloned.1.call-update) | async-done | bytes 524304 | tf_op jit(solution)/shard_map/reduce_scatter | solution.py:245
  1163.9 40.0 %reduce-scatter.19.cloned.1.call-done = f32[256,128]{1,0:T(8,128)} async-done(((f32[256,1024]{1,0:T(8,128)}), f32[256,128]{1,0:T(8,128)}) %reduce-scatter.19.cloned.1.call-update) | async-done | bytes 131088 | tf_op jit(solution)/shard_map/reduce_scatter | solution.py:243
  (205 shorter events, 70.1 us)
Async XLA Ops:
  7.2 9.4 copy-start.19
  7.2 22.4 %copy-start.35 = (s32[6]{0:T(128)S(1)}, s32[6]{0:T(128)}, u32[]{:S(2)}) copy-start(s32[6]{0:T(128)} %param.17) | copy-start | bytes 76
  7.2 22.5 %copy-start.32 = (f32[2,256]{1,0:T(2,128)S(1)}, f32[2,256]{1,0:T(2,128)}, u32[]{:S(2)}) copy-start(f32[2,256]{1,0:T(2,128)} %param.21) | copy-start | bytes 6148
  7.2 31.9 %all-gather.10.cloned.1.call-start = ((), (), s32[]{:S(2)}) async-start(), calls=%async_computation.9 | async-start | bytes 1769472 | tf_op jit(solution)/shard_map/all_gather | solution.py:155
  7.9 109.7 %all-gather.8.cloned.1.call-start = ((), (), s32[]{:S(2)}) async-start(), calls=%async_computation.8 | async-start | bytes 4915200 | tf_op jit(solution)/shard_map/all_gather | solution.py:164
  9.4 108.3 %copy-start.9 = (f32[80,6]{0,1:T(8,128)}, f32[80,6]{0,1:T(8,128)S(1)}, u32[]{:S(2)}) copy-start(f32[80,6]{0,1:T(8,128)S(1)} %broadcast_multiply_fusion.1) | copy-start | bytes 5764
  11.6 106.0 %copy-start.17 = (f32[80,6]{0,1:T(8,128)}, f32[80,6]{0,1:T(8,128)S(1)}, u32[]{:S(2)}) copy-start(f32[80,6]{0,1:T(8,128)S(1)} %fusion.68) | copy-start | bytes 5764
  12.4 105.3 %copy-start.13 = (f32[1,1024]{1,0:T(1,128)}, f32[1,1024]{1,0:T(1,128)S(1)}, u32[]{:S(2)}) copy-start(f32[1,1024]{1,0:T(1,128)S(1)} %get-tuple-element.299) | copy-start | bytes 12292
  12.4 277.4 %copy-start.20 = (f32[1,1024]{1,0:T(1,128)}, f32[1,1024]{1,0:T(1,128)S(1)}, u32[]{:S(2)}) copy-start(f32[1,1024]{1,0:T(1,128)S(1)} %get-tuple-element.298) | copy-start | bytes 12292
  16.4 270.1 %reduce-scatter.9.cloned.1.call-start = ((), (), s32[]{:S(2)}) async-start(), calls=%async_computation.10 | async-start | bytes 9830400 | tf_op jit(solution)/shard_map/reduce_scatter | solution.py:172
  151.5 165.1 %all-gather.14.cloned.1.call-start = ((), (), s32[]{:S(2)}) async-start(), calls=%async_computation.12 | async-start | bytes 2359296 | tf_op jit(solution)/shard_map/all_gather | solution.py:157
  152.1 243.0 %all-gather.12.cloned.1.call-start = ((), (), s32[]{:S(2)}) async-start(), calls=%async_computation.11 | async-start | bytes 4915200 | tf_op jit(solution)/shard_map/all_gather | solution.py:180
  291.9 131.7 %all-gather.16.cloned.1.call-start = ((), (), s32[]{:S(2)}) async-start(), calls=%async_computation.13 | async-start | bytes 2359296 | tf_op jit(solution)/shard_map/all_gather | solution.py:158
  292.5 209.8 %all-gather.18.cloned.1.call-start = ((), (), s32[]{:S(2)}) async-start(), calls=%async_computation.15 | async-start | bytes 4915200 | tf_op jit(solution)/shard_map/all_gather | solution.py:196
  292.7 443.9 %copy-start.15 = (f32[80,6]{0,1:T(8,128)}, f32[80,6]{0,1:T(8,128)S(1)}, u32[]{:S(2)}) copy-start(f32[80,6]{0,1:T(8,128)S(1)} %dynamic-slice_convert_fusion) | copy-start | bytes 5764
  295.1 361.6 %reduce-scatter.13.cloned.1.call-start = ((), (), s32[]{:S(2)}) async-start(), calls=%async_computation.16 | async-start | bytes 9830400 | tf_op jit(solution)/shard_map/reduce_scatter | solution.py:209
  502.3 12.9 %copy-start.33 = (bf16[1024,1024]{1,0:T(8,128)(2,1)S(1)}, bf16[1024,1024]{1,0:T(8,128)(2,1)}, u32[]{:S(2)}) copy-start(bf16[1024,1024]{1,0:T(8,128)(2,1)} %all-gather.14.cloned.1.call-done) | copy-start | bytes 6291460
  521.7 210.5 %reduce-scatter.11.cloned.1.call-start = ((), (), s32[]{:S(2)}) async-start(), calls=%async_computation.14 | async-start | bytes 4915200 | tf_op jit(solution)/shard_map/reduce_scatter | solution.py:186
  532.9 21.5 %copy-start.34 = (bf16[1024,1024]{1,0:T(8,128)(2,1)S(1)}, bf16[1024,1024]{1,0:T(8,128)(2,1)}, u32[]{:S(2)}) copy-start(bf16[1024,1024]{1,0:T(8,128)(2,1)} %all-gather.16.cloned.1.call-done) | copy-start | bytes 6291460
  560.2 256.7 %all-gather.20.cloned.1.call-start = ((), (), s32[]{:S(2)}) async-start(), calls=%async_computation.17 | async-start | bytes 4915200 | tf_op jit(solution)/shard_map/all_gather | solution.py:217
  656.7 3.5 copy-start.24
  732.2 5.6 copy-start.7
  736.5 3.3 copy-start.25
  739.9 173.8 %reduce-scatter.17.cloned.1.call-start = ((), (), s32[]{:S(2)}) async-start(), calls=%async_computation.19 | async-start | bytes 3538944 | tf_op jit(solution)/shard_map/reduce_scatter | solution.py:242
  833.4 2.4 copy-start.1
  833.4 2.4 copy-start.12
  845.6 2.4 copy-start.1
  845.6 2.4 copy-start.12
  857.9 2.4 copy-start.1
  857.9 2.4 copy-start.12
  860.3 8.5 copy-start.6
  868.8 183.5 %reduce-scatter.15.cloned.1.call-start = ((), (), s32[]{:S(2)}) async-start(), calls=%async_computation.18 | async-start | bytes 9830400 | tf_op jit(solution)/shard_map/reduce_scatter | solution.py:233
  876.5 232.2 %reduce-scatter.21.cloned.1.call-start = ((), (), s32[]{:S(2)}) async-start(), calls=%async_computation.21 | async-start | bytes 4718592 | tf_op jit(solution)/shard_map/reduce_scatter | solution.py:244
  887.2 276.7 %reduce-scatter.23.cloned.1.call-start = ((), (), s32[]{:S(2)}) async-start(), calls=%async_computation.22 | async-start | bytes 4718592 | tf_op jit(solution)/shard_map/reduce_scatter | solution.py:245
  897.7 306.2 %reduce-scatter.19.cloned.1.call-start = ((), (), s32[]{:S(2)}) async-start(), calls=%async_computation.20 | async-start | bytes 1179648 | tf_op jit(solution)/shard_map/reduce_scatter | solution.py:243
  900.9 4.8 copy-start.30
  900.9 4.9 copy-start.31
  900.9 151.3 %copy-start.3 = (bf16[80,6,1024]{2,0,1:T(8,128)(2,1)S(1)}, bf16[80,6,1024]{2,0,1:T(8,128)(2,1)}, u32[]{:S(2)}) copy-start(bf16[80,6,1024]{2,0,1:T(8,128)(2,1)} %param.16) | copy-start | bytes 2949124
  900.9 151.3 %copy-start.10 = (f32[80,6]{0,1:T(8,128)S(1)}, f32[80,6]{0,1:T(8,128)}, u32[]{:S(2)}) copy-start(f32[80,6]{0,1:T(8,128)} %copy-done.9) | copy-start | bytes 5764
  900.9 151.3 %copy-start.14 = (f32[1,1024]{1,0:T(1,128)S(1)}, f32[1,1024]{1,0:T(1,128)}, u32[]{:S(2)}) copy-start(f32[1,1024]{1,0:T(1,128)} %copy-done.13) | copy-start | bytes 12292
  905.7 148.8 %copy-start.22 = (f32[80,6]{0,1:T(8,128)S(1)}, f32[80,6]{0,1:T(8,128)}, u32[]{:S(2)}) copy-start(f32[80,6]{0,1:T(8,128)} %copy-done.21) | copy-start | bytes 5764
  905.7 148.8 %copy-start.18 = (f32[80,6]{0,1:T(8,128)S(1)}, f32[80,6]{0,1:T(8,128)}, u32[]{:S(2)}) copy-start(f32[80,6]{0,1:T(8,128)} %copy-done.17) | copy-start | bytes 5764
  905.7 149.7 %copy-start.28 = (f32[1024]{0:T(1024)S(1)}, f32[1024]{0:T(1024)}, u32[]{:S(2)}) copy-start(f32[1024]{0:T(1024)} %get-tuple-element.242) | copy-start | bytes 12292
  905.7 149.8 %copy-start.29 = (f32[1024]{0:T(1024)S(1)}, f32[1024]{0:T(1024)}, u32[]{:S(2)}) copy-start(f32[1024]{0:T(1024)} %get-tuple-element.250) | copy-start | bytes 12292
  905.7 149.8 %copy-start.27 = (f32[2,1024]{1,0:T(2,128)S(1)}, f32[2,1024]{1,0:T(2,128)}, u32[]{:S(2)}) copy-start(f32[2,1024]{1,0:T(2,128)} %pad_maximum_fusion.2) | copy-start | bytes 24580
  905.7 193.1 %copy-start.16 = (f32[80,6]{0,1:T(8,128)S(1)}, f32[80,6]{0,1:T(8,128)}, u32[]{:S(2)}) copy-start(f32[80,6]{0,1:T(8,128)} %copy-done.15) | copy-start | bytes 5764
  905.7 193.1 %copy-start.26 = (f32[80,6]{0,1:T(8,128)S(1)}, f32[80,6]{0,1:T(8,128)}, u32[]{:S(2)}) copy-start(f32[80,6]{0,1:T(8,128)} %copy-done.25) | copy-start | bytes 5764
  1052.2 2.3 copy-start.4
  (12 other events, 14.9 us)
Sparse Core Ops, SparseCore 0:
  9.9 29.0 all-gather.9
  41.2 76.4 all-gather.7
  151.7 134.8 reduce-scatter.8
  288.2 28.3 all-gather.13
  318.7 76.4 all-gather.11
  396.9 26.7 all-gather.15
  425.8 76.4 all-gather.17
  521.8 134.8 reduce-scatter.12
  659.0 73.1 reduce-scatter.10
  740.0 76.7 all-gather.19
  868.9 44.7 reduce-scatter.16
  916.0 136.2 reduce-scatter.14
  1056.5 52.1 reduce-scatter.20
  1112.5 51.3 reduce-scatter.22
  1167.8 36.0 reduce-scatter.18
where the time goes:
time: 1220 us; the launch traced here: 1210 us
  waiting for transfers between devices  907 us (74%)
  matrix products  116 us (10%)
  other arithmetic  61.8 us (5%)
  blocking collectives  55.1 us (5%)
  local copies, waits for them, and re-layouts  43.6 us (4%)
  between operations  14.7 us (1%)
  starting transfers between devices  12.3 us (1%)
    reduce_scatter x1, waiting for transfers between devices, local(): lax.psum_scatter(jnp.einsum('tsbe,tde->sbd', rows_in, qkv_full, preferred...  137 us
    reduce_scatter x1, waiting for transfers between devices, local(): lax.psum_scatter(jnp.einsum('sbe,ed->sbd', rows_in, proj_full, preferred_...  133 us
    reduce_scatter x1, waiting for transfers between devices, local(): lax.psum_scatter(jnp.einsum('sbf,df->sbd', rows_in, up_full, preferred_el...  96.4 us
    all_gather x1, waiting for transfers between devices, local(): lax.all_gather(normed_one.astype(jnp.bfloat16), 'mp', axis=0, tiled=True)  78.6 us
    all_gather x1, waiting for transfers between devices, local(): lax.all_gather(grad_out.astype(jnp.bfloat16), 'mp', axis=0, tiled=True)  78.6 us
    all_gather x1, waiting for transfers between devices, local(): lax.all_gather(normed_two.astype(jnp.bfloat16), 'mp', axis=0, tiled=True)  78.5 us
    all_gather x1, waiting for transfers between devices, local(): lax.all_gather(grad_hidden.astype(jnp.bfloat16), 'mp', axis=0, tiled=True)  76.9 us
    reduce_scatter x1, waiting for transfers between devices, local(): lax.psum_scatter(jnp.einsum('sbf,fd->sbd', rows_in, down_full, preferred_...  71.5 us
  transfers between devices with their start and end apart: 15, of which 15 were waited for; matrix products, arithmetic and copies ran while one was open for 9% of the time, Pallas kernels for 0%

commit v1 on v0

v1 whole, which is shorter than its diff:
```python
import jax
import jax.numpy as jnp
from jax import lax
from jax.sharding import PartitionSpec as P

HEAD = 64
BUF = 64
BF = jnp.bfloat16
F32 = jnp.float32

epsilon = 1e-06
masked_score = -1e30


def swap(x, axis, bits):
    n = lax.axis_size(axis)
    return lax.ppermute(x, axis, [(i, i ^ bits) for i in range(n)])


def gather_q(own):
    n_q = lax.axis_size("dp") // 2
    if n_q != 4:
        blocks = own[None]
        bit = 1
        while bit < n_q:
            blocks = jnp.concatenate([blocks, swap(blocks, "dp", 2 * bit)])
            bit *= 2
        return blocks
    half = own.shape[0] // 2
    one = swap(own, "dp", 2)
    two = swap(own, "dp", 4)
    three = jnp.concatenate([swap(one[:half], "dp", 4), swap(two[half:], "dp", 2)])
    return jnp.stack([own, one, two, three])


def add(*parts):
    total = parts[0].astype(F32)
    for part in parts[1:]:
        total = total + part.astype(F32)
    return total.astype(parts[0].dtype)


def scatter_q(parts):
    n_q = lax.axis_size("dp") // 2
    if n_q != 4:
        bit = n_q // 2
        while bit >= 1:
            parts = add(parts[:bit], swap(parts[bit:], "dp", 2 * bit))
            bit //= 2
        return parts[0]
    half = parts.shape[1] // 2
    into_one = swap(parts[3][:half], "dp", 4)
    into_two = swap(parts[3][half:], "dp", 2)
    one = jnp.concatenate([add(parts[1][:half], into_one), parts[1][half:]])
    two = jnp.concatenate([parts[2][:half], add(parts[2][half:], into_two)])
    return add(parts[0], swap(one, "dp", 2), swap(two, "dp", 4))


def gather_z(own):
    two = swap(own, "mp", 2)
    one = swap(own, "mp", 1)
    three = swap(two, "mp", 1)
    return jnp.stack([own, one, two, three])


def scatter_z(parts):
    into_two = swap(parts[3], "mp", 1)
    return add(parts[0], swap(parts[1], "mp", 1), swap(add(parts[2], into_two), "mp", 2))


def ordered_pair(own, other, core):
    return jnp.stack([jnp.where(core == 0, own, other), jnp.where(core == 0, other, own)])


def image_routes(n_dp, n_mp, odd):
    pairs = []
    for plane in range(n_dp // 2):
        for core in range(2):
            for z in range(n_mp):
                shift = 2 * core + odd
                worker = (plane * 2 + core) * n_mp + z
                holder = (plane * 2 + (z >> 1)) * n_mp + (z ^ shift)
                pairs.append((holder, worker))
    return pairs


def to_images(x, core, z):
    n_dp, n_mp = lax.axis_size("dp"), lax.axis_size("mp")
    slots, images, width = x.shape
    groups = jnp.transpose(x, (1, 0, 2)).reshape(2, images // 2, slots, width)
    got = []
    for odd in (0, 1):
        which = (z ^ odd) & 1
        send = lax.dynamic_index_in_dim(groups, which, 0, False)
        got.append(lax.ppermute(send, ("dp", "mp"), image_routes(n_dp, n_mp, odd)))
    return jnp.stack(got, 1)


def from_images(y, core, z):
    n_dp, n_mp = lax.axis_size("dp"), lax.axis_size("mp")
    back = []
    for odd in (0, 1):
        routes = [(b, a) for a, b in image_routes(n_dp, n_mp, odd)]
        back.append(lax.ppermute(y[:, odd], ("dp", "mp"), routes))
    flip = (z & 1) == 1
    groups = jnp.concatenate([jnp.where(flip, back[1], back[0]), jnp.where(flip, back[0], back[1])])
    return jnp.transpose(groups, (1, 0, 2))


def layer_norm(values, scales, shifts):
    average = jnp.mean(values, axis=-1, keepdims=True)
    centred = values - average
    spread = jnp.mean(centred * centred, axis=-1, keepdims=True)
    inv = lax.rsqrt(spread + epsilon)
    n = centred * inv
    return n * scales + shifts, n, inv


def layer_norm_back(n, inv, scales, grad):
    e = grad * scales
    mean_e = jnp.mean(e, axis=-1, keepdims=True)
    mean_en = jnp.mean(e * n, axis=-1, keepdims=True)
    return (e - mean_e - n * mean_en) * inv


def gelu_parts(inputs):
    normal_cdf = 0.5 * (1.0 + lax.erf(inputs * 0.7071067811865476))
    density = jnp.exp(-0.5 * inputs * inputs) * 0.3989422804014327
    return inputs * normal_cdf, normal_cdf + inputs * density


def local(
    tokens,
    counts,
    norm_gains,
    norm_shifts,
    qkv_weight,
    qkv_bias,
    proj_weight,
    out_biases,
    up_weight,
    up_bias,
    down_weight,
    cotangent,
):
    slots, images, width = tokens.shape
    n_dp, n_mp = lax.axis_size("dp"), lax.axis_size("mp")
    n_q = n_dp // 2
    wq = width // n_q
    dp, z = lax.axis_index("dp"), lax.axis_index("mp")
    q, core = dp >> 1, dp & 1
    own_images = images // 2
    all_slots = slots * n_mp
    rows = own_images * all_slots

    def rel(v):
        blocks = [lax.dynamic_slice_in_dim(v, (q ^ j) * wq, wq, v.ndim - 1) for j in range(n_q)]
        return jnp.concatenate(blocks, -1)

    def half_of(v, which, axis):
        size = v.shape[axis] // 2
        return lax.dynamic_slice_in_dim(v, which * size, size, axis)

    att = jnp.concatenate([qkv_weight, jnp.transpose(proj_weight)[None]])
    ffn = jnp.stack([up_weight, jnp.transpose(down_weight)])
    att_own = ordered_pair(half_of(att, core, 2), swap(half_of(att, 1 - core, 2), "dp", 1), core)
    att_own = jnp.transpose(att_own, (1, 0, 2, 3)).reshape(4, wq, -1)
    ffn_own = ordered_pair(half_of(ffn, core, 2), swap(half_of(ffn, 1 - core, 2), "dp", 1), core)
    ffn_own = jnp.transpose(ffn_own, (1, 0, 2, 3)).reshape(2, wq, -1)
    bias_own = jnp.concatenate(
        [half_of(qkv_bias, core, 1), half_of(up_bias, core, 0).reshape(-1, 128)]
    )
    bias_all = gather_z(bias_own)
    att_all = gather_q(gather_z(att_own))
    ffn_z = gather_z(ffn_own)
    ffn_all = [gather_q(ffn_z[:2]), gather_q(ffn_z[2:])]

    def whole_rows(v):
        got = to_images(rel(v), core, z)
        pair = ordered_pair(got, swap(got, "dp", 1), core)
        return jnp.transpose(pair, (1, 0, 2, 3, 4)).reshape(rows, width)

    other_counts = swap(counts, "dp", 1)
    source = z >> 1
    counts_here = jnp.where(source == core, counts, other_counts)
    counts_here = lax.dynamic_slice_in_dim(counts_here, (z & 1) * own_images, own_images, 0)
    slot_of = (z ^ jnp.arange(n_mp, dtype=jnp.int32))[:, None] * slots + jnp.arange(slots, dtype=jnp.int32)
    valid = (slot_of.reshape(1, -1) < BUF + counts_here[:, None])
    keep_mine = (z * slots + jnp.arange(slots, dtype=jnp.int32))[:, None] < BUF + counts[None, :]

    x = whole_rows(tokens)
    go = whole_rows(jnp.where(keep_mine[:, :, None], cotangent, jnp.zeros_like(cotangent)))
    gains, shifts, out_b = rel(norm_gains), rel(norm_shifts), rel(out_biases)

    x32 = x.astype(F32)
    n1f, hat1, inv1 = layer_norm(x32, gains[0], shifts[0])
    n1 = n1f.astype(BF)
    n_i, he = att_all.shape[1], att_all.shape[-1]
    heads = n_i * he // HEAD
    w_att = jnp.transpose(att_all, (2, 0, 3, 1, 4)).reshape(4, width, n_i * he)
    bias_rows = jnp.stack([bias_all[:, 0], jnp.zeros_like(bias_all[:, 0]), bias_all[:, 1]]).reshape(3, 1, -1)
    qkv = (jnp.einsum("rd,tde->tre", n1, w_att[:3], preferred_element_type=F32) + bias_rows).astype(BF)
    qkv = qkv.reshape(3, own_images, all_slots, heads, HEAD)
    factor = HEAD ** (-0.5)
    scores = jnp.einsum("bqhe,bkhe->bhqk", qkv[0], qkv[1], preferred_element_type=F32) * factor
    scores = jnp.where(valid[:, None, None, :], scores, masked_score)
    top = jnp.max(scores, axis=-1, keepdims=True)
    powers = jnp.exp(scores - top)
    probs = powers / jnp.sum(powers, axis=-1, keepdims=True)
    probs_low = probs.astype(BF)
    mixture = jnp.einsum("bhqk,bkhe->bqhe", probs_low, qkv[2], preferred_element_type=F32)
    mixture = mixture.astype(BF).reshape(rows, heads * HEAD)

    part = jnp.einsum("re,de->rd", mixture, w_att[3], preferred_element_type=F32).astype(BF)
    hidden = x32 + add(part.astype(F32), swap(part, "dp", 1)) + out_b[0]
    n2f, hat2, inv2 = layer_norm(hidden, gains[1], shifts[1])
    n2 = n2f.astype(BF)

    branch = 0.0
    gn2 = 0.0
    ffn_grads = []
    upbias_parts = []
    for group in (0, 1):
        w = ffn_all[group]
        w = jnp.transpose(w, (2, 0, 3, 1, 4)).reshape(2, width, -1)
        bias = bias_all[2 * group : 2 * group + 2, 2:].reshape(-1)
        up_pre = jnp.einsum("rd,df->rf", n2, w[0], preferred_element_type=F32) + bias
        act, slope = gelu_parts(up_pre)
        act = act.astype(BF)
        branch = branch + jnp.einsum("rf,df->rd", act, w[1], preferred_element_type=F32)
        grad_act = jnp.einsum("rd,df->rf", go, w[1], preferred_element_type=F32)
        grad_pre = (grad_act * slope).astype(BF)
        gn2 = gn2 + jnp.einsum("rf,df->rd", grad_pre, w[0], preferred_element_type=F32)
        up_g = jnp.einsum("rd,rf->df", n2, grad_pre, preferred_element_type=F32).astype(BF)
        down_g = jnp.einsum("rd,rf->df", go, act, preferred_element_type=F32).astype(BF)
        upbias_parts.append(jnp.sum(grad_pre.astype(F32), 0))
        g = jnp.stack([up_g, down_g]).reshape(2, n_q, wq, 2, -1)
        ffn_grads.append(scatter_q(jnp.transpose(g, (1, 3, 0, 2, 4))))
    ffn_grad = scatter_z(jnp.concatenate(ffn_grads))

    row_half = lambda v, which: half_of(v.reshape(own_images, n_mp, slots, width), which, 1)
    branch = branch.astype(BF)
    mine = row_half(branch, core).astype(F32)
    theirs = swap(row_half(branch, 1 - core), "dp", 1).astype(F32)
    out_half = row_half(hidden, core) + mine + theirs + out_b[1]
    block_out = from_images(rel(out_half.astype(BF)), core, z)
    block_out = jnp.where(keep_mine[:, :, None], block_out, jnp.zeros_like(block_out))

    gn2 = gn2.astype(BF)
    gn2 = gn2.astype(F32) + swap(gn2, "dp", 1).astype(F32)
    grad_hidden = go.astype(F32) + layer_norm_back(hat2, inv2, gains[1], gn2)
    gain_two, shift_two = jnp.sum(gn2 * hat2, 0), jnp.sum(gn2, 0)
    gh = grad_hidden.astype(BF)
    proj_g = jnp.einsum("rd,re->de", gh, mixture, preferred_element_type=F32).astype(BF)
    grad_mix = jnp.einsum("rd,de->re", gh, w_att[3], preferred_element_type=F32).astype(BF)
    grad_mix = grad_mix.reshape(own_images, all_slots, heads, HEAD)
    grad_probs = jnp.einsum("bqhe,bkhe->bhqk", grad_mix, qkv[2], preferred_element_type=F32)
    row_dot = jnp.sum(probs * grad_probs, axis=-1, keepdims=True)
    grad_scores = (probs * (grad_probs - row_dot)).astype(BF)
    grad_q = jnp.einsum("bhqk,bkhe->bqhe", grad_scores, qkv[1], preferred_element_type=F32) * factor
    grad_k = jnp.einsum("bhqk,bqhe->bkhe", grad_scores, qkv[0], preferred_element_type=F32) * factor
    grad_v = jnp.einsum("bhqk,bqhe->bkhe", probs_low, grad_mix, preferred_element_type=F32)
    grad_qkv = jnp.stack([grad_q, grad_k, grad_v]).astype(BF).reshape(3, rows, heads * HEAD)
    qkv_g = jnp.einsum("rd,tre->tde", n1, grad_qkv, preferred_element_type=F32).astype(BF)
    bias_part = jnp.stack([jnp.sum(grad_qkv[0].astype(F32), 0), jnp.sum(grad_qkv[2].astype(F32), 0)])
    att_g = jnp.concatenate([qkv_g, proj_g[None]]).reshape(4, n_q, wq, n_i, he)
    att_grad = scatter_z(scatter_q(jnp.transpose(att_g, (1, 3, 0, 2, 4))))

    gn1 = jnp.einsum("tre,tde->rd", grad_qkv, w_att[:3], preferred_element_type=F32).astype(BF)
    gn1 = row_half(gn1, core).astype(F32) + swap(row_half(gn1, 1 - core), "dp", 1).astype(F32)
    my_hat1, my_inv1 = row_half(hat1, core), half_of(inv1.reshape(own_images, n_mp, slots, 1), core, 1)
    input_half = row_half(grad_hidden, core) + layer_norm_back(my_hat1, my_inv1, gains[0], gn1)
    gain_one, shift_one = jnp.sum(gn1 * my_hat1, (0, 1, 2)), jnp.sum(gn1, (0, 1, 2))
    input_grad = from_images(rel(input_half.astype(BF)), core, z)

    def own_shard(grad, last):
        kinds = grad.shape[0]
        pair = grad.reshape(kinds, 2, wq // 2, last // 2)
        keep = lax.dynamic_index_in_dim(pair, core, 1, False)
        got = swap(lax.dynamic_index_in_dim(pair, 1 - core, 1, False), "dp", 1)
        both = ordered_pair(keep, got, core)
        return jnp.transpose(both, (1, 2, 0, 3)).reshape(kinds, wq // 2, last).astype(F32)

    att_shard = own_shard(att_grad, 2 * he)
    ffn_shard = own_shard(ffn_grad, 2 * ffn_own.shape[-1])
    qkv_owned, proj_owned = att_shard[:3], jnp.transpose(att_shard[3])
    up_owned, down_owned = ffn_shard[0], jnp.transpose(ffn_shard[1])

    fh = ffn_own.shape[-1]
    wide_up = jnp.zeros((n_mp, 2, fh), F32)
    wide_bias = jnp.zeros((2, n_mp, 2, he), F32)
    ups = jnp.concatenate(upbias_parts).reshape(n_mp, fh)
    biases = bias_part.reshape(2, n_mp, he)
    for i in range(n_mp):
        wide_up = lax.dynamic_update_slice(wide_up, ups[i][None, None], (z ^ i, core, 0))
        wide_bias = lax.dynamic_update_slice(wide_bias, biases[:, i][:, None, None], (0, z ^ i, core, 0))
    go_half = row_half(go, core).astype(F32)
    gh_half = row_half(grad_hidden, core)
    small = rel(
        jnp.stack(
            [
                gain_one,
                gain_two * 0.5,
                shift_one,
                shift_two * 0.5,
                jnp.sum(gh_half, (0, 1, 2)),
                jnp.sum(go_half, (0, 1, 2)),
            ]
        )
    )
    small, wide_bias, wide_up = lax.psum((small, wide_bias, wide_up), ("dp", "mp"))
    bias_grad = lax.dynamic_index_in_dim(wide_bias, z, 1, False).reshape(2, -1)
    upbias_grad = lax.dynamic_index_in_dim(wide_up, z, 0, False).reshape(-1)
    return (
        block_out,
        input_grad,
        small[0:2],
        small[2:4],
        qkv_owned,
        bias_grad,
        proj_owned,
        small[4:6],
        up_owned,
        upbias_grad,
        down_owned,
    )


def solution(mesh):
    return jax.shard_map(
        local,
        mesh=mesh,
        in_specs=(
            P("mp", "dp", None),
            P("dp"),
            P(),
            P(),
            P(None, "dp", "mp"),
            P(None, "mp"),
            P("mp", "dp"),
            P(),
            P("dp", "mp"),
            P("mp"),
            P("mp", "dp"),
            P("mp", "dp", None),
        ),
        out_specs=(
            P("mp", "dp", None),
            P("mp", "dp", None),
            P(),
            P(),
            P(None, "dp", "mp"),
            P(None, "mp"),
            P("mp", "dp"),
            P(),
            P("dp", "mp"),
            P("mp"),
            P("mp", "dp"),
        ),
        check_vma=False,
    )
```

time: 1220 us -> 687 us (0.56)
  waiting for transfers between devices: 907 us -> 205 us
  local copies, waits for them, and re-layouts: 43.6 us -> 166 us
  starting transfers between devices: 12.3 us -> 86.8 us
  matrix products: 116 us -> 102 us
    reduce_scatter x8 -> x0, waiting for transfers between devices: 547 us -> none  [the longest x1 137 us: local(): lax.psum_scatter(jnp.einsum('tsbe,tde->sbd', rows_in, qkv_full, preferred...]
    all_gather x7 -> x0, waiting for transfers between devices: 358 us -> none  [the longest x1 78.6 us: local(): lax.all_gather(normed_one.astype(jnp.bfloat16), 'mp', axis=0, tiled=True)]
    ppermute x0 -> x58, waiting for transfers between devices: none -> 205 us  [the longest x50 187 us: swap(): return lax.ppermute(x, axis, [(i, i ^ bits) for i in range(n)])]
    ppermute x0 -> x58, starting transfers between devices: none -> 86.8 us  [the longest x50 74.8 us: swap(): return lax.ppermute(x, axis, [(i, i ^ bits) for i in range(n)])]
    another operation x1 -> x19, local copies, waits for them, and re-layouts: 0.07 us -> 41.5 us  [the longest x8 29.6 us: local(): g = jnp.stack([up_g, down_g]).reshape(2, n_q, wq, 2, -1)]
    unnamed x67 -> x176, local copies, waits for them, and re-layouts: 8.63 us -> 35.2 us
    slice x10 -> x35, local copies, waits for them, and re-layouts: 7.98 us -> 34.1 us  [the longest x3 10.1 us: local(): w_att[:3]]
    dot_general x33 -> x23, matrix products: 116 us -> 91.6 us  [the longest x2 11.3 us: local(): grad_act = jnp.einsum('rd,df->rf', go, w[1], preferred_element_type=F32)]
  transfers between devices with their start and end apart: 15 -> 58, of which waited for: 15 -> 25; matrix products, arithmetic and copies ran while one was open for 9% -> 37% of each run, Pallas kernels for 0% -> 0%
where the time goes in v1:
time: 687 us; the launch traced here: 680 us
  waiting for transfers between devices  205 us (30%)
  local copies, waits for them, and re-layouts  166 us (24%)
  matrix products  102 us (15%)
  starting transfers between devices  86.8 us (13%)
  other arithmetic  71.8 us (10%)
  blocking collectives  45.9 us (7%)
    ppermute x50, waiting for transfers between devices, swap(): return lax.ppermute(x, axis, [(i, i ^ bits) for i in range(n)])  187 us
    ppermute x50, starting transfers between devices, swap(): return lax.ppermute(x, axis, [(i, i ^ bits) for i in range(n)])  74.8 us
    psum x1, blocking collectives, local(): lax.psum((small, wide_bias, wide_up), ('dp', 'mp'))  45.9 us
    unnamed x176, local copies, waits for them, and re-layouts  35.2 us
    another operation x8, local copies, waits for them, and re-layouts, local(): g = jnp.stack([up_g, down_g]).reshape(2, n_q, wq, 2, -1)  29.6 us
    convert_element_type x10, other arithmetic, add(): return total.astype(parts[0].dtype)  14.2 us
  transfers between devices with their start and end apart: 58, of which 25 were waited for; matrix products, arithmetic and copies ran while one was open for 37% of the time, Pallas kernels for 0%

profile of v1, /device:TPU:0, one launch (start us, length us, event | category | flops | bytes accessed | tf_op | source)
XLA Modules:
  0.0 680.2 jit_solution(1349718579095181433)
XLA Ops:
  2.1 4.0 collective-permute-start.12
  20.0 30.1 %collective-permute-done.5 = bf16[4,256,128]{2,1,0:T(8,128)(2,1)S(1)} collective-permute-done((bf16[4,256,128]{2,1,0:T(8,128)(2,1)S(1)}, bf16[4,256,128]{2,1,0:T(8,128)(2,1)S(1)}, u32[]{:S(2)}, u32[]{:S(2)}) %collective-permute-start.5) | collective-permute-done | bytes 262176 | tf_op jit(solution)/shard_map/ppermute | solution.py:17
  52.6 18.5 %collective-permute-done.13 = f32[6,128]{1,0:T(8,128)S(1)} collective-permute-done((f32[6,128]{1,0:T(8,128)S(1)}, f32[6,128]{1,0:T(8,128)S(1)}, u32[]{:S(2)}, u32[]{:S(2)}) %collective-permute-start.13) | collective-permute-done | bytes 3104 | tf_op jit(solution)/shard_map/ppermute | solution.py:17
  77.0 9.4 %collective-permute-done.17 = bf16[2,256,512]{2,1,0:T(8,128)(2,1)S(1)} collective-permute-done((bf16[2,256,512]{2,1,0:T(8,128)(2,1)S(1)}, bf16[2,256,512]{2,1,0:T(8,128)(2,1)S(1)}, u32[]{:S(2)}, u32[]{:S(2)}) %collective-permute-start.17) | collective-permute-done | bytes 524320 | tf_op jit(solution)/shard_map/ppermute | solution.py:17
  89.0 6.6 collective-permute-done.23
  105.0 19.0 %collective-permute-done.18 = bf16[2,2,256,512]{3,2,1,0:T(8,128)(2,1)S(1)} collective-permute-done((bf16[2,2,256,512]{3,2,1,0:T(8,128)(2,1)S(1)}, bf16[2,2,256,512]{3,2,1,0:T(8,128)(2,1)S(1)}, u32[]{:S(2)}, u32[]{:S(2)}) %collective-permute-start.18) | collective-permute-done | bytes 1048608 | tf_op jit(solution)/shard_map/ppermute | solution.py:17
  127.7 26.9 %collective-permute-done.10 = bf16[2,4,256,128]{3,2,1,0:T(8,128)(2,1)S(1)} collective-permute-done((bf16[2,4,256,128]{3,2,1,0:T(8,128)(2,1)S(1)}, bf16[2,4,256,128]{3,2,1,0:T(8,128)(2,1)S(1)}, u32[]{:S(2)}, u32[]{:S(2)}) %collective-permute-start.10) | collective-permute-done | bytes 524320 | tf_op jit(solution)/shard_map/ppermute | solution.py:17
  159.3 4.2 copy.284
  163.5 5.7 slice.346
  169.2 5.7 fusion.30
  181.3 4.0 reshape.523
  185.3 3.8 copy.295
  192.8 4.0 copy.296
  196.8 10.3 %fusion.120 = (f32[3,8,320]{2,1,0:T(8,128)S(1)}, f32[3,8,320,320]{2,3,1,0:T(8,128)}) fusion(pred[3,320]{1,0:T(4,128)(4,1)S(1)} %broadcast_compare_fusion, bf16[3,320,8,64]{1,3,2,0:T(8,128)(2,1)S(1)} %copy.294, bf16[3,320,8,64]{1,3,2,0:T(8,128)(2,1)} %copy.295), kind=kOutput, calls=%fused_computation.355 | convolution fusion | flops 324403520 | bytes 11828160 | tf_op jit(solution)/shard_map/sub | solution.py:208
  207.1 6.0 fusion.61
  215.2 4.0 reshape.485
  220.0 4.3 convolution_convert_fusion.4
  252.0 6.1 fusion.20
  265.4 4.0 multiply_convert_fusion.1
  269.4 4.2 multiply_convert_fusion.2
  285.0 5.3 collective-permute-start.30
  290.4 6.8 %collective-permute-done.29 = bf16[3,80,1024]{2,1,0:T(8,128)(2,1)S(1)} collective-permute-done((bf16[3,80,1024]{2,1,0:T(8,128)(2,1)}, bf16[3,80,1024]{2,1,0:T(8,128)(2,1)S(1)}, u32[]{:S(2)}, u32[]{:S(2)}) %collective-permute-start.29) | collective-permute-done | bytes 491552 | tf_op jit(solution)/shard_map/ppermute | solution.py:104
  302.8 11.0 %collective-permute-done.32 = bf16[3,80,1024]{2,1,0:T(8,128)(2,1)S(1)} collective-permute-done((bf16[3,80,1024]{2,1,0:T(8,128)(2,1)S(1)}, bf16[3,80,1024]{2,1,0:T(8,128)(2,1)S(1)}, u32[]{:S(2)}, u32[]{:S(2)}) %collective-permute-start.32) | collective-permute-done | bytes 491552 | tf_op jit(solution)/shard_map/ppermute | solution.py:95
  314.8 19.0 %collective-permute-start.33 = (bf16[3,2,80,1024]{3,2,1,0:T(8,128)(2,1)}, bf16[3,2,80,1024]{3,2,1,0:T(8,128)(2,1)}, u32[]{:S(2)}, u32[]{:S(2)}) collective-permute-start(bf16[3,2,80,1024]{3,2,1,0:T(8,128)(2,1)} %pad_maximum_fusion.14), channel_id=1, source_target_pairs={{0,4},{4,0},{8,12},{12,8},{16,20},{20,16},{24,28},{28,24},{1,5},{5... | collective-permute-start | bytes 2949128 | tf_op jit(solution)/shard_map/ppermute | solution.py:17
  340.4 3.8 convolution_convert_fusion.2
  347.9 4.9 stack.315
  356.2 5.9 convert_reduce_fusion.1
  363.5 3.8 convolution_convert_fusion.3
  367.3 4.5 stack.314
  379.7 4.5 stack.318
  387.7 5.3 convert_reduce_fusion
  394.4 3.8 convolution_convert_fusion.1
  398.1 4.6 stack.317
  427.0 16.6 %collective-permute-done.47 = bf16[2,2,256,512]{3,2,1,0:T(8,128)(2,1)} collective-permute-done((bf16[2,2,256,512]{3,2,1,0:T(8,128)(2,1)}, bf16[2,2,256,512]{3,2,1,0:T(8,128)(2,1)}, u32[]{:S(2)}, u32[]{:S(2)}) %collective-permute-start.47) | collective-permute-done | bytes 1048608 | tf_op jit(solution)/shard_map/ppermute | solution.py:17
  446.9 5.8 collective-permute-start.50
  452.6 11.6 %collective-permute-done.52 = bf16[2,2,256,512]{3,2,1,0:T(8,128)(2,1)} collective-permute-done((bf16[2,2,256,512]{3,2,1,0:T(8,128)(2,1)}, bf16[2,2,256,512]{3,2,1,0:T(8,128)(2,1)}, u32[]{:S(2)}, u32[]{:S(2)}) %collective-permute-start.52) | collective-permute-done | bytes 1048608 | tf_op jit(solution)/shard_map/ppermute | solution.py:17
  468.3 5.8 collective-permute-start.55
  474.1 4.3 multiply_reduce_fusion.1
  486.2 3.8 reshape.524
  493.8 7.9 %convert_reduce_fusion.2 = (f32[8,64]{1,0:T(8,128)S(1)}, bf16[3,320,8,64]{1,3,2,0:T(8,128)(2,1)}) fusion(bf16[3,320,8,64]{1,3,2,0:T(8,128)(2,1)} %copy.312, f32[3,8,320,320]{2,3,1,0:T(8,128)} %get-tuple-element.180, f32[3,8,320]{2,1,0:T(8,128)S(1)} %copy-done.57), kind=kOutput, calls=%fused_computation.70 | convolution fusion | flops 320962048 | bytes 11829248 | tf_op jit(solution)/shard_map/bhqk,bqhe->bkhe/dot_general | solution.py:262
  531.0 4.5 bitcast_convert_fusion
  535.5 4.9 convert_bitcast_fusion
  540.3 4.8 concatenate.97
  565.0 4.0 collective-permute-done.38
  571.8 17.7 %collective-permute-done.56 = bf16[2,256,512]{2,1,0:T(8,128)(2,1)} collective-permute-done((bf16[2,256,512]{2,1,0:T(8,128)(2,1)}, bf16[2,256,512]{2,1,0:T(8,128)(2,1)}, u32[]{:S(2)}, u32[]{:S(2)}) %collective-permute-start.56) | collective-permute-done | bytes 524320 | tf_op jit(solution)/shard_map/ppermute | solution.py:17
  606.1 45.9 %all-reduce = (f32[6,1024]{1,0:T(8,128)S(1)}, f32[2,4,2,128]{3,2,0,1:T(2,128)S(1)}, f32[4,2,512]{2,1,0:T(2,128)S(1)}) all-reduce(f32[6,1024]{1,0:T(8,128)S(1)} %pad_maximum_fusion.18, f32[2,4,2,128]{3,2,0,1:T(2,128)S(1)} %dynamic_update_slice.27, f32[4,2,512]{2,1,0:T(2,128)S(1)} %copy-done.55), channel_id=1, replica_groups=mesh['dp'=8,'mp'=4] {'dp','mp'}, use_global_device_ids=true, to_apply=%region_17.18 | all-reduce | flops 12288 | bytes 98304 | tf_op jit(solution)/shard_map/psum | solution.py:311
  658.3 8.2 %collective-permute-done.43 = bf16[4,256,128]{2,1,0:T(8,128)(2,1)S(1)} collective-permute-done((bf16[4,256,128]{2,1,0:T(8,128)(2,1)S(1)}, bf16[4,256,128]{2,1,0:T(8,128)(2,1)S(1)}, u32[]{:S(2)}, u32[]{:S(2)}) %collective-permute-start.43) | collective-permute-done | bytes 262176 | tf_op jit(solution)/shard_map/ppermute | solution.py:17
  670.2 6.0 collective-permute-done.44
  (473 shorter events, 261.5 us)
Async XLA Ops:
  2.1 50.3 %collective-permute-start.12 = (f32[6,128]{1,0:T(8,128)S(1)}, f32[6,128]{1,0:T(8,128)S(1)}, u32[]{:S(2)}, u32[]{:S(2)}) collective-permute-start(f32[6,128]{1,0:T(8,128)S(1)} %get-tuple-element.174), channel_id=1, source_target_pairs={{0,2},{1,3},{2,0},{3,1},{4,6},{5,7},{6,4},{7,5},{8,10},{9,11},{10,... | collective-permute-start | bytes 9224 | tf_op jit(solution)/shard_map/ppermute | solution.py:17
  6.1 46.4 %collective-permute-start.11 = (f32[6,128]{1,0:T(8,128)S(1)}, f32[6,128]{1,0:T(8,128)S(1)}, u32[]{:S(2)}, u32[]{:S(2)}) collective-permute-start(f32[6,128]{1,0:T(8,128)S(1)} %get-tuple-element.174), channel_id=1, source_target_pairs={{0,1},{1,0},{2,3},{3,2},{4,5},{5,4},{6,7},{7,6},{8,9},{9,8},{10,11... | collective-permute-start | bytes 9224 | tf_op jit(solution)/shard_map/ppermute | solution.py:17
  11.4 38.8 %collective-permute-start = (bf16[3,80,1024]{2,1,0:T(8,128)(2,1)S(1)}, bf16[3,80,1024]{2,1,0:T(8,128)(2,1)S(1)}, u32[]{:S(2)}, u32[]{:S(2)}) collective-permute-start(bf16[3,80,1024]{2,1,0:T(8,128)(2,1)S(1)} %get-tuple-element.124), channel_id=1, source_target_pairs={{0,0},{1,1},{6,2},{7,3},{2,4},{3,5},{4,6},{5,7},{8,8},{9,9},{14,10... | collective-permute-start | bytes 1474568 | tf_op jit(solution)/shard_map/ppermute | solution.py:95
  14.7 35.5 %collective-permute-start.1 = (bf16[3,80,1024]{2,1,0:T(8,128)(2,1)S(1)}, bf16[3,80,1024]{2,1,0:T(8,128)(2,1)S(1)}, u32[]{:S(2)}, u32[]{:S(2)}) collective-permute-start(bf16[3,80,1024]{2,1,0:T(8,128)(2,1)S(1)} %get-tuple-element.125), channel_id=1, source_target_pairs={{1,0},{0,1},{7,2},{6,3},{3,4},{2,5},{5,6},{4,7},{9,8},{8,9},{15,10... | collective-permute-start | bytes 1474568 | tf_op jit(solution)/shard_map/ppermute | solution.py:95
  19.1 31.1 %collective-permute-start.5 = (bf16[4,256,128]{2,1,0:T(8,128)(2,1)S(1)}, bf16[4,256,128]{2,1,0:T(8,128)(2,1)S(1)}, u32[]{:S(2)}, u32[]{:S(2)}) collective-permute-start(bf16[4,256,128]{2,1,0:T(8,128)(2,1)S(1)} %bitcast.494), channel_id=1, source_target_pairs={{0,2},{1,3},{2,0},{3,1},{4,6},{5,7},{6,4},{7,5},{8,10},{9,11},{10,... | collective-permute-start | bytes 786440 | tf_op jit(solution)/shard_map/ppermute | solution.py:17
  50.2 23.5 %collective-permute-start.4 = (bf16[4,256,128]{2,1,0:T(8,128)(2,1)S(1)}, bf16[4,256,128]{2,1,0:T(8,128)(2,1)S(1)}, u32[]{:S(2)}, u32[]{:S(2)}) collective-permute-start(bf16[4,256,128]{2,1,0:T(8,128)(2,1)S(1)} %bitcast.495), channel_id=1, source_target_pairs={{0,1},{1,0},{2,3},{3,2},{4,5},{5,4},{6,7},{7,6},{8,9},{9,8},{10,11... | collective-permute-start | bytes 786440 | tf_op jit(solution)/shard_map/ppermute | solution.py:17
  50.2 23.4 %collective-permute-start.22 = (bf16[2,256,512]{2,1,0:T(8,128)(2,1)S(1)}, bf16[2,256,512]{2,1,0:T(8,128)(2,1)S(1)}, u32[]{:S(2)}, u32[]{:S(2)}) collective-permute-start(bf16[2,256,512]{2,1,0:T(8,128)(2,1)S(1)} %bitcast.479), channel_id=1, source_target_pairs={{0,2},{1,3},{2,0},{3,1},{4,6},{5,7},{6,4},{7,5},{8,10},{9,11},{10,... | collective-permute-start | bytes 1572872 | tf_op jit(solution)/shard_map/ppermute | solution.py:17
  50.2 23.5 %collective-permute-start.6 = (bf16[4,256,128]{2,1,0:T(8,128)(2,1)S(1)}, bf16[4,256,128]{2,1,0:T(8,128)(2,1)S(1)}, u32[]{:S(2)}, u32[]{:S(2)}) collective-permute-start(bf16[4,256,128]{2,1,0:T(8,128)(2,1)S(1)} %collective-permute-done.5), channel_id=1, source_target_pairs={{0,1},{1,0},{2,3},{3,2},{4,5},{5,4},{6,7},{7,6},{8,9},{9,8},{10,11... | collective-permute-start | bytes 786440 | tf_op jit(solution)/shard_map/ppermute | solution.py:17
  52.4 46.2 %collective-permute-start.2 = (bf16[3,2,80,1024]{3,2,1,0:T(8,128)(2,1)S(1)}, bf16[3,2,80,1024]{3,2,1,0:T(8,128)(2,1)S(1)}, u32[]{:S(2)}, u32[]{:S(2)}) collective-permute-start(bf16[3,2,80,1024]{3,2,1,0:T(8,128)(2,1)S(1)} %pad_maximum_fusion.11), channel_id=1, source_target_pairs={{0,4},{4,0},{8,12},{12,8},{16,20},{20,16},{24,28},{28,24},{1,5},{5... | collective-permute-start | bytes 2949128 | tf_op jit(solution)/shard_map/ppermute | solution.py:17
  52.5 18.6 %collective-permute-start.13 = (f32[6,128]{1,0:T(8,128)S(1)}, f32[6,128]{1,0:T(8,128)S(1)}, u32[]{:S(2)}, u32[]{:S(2)}) collective-permute-start(f32[6,128]{1,0:T(8,128)S(1)} %collective-permute-done.12), channel_id=1, source_target_pairs={{0,1},{1,0},{2,3},{3,2},{4,5},{5,4},{6,7},{7,6},{8,9},{9,8},{10,11... | collective-permute-start | bytes 9224 | tf_op jit(solution)/shard_map/ppermute | solution.py:17
  71.1 15.3 %collective-permute-start.17 = (bf16[2,256,512]{2,1,0:T(8,128)(2,1)S(1)}, bf16[2,256,512]{2,1,0:T(8,128)(2,1)S(1)}, u32[]{:S(2)}, u32[]{:S(2)}) collective-permute-start(bf16[2,256,512]{2,1,0:T(8,128)(2,1)S(1)} %bitcast.480), channel_id=1, source_target_pairs={{0,1},{1,0},{2,3},{3,2},{4,5},{5,4},{6,7},{7,6},{8,9},{9,8},{10,11... | collective-permute-start | bytes 1572872 | tf_op jit(solution)/shard_map/ppermute | solution.py:17
  73.6 22.0 %collective-permute-start.23 = (bf16[2,256,512]{2,1,0:T(8,128)(2,1)S(1)}, bf16[2,256,512]{2,1,0:T(8,128)(2,1)S(1)}, u32[]{:S(2)}, u32[]{:S(2)}) collective-permute-start(bf16[2,256,512]{2,1,0:T(8,128)(2,1)S(1)} %collective-permute-done.22), channel_id=1, source_target_pairs={{0,1},{1,0},{2,3},{3,2},{4,5},{5,4},{6,7},{7,6},{8,9},{9,8},{10,11... | collective-permute-start | bytes 1572872 | tf_op jit(solution)/shard_map/ppermute | solution.py:17
  73.9 26.7 %collective-permute-start.8 = (bf16[4,4,256,128]{3,2,1,0:T(8,128)(2,1)S(1)}, bf16[4,4,256,128]{3,2,1,0:T(8,128)(2,1)S(1)}, u32[]{:S(2)}, u32[]{:S(2)}) collective-permute-start(bf16[4,4,256,128]{3,2,1,0:T(8,128)(2,1)S(1)} %get-tuple-element.101), channel_id=1, source_target_pairs={{0,16},{4,20},{8,24},{12,28},{16,0},{20,4},{24,8},{28,12},{1,17},{... | collective-permute-start | bytes 3145736 | tf_op jit(solution)/shard_map/ppermute | solution.py:17
  75.5 26.1 %collective-permute-start.7 = (bf16[4,4,256,128]{3,2,1,0:T(8,128)(2,1)S(1)}, bf16[4,4,256,128]{3,2,1,0:T(8,128)(2,1)S(1)}, u32[]{:S(2)}, u32[]{:S(2)}) collective-permute-start(bf16[4,4,256,128]{3,2,1,0:T(8,128)(2,1)S(1)} %get-tuple-element.101), channel_id=1, source_target_pairs={{0,8},{4,12},{8,0},{12,4},{16,24},{20,28},{24,16},{28,20},{1,9},{5... | collective-permute-start | bytes 3145736 | tf_op jit(solution)/shard_map/ppermute | solution.py:17
  87.5 36.5 %collective-permute-start.18 = (bf16[2,2,256,512]{3,2,1,0:T(8,128)(2,1)S(1)}, bf16[2,2,256,512]{3,2,1,0:T(8,128)(2,1)S(1)}, u32[]{:S(2)}, u32[]{:S(2)}) collective-permute-start(bf16[2,2,256,512]{3,2,1,0:T(8,128)(2,1)S(1)} %get-tuple-element.99), channel_id=1, source_target_pairs={{0,8},{4,12},{8,0},{12,4},{16,24},{20,28},{24,16},{28,20},{1,9},{5... | collective-permute-start | bytes 3145736 | tf_op jit(solution)/shard_map/ppermute | solution.py:17
  95.6 29.8 %collective-permute-start.19 = (bf16[2,2,256,512]{3,2,1,0:T(8,128)(2,1)S(1)}, bf16[2,2,256,512]{3,2,1,0:T(8,128)(2,1)S(1)}, u32[]{:S(2)}, u32[]{:S(2)}) collective-permute-start(bf16[2,2,256,512]{3,2,1,0:T(8,128)(2,1)S(1)} %get-tuple-element.99), channel_id=1, source_target_pairs={{0,16},{4,20},{8,24},{12,28},{16,0},{20,4},{24,8},{28,12},{1,17},{... | collective-permute-start | bytes 3145736 | tf_op jit(solution)/shard_map/ppermute | solution.py:17
  98.6 125.9 %collective-permute-start.24 = (bf16[2,2,256,512]{3,2,1,0:T(8,128)(2,1)}, bf16[2,2,256,512]{3,2,1,0:T(8,128)(2,1)}, u32[]{:S(2)}, u32[]{:S(2)}) collective-permute-start(bf16[2,2,256,512]{3,2,1,0:T(8,128)(2,1)} %get-tuple-element.97), channel_id=1, source_target_pairs={{0,8},{4,12},{8,0},{12,4},{16,24},{20,28},{24,16},{28,20},{1,9},{5... | collective-permute-start | bytes 3145736 | tf_op jit(solution)/shard_map/ppermute | solution.py:17
  100.6 54.0 %collective-permute-start.10 = (bf16[2,4,256,128]{3,2,1,0:T(8,128)(2,1)S(1)}, bf16[2,4,256,128]{3,2,1,0:T(8,128)(2,1)S(1)}, u32[]{:S(2)}, u32[]{:S(2)}) collective-permute-start(bf16[2,4,256,128]{3,2,1,0:T(8,128)(2,1)S(1)} %slice.433), channel_id=1, source_target_pairs={{0,8},{4,12},{8,0},{12,4},{16,24},{20,28},{24,16},{28,20},{1,9},{5... | collective-permute-start | bytes 1572872 | tf_op jit(solution)/shard_map/ppermute | solution.py:17
  101.6 54.5 %collective-permute-start.9 = (bf16[2,4,256,128]{3,2,1,0:T(8,128)(2,1)S(1)}, bf16[2,4,256,128]{3,2,1,0:T(8,128)(2,1)S(1)}, u32[]{:S(2)}, u32[]{:S(2)}) collective-permute-start(bf16[2,4,256,128]{3,2,1,0:T(8,128)(2,1)S(1)} %slice.432), channel_id=1, source_target_pairs={{0,16},{4,20},{8,24},{12,28},{16,0},{20,4},{24,8},{28,12},{1,17},{... | collective-permute-start | bytes 1572872 | tf_op jit(solution)/shard_map/ppermute | solution.py:17
  124.0 102.3 %collective-permute-start.25 = (bf16[2,2,256,512]{3,2,1,0:T(8,128)(2,1)}, bf16[2,2,256,512]{3,2,1,0:T(8,128)(2,1)}, u32[]{:S(2)}, u32[]{:S(2)}) collective-permute-start(bf16[2,2,256,512]{3,2,1,0:T(8,128)(2,1)} %get-tuple-element.97), channel_id=1, source_target_pairs={{0,16},{4,20},{8,24},{12,28},{16,0},{20,4},{24,8},{28,12},{1,17},{... | collective-permute-start | bytes 3145736 | tf_op jit(solution)/shard_map/ppermute | solution.py:17
  125.4 102.7 %collective-permute-start.20 = (bf16[1,2,256,512]{3,2,1,0:T(8,128)(2,1)}, bf16[1,2,256,512]{3,2,1,0:T(8,128)(2,1)}, u32[]{:S(2)}, u32[]{:S(2)}) collective-permute-start(bf16[1,2,256,512]{3,2,1,0:T(8,128)(2,1)} %slice.442), channel_id=1, source_target_pairs={{0,16},{4,20},{8,24},{12,28},{16,0},{20,4},{24,8},{28,12},{1,17},{... | collective-permute-start | bytes 1572872 | tf_op jit(solution)/shard_map/ppermute | solution.py:17
  154.6 73.4 %collective-permute-start.21 = (bf16[1,2,256,512]{3,2,1,0:T(8,128)(2,1)}, bf16[1,2,256,512]{3,2,1,0:T(8,128)(2,1)}, u32[]{:S(2)}, u32[]{:S(2)}) collective-permute-start(bf16[1,2,256,512]{3,2,1,0:T(8,128)(2,1)} %slice.443), channel_id=1, source_target_pairs={{0,8},{4,12},{8,0},{12,4},{16,24},{20,28},{24,16},{28,20},{1,9},{5... | collective-permute-start | bytes 1572872 | tf_op jit(solution)/shard_map/ppermute | solution.py:17
  224.3 27.7 %collective-permute-start.15 = (bf16[960,1024]{1,0:T(8,128)(2,1)}, bf16[960,1024]{1,0:T(8,128)(2,1)}, u32[]{:S(2)}, u32[]{:S(2)}) collective-permute-start(bf16[960,1024]{1,0:T(8,128)(2,1)} %convolution_convert_fusion.4), channel_id=1, source_target_pairs={{0,4},{4,0},{8,12},{12,8},{16,20},{20,16},{24,28},{28,24},{1,5},{5... | collective-permute-start | bytes 5898248 | tf_op jit(solution)/shard_map/ppermute | solution.py:17
  225.7 14.4 %collective-permute-start.26 = (bf16[1,2,256,512]{3,2,1,0:T(8,128)(2,1)S(1)}, bf16[1,2,256,512]{3,2,1,0:T(8,128)(2,1)S(1)}, u32[]{:S(2)}, u32[]{:S(2)}) collective-permute-start(bf16[1,2,256,512]{3,2,1,0:T(8,128)(2,1)S(1)} %slice.446), channel_id=1, source_target_pairs={{0,16},{4,20},{8,24},{12,28},{16,0},{20,4},{24,8},{28,12},{1,17},{... | collective-permute-start | bytes 1572872 | tf_op jit(solution)/shard_map/ppermute | solution.py:17
  227.4 14.1 %collective-permute-start.27 = (bf16[1,2,256,512]{3,2,1,0:T(8,128)(2,1)S(1)}, bf16[1,2,256,512]{3,2,1,0:T(8,128)(2,1)S(1)}, u32[]{:S(2)}, u32[]{:S(2)}) collective-permute-start(bf16[1,2,256,512]{3,2,1,0:T(8,128)(2,1)S(1)} %slice.447), channel_id=1, source_target_pairs={{0,8},{4,12},{8,0},{12,4},{16,24},{20,28},{24,16},{28,20},{1,9},{5... | collective-permute-start | bytes 1572872 | tf_op jit(solution)/shard_map/ppermute | solution.py:17
  283.0 14.2 %collective-permute-start.29 = (bf16[3,80,1024]{2,1,0:T(8,128)(2,1)}, bf16[3,80,1024]{2,1,0:T(8,128)(2,1)S(1)}, u32[]{:S(2)}, u32[]{:S(2)}) collective-permute-start(bf16[3,80,1024]{2,1,0:T(8,128)(2,1)} %get-tuple-element.118), channel_id=1, source_target_pairs={{0,1},{1,0},{2,7},{3,6},{4,3},{5,2},{6,5},{7,4},{8,9},{9,8},{10,15... | collective-permute-start | bytes 1474568 | tf_op jit(solution)/shard_map/ppermute | solution.py:104
  285.0 12.2 %collective-permute-start.30 = (bf16[3,80,1024]{2,1,0:T(8,128)(2,1)}, bf16[3,80,1024]{2,1,0:T(8,128)(2,1)}, u32[]{:S(2)}, u32[]{:S(2)}) collective-permute-start(bf16[3,80,1024]{2,1,0:T(8,128)(2,1)} %get-tuple-element.119), channel_id=1, source_target_pairs={{0,0},{1,1},{2,6},{3,7},{4,2},{5,3},{6,4},{7,5},{8,8},{9,9},{10,14... | collective-permute-start | bytes 1474568 | tf_op jit(solution)/shard_map/ppermute | solution.py:104
  300.6 13.1 %collective-permute-start.32 = (bf16[3,80,1024]{2,1,0:T(8,128)(2,1)S(1)}, bf16[3,80,1024]{2,1,0:T(8,128)(2,1)S(1)}, u32[]{:S(2)}, u32[]{:S(2)}) collective-permute-start(bf16[3,80,1024]{2,1,0:T(8,128)(2,1)S(1)} %get-tuple-element.111), channel_id=1, source_target_pairs={{1,0},{0,1},{7,2},{6,3},{3,4},{2,5},{5,6},{4,7},{9,8},{8,9},{15,10... | collective-permute-start | bytes 1474568 | tf_op jit(solution)/shard_map/ppermute | solution.py:95
  314.8 22.4 %collective-permute-start.33 = (bf16[3,2,80,1024]{3,2,1,0:T(8,128)(2,1)}, bf16[3,2,80,1024]{3,2,1,0:T(8,128)(2,1)}, u32[]{:S(2)}, u32[]{:S(2)}) collective-permute-start(bf16[3,2,80,1024]{3,2,1,0:T(8,128)(2,1)} %pad_maximum_fusion.14), channel_id=1, source_target_pairs={{0,4},{4,0},{8,12},{12,8},{16,20},{20,16},{24,28},{28,24},{1,5},{5... | collective-permute-start | bytes 2949128 | tf_op jit(solution)/shard_map/ppermute | solution.py:17
  377.6 33.7 %collective-permute-start.46 = (bf16[1,2,256,512]{3,2,1,0:T(8,128)(2,1)}, bf16[1,2,256,512]{3,2,1,0:T(8,128)(2,1)S(1)}, u32[]{:S(2)}, u32[]{:S(2)}) collective-permute-start(bf16[1,2,256,512]{3,2,1,0:T(8,128)(2,1)} %get-tuple-element.59), channel_id=1, source_target_pairs={{0,16},{4,20},{8,24},{12,28},{16,0},{20,4},{24,8},{28,12},{1,17},{... | collective-permute-start | bytes 1572872 | tf_op jit(solution)/shard_map/ppermute | solution.py:17
  379.2 32.2 %collective-permute-start.48 = (bf16[1,2,256,512]{3,2,1,0:T(8,128)(2,1)}, bf16[1,2,256,512]{3,2,1,0:T(8,128)(2,1)}, u32[]{:S(2)}, u32[]{:S(2)}) collective-permute-start(bf16[1,2,256,512]{3,2,1,0:T(8,128)(2,1)} %get-tuple-element.60), channel_id=1, source_target_pairs={{0,8},{4,12},{8,0},{12,4},{16,24},{20,28},{24,16},{28,20},{1,9},{5... | collective-permute-start | bytes 1572872 | tf_op jit(solution)/shard_map/ppermute | solution.py:17
  405.6 14.7 %collective-permute-start.51 = (bf16[1,2,256,512]{3,2,1,0:T(8,128)(2,1)S(1)}, bf16[1,2,256,512]{3,2,1,0:T(8,128)(2,1)S(1)}, u32[]{:S(2)}, u32[]{:S(2)}) collective-permute-start(bf16[1,2,256,512]{3,2,1,0:T(8,128)(2,1)S(1)} %get-tuple-element.65), channel_id=1, source_target_pairs={{0,16},{4,20},{8,24},{12,28},{16,0},{20,4},{24,8},{28,12},{1,17},{... | collective-permute-start | bytes 1572872 | tf_op jit(solution)/shard_map/ppermute | solution.py:17
  406.2 14.9 %collective-permute-start.53 = (bf16[1,2,256,512]{3,2,1,0:T(8,128)(2,1)S(1)}, bf16[1,2,256,512]{3,2,1,0:T(8,128)(2,1)S(1)}, u32[]{:S(2)}, u32[]{:S(2)}) collective-permute-start(bf16[1,2,256,512]{3,2,1,0:T(8,128)(2,1)S(1)} %get-tuple-element.66), channel_id=1, source_target_pairs={{0,8},{4,12},{8,0},{12,4},{16,24},{20,28},{24,16},{28,20},{1,9},{5... | collective-permute-start | bytes 1572872 | tf_op jit(solution)/shard_map/ppermute | solution.py:17
  414.1 29.5 %collective-permute-start.47 = (bf16[2,2,256,512]{3,2,1,0:T(8,128)(2,1)}, bf16[2,2,256,512]{3,2,1,0:T(8,128)(2,1)}, u32[]{:S(2)}, u32[]{:S(2)}) collective-permute-start(bf16[2,2,256,512]{3,2,1,0:T(8,128)(2,1)} %pad_maximum_fusion.6), channel_id=1, source_target_pairs={{0,8},{4,12},{8,0},{12,4},{16,24},{20,28},{24,16},{28,20},{1,9},{5... | collective-permute-start | bytes 3145736 | tf_op jit(solution)/shard_map/ppermute | solution.py:17
  415.7 27.9 %collective-permute-start.49 = (bf16[2,2,256,512]{3,2,1,0:T(8,128)(2,1)S(1)}, bf16[2,2,256,512]{3,2,1,0:T(8,128)(2,1)}, u32[]{:S(2)}, u32[]{:S(2)}) collective-permute-start(bf16[2,2,256,512]{3,2,1,0:T(8,128)(2,1)S(1)} %pad_maximum_fusion.7), channel_id=1, source_target_pairs={{0,16},{4,20},{8,24},{12,28},{16,0},{20,4},{24,8},{28,12},{1,17},{... | collective-permute-start | bytes 3145736 | tf_op jit(solution)/shard_map/ppermute | solution.py:17
  419.8 54.3 %collective-permute-start.34 = (bf16[960,1024]{1,0:T(8,128)(2,1)}, bf16[960,1024]{1,0:T(8,128)(2,1)}, u32[]{:S(2)}, u32[]{:S(2)}) collective-permute-start(bf16[960,1024]{1,0:T(8,128)(2,1)} %add_convert_fusion.1), channel_id=1, source_target_pairs={{0,4},{4,0},{8,12},{12,8},{16,20},{20,16},{24,28},{28,24},{1,5},{5... | collective-permute-start | bytes 5898248 | tf_op jit(solution)/shard_map/ppermute | solution.py:17
  422.4 41.8 %collective-permute-start.52 = (bf16[2,2,256,512]{3,2,1,0:T(8,128)(2,1)}, bf16[2,2,256,512]{3,2,1,0:T(8,128)(2,1)}, u32[]{:S(2)}, u32[]{:S(2)}) collective-permute-start(bf16[2,2,256,512]{3,2,1,0:T(8,128)(2,1)} %pad_maximum_fusion.8), channel_id=1, source_target_pairs={{0,8},{4,12},{8,0},{12,4},{16,24},{20,28},{24,16},{28,20},{1,9},{5... | collective-permute-start | bytes 3145736 | tf_op jit(solution)/shard_map/ppermute | solution.py:17
  425.0 39.2 %collective-permute-start.54 = (bf16[2,2,256,512]{3,2,1,0:T(8,128)(2,1)}, bf16[2,2,256,512]{3,2,1,0:T(8,128)(2,1)}, u32[]{:S(2)}, u32[]{:S(2)}) collective-permute-start(bf16[2,2,256,512]{3,2,1,0:T(8,128)(2,1)} %pad_maximum_fusion.9), channel_id=1, source_target_pairs={{0,16},{4,20},{8,24},{12,28},{16,0},{20,4},{24,8},{28,12},{1,17},{... | collective-permute-start | bytes 3145736 | tf_op jit(solution)/shard_map/ppermute | solution.py:17
  446.9 125.0 %collective-permute-start.50 = (bf16[2,256,512]{2,1,0:T(8,128)(2,1)}, bf16[2,256,512]{2,1,0:T(8,128)(2,1)}, u32[]{:S(2)}, u32[]{:S(2)}) collective-permute-start(bf16[2,256,512]{2,1,0:T(8,128)(2,1)} %slice_bitcast_fusion.11), channel_id=1, source_target_pairs={{0,1},{1,0},{2,3},{3,2},{4,5},{5,4},{6,7},{7,6},{8,9},{9,8},{10,11... | collective-permute-start | bytes 1572872 | tf_op jit(solution)/shard_map/ppermute | solution.py:17
  468.3 94.2 %collective-permute-start.55 = (bf16[2,256,512]{2,1,0:T(8,128)(2,1)}, bf16[2,256,512]{2,1,0:T(8,128)(2,1)}, u32[]{:S(2)}, u32[]{:S(2)}) collective-permute-start(bf16[2,256,512]{2,1,0:T(8,128)(2,1)} %slice_bitcast_fusion.3), channel_id=1, source_target_pairs={{0,1},{1,0},{2,3},{3,2},{4,5},{5,4},{6,7},{7,6},{8,9},{9,8},{10,11... | collective-permute-start | bytes 1572872 | tf_op jit(solution)/shard_map/ppermute | solution.py:17
  556.6 12.4 %collective-permute-start.38 = (bf16[2,4,256,128]{3,2,1,0:T(8,128)(2,1)}, bf16[2,4,256,128]{3,2,1,0:T(8,128)(2,1)}, u32[]{:S(2)}, u32[]{:S(2)}) collective-permute-start(bf16[2,4,256,128]{3,2,1,0:T(8,128)(2,1)} %get-tuple-element.71), channel_id=1, source_target_pairs={{0,16},{4,20},{8,24},{12,28},{16,0},{20,4},{24,8},{28,12},{1,17},{... | collective-permute-start | bytes 1572872 | tf_op jit(solution)/shard_map/ppermute | solution.py:17
  561.0 38.7 %collective-permute-start.35 = (bf16[3,2,80,1024]{3,2,0,1:T(8,128)(2,1)}, bf16[3,2,80,1024]{3,2,0,1:T(8,128)(2,1)}, u32[]{:S(2)}, u32[]{:S(2)}) collective-permute-start(bf16[3,2,80,1024]{3,2,0,1:T(8,128)(2,1)} %copy.382), channel_id=1, source_target_pairs={{0,4},{4,0},{8,12},{12,8},{16,20},{20,16},{24,28},{28,24},{1,5},{5... | collective-permute-start | bytes 2949128 | tf_op jit(solution)/shard_map/ppermute | solution.py:17
  564.8 24.7 %collective-permute-start.56 = (bf16[2,256,512]{2,1,0:T(8,128)(2,1)}, bf16[2,256,512]{2,1,0:T(8,128)(2,1)}, u32[]{:S(2)}, u32[]{:S(2)}) collective-permute-start(bf16[2,256,512]{2,1,0:T(8,128)(2,1)} %fusion.68), channel_id=1, source_target_pairs={{0,2},{1,3},{2,0},{3,1},{4,6},{5,7},{6,4},{7,5},{8,10},{9,11},{10,... | collective-permute-start | bytes 1572872 | tf_op jit(solution)/shard_map/ppermute | solution.py:17
  592.1 60.0 %collective-permute-start.39 = (bf16[4,4,256,128]{3,2,1,0:T(8,128)(2,1)}, bf16[4,4,256,128]{3,2,1,0:T(8,128)(2,1)}, u32[]{:S(2)}, u32[]{:S(2)}) collective-permute-start(bf16[4,4,256,128]{3,2,1,0:T(8,128)(2,1)} %pad_maximum_fusion.4), channel_id=1, source_target_pairs={{0,8},{4,12},{8,0},{12,4},{16,24},{20,28},{24,16},{28,20},{1,9},{5... | collective-permute-start | bytes 3145736 | tf_op jit(solution)/shard_map/ppermute | solution.py:17
  593.7 58.4 %collective-permute-start.41 = (bf16[4,4,256,128]{3,2,1,0:T(8,128)(2,1)}, bf16[4,4,256,128]{3,2,1,0:T(8,128)(2,1)}, u32[]{:S(2)}, u32[]{:S(2)}) collective-permute-start(bf16[4,4,256,128]{3,2,1,0:T(8,128)(2,1)} %pad_maximum_fusion.5), channel_id=1, source_target_pairs={{0,16},{4,20},{8,24},{12,28},{16,0},{20,4},{24,8},{28,12},{1,17},{... | collective-permute-start | bytes 3145736 | tf_op jit(solution)/shard_map/ppermute | solution.py:17
  605.2 61.4 %collective-permute-start.36 = (bf16[3,80,1024]{2,1,0:T(8,128)(2,1)S(1)}, bf16[3,80,1024]{2,1,0:T(8,128)(2,1)S(1)}, u32[]{:S(2)}, u32[]{:S(2)}) collective-permute-start(bf16[3,80,1024]{2,1,0:T(8,128)(2,1)S(1)} %get-tuple-element.104), channel_id=1, source_target_pairs={{0,1},{1,0},{2,7},{3,6},{4,3},{5,2},{6,5},{7,4},{8,9},{9,8},{10,15... | collective-permute-start | bytes 1474568 | tf_op jit(solution)/shard_map/ppermute | solution.py:104
  605.3 61.3 %collective-permute-start.37 = (bf16[3,80,1024]{2,1,0:T(8,128)(2,1)S(1)}, bf16[3,80,1024]{2,1,0:T(8,128)(2,1)S(1)}, u32[]{:S(2)}, u32[]{:S(2)}) collective-permute-start(bf16[3,80,1024]{2,1,0:T(8,128)(2,1)S(1)} %get-tuple-element.105), channel_id=1, source_target_pairs={{0,0},{1,1},{2,6},{3,7},{4,2},{5,3},{6,4},{7,5},{8,8},{9,9},{10,14... | collective-permute-start | bytes 1474568 | tf_op jit(solution)/shard_map/ppermute | solution.py:104
  656.3 13.8 %collective-permute-start.42 = (bf16[4,256,128]{2,1,0:T(8,128)(2,1)S(1)}, bf16[4,256,128]{2,1,0:T(8,128)(2,1)S(1)}, u32[]{:S(2)}, u32[]{:S(2)}) collective-permute-start(bf16[4,256,128]{2,1,0:T(8,128)(2,1)S(1)} %get-tuple-element.94), channel_id=1, source_target_pairs={{0,1},{1,0},{2,3},{3,2},{4,5},{5,4},{6,7},{7,6},{8,9},{9,8},{10,11... | collective-permute-start | bytes 786440 | tf_op jit(solution)/shard_map/ppermute | solution.py:17
  (91 other events, 976.2 us)

commit v2 on v1

v2 whole, which is shorter than its diff:
```python
import functools

import jax
import jax.numpy as jnp
from jax import lax
from jax.experimental import pallas as pl
from jax.experimental.pallas import tpu as pltpu
from jax.sharding import PartitionSpec as P

HEAD = 64
BUF = 64
BF = jnp.bfloat16
F32 = jnp.float32
epsilon = 1e-06
masked_score = -1e30
MIB = 1 << 20
NT = (((1,), (1,)), ((), ()))
NN = (((1,), (0,)), ((), ()))
TN = (((0,), (0,)), ((), ()))
factor = HEAD ** (-0.5)
VMEM_SPEC = pl.BlockSpec(memory_space=pltpu.VMEM)
ANY_SPEC = pl.BlockSpec(memory_space=pl.ANY)


def mm(a, b, dims=NN):
    return lax.dot_general(a, b, dims, preferred_element_type=F32)


def normalise(values):
    average = jnp.mean(values, axis=-1, keepdims=True)
    centred = values - average
    spread = jnp.mean(centred * centred, axis=-1, keepdims=True)
    inv = lax.rsqrt(spread + epsilon)
    return centred * inv, inv


def norm_back(n, inv, scales, grad):
    e = grad * scales
    mean_e = jnp.mean(e, axis=-1, keepdims=True)
    mean_en = jnp.mean(e * n, axis=-1, keepdims=True)
    return (e - mean_e - n * mean_en) * inv


def gelu_parts(inputs):
    normal_cdf = 0.5 + 0.5 * lax.erf(inputs * 0.7071067811865476)
    density = jnp.exp(-0.5 * inputs * inputs) * 0.3989422804014327
    return inputs * normal_cdf, normal_cdf + inputs * density


def for_each(count, step):
    if count <= 4:
        for index in range(count):
            step(index)
    else:
        pl.loop(0, count)(step)


def copy_att(parts, refs, w_scr, sem, kinds, n_i):
    for (j0, i0), ref in zip(parts, refs):
        nj, ni, _, wq, he = ref.shape

        def one(jj, ref=ref, j0=j0, i0=i0, ni=ni, wq=wq, he=he):
            rows = pl.ds(pl.multiple_of((j0 + jj) * wq, wq), wq) if not isinstance(jj, int) else pl.ds((j0 + jj) * wq, wq)
            for ii in range(ni):
                for t in range(kinds):
                    pltpu.make_async_copy(
                        ref.at[jj, ii, t], w_scr.at[rows, pl.ds((t * n_i + i0 + ii) * he, he)], sem
                    ).start()

        for_each(nj, one)
    pltpu.make_async_copy(w_scr, w_scr, sem).wait()


def att_fwd_kernel(parts, n_i, x_ref, g_ref, c_ref, bias_ref, valid_ref, *rest):
    w_refs = rest[: len(parts)]
    n1_ref, qkv_ref, mix_ref, part_ref, w_scr, m_scr, sem = rest[len(parts) :]
    he = 2 * HEAD

    @pl.when(pl.program_id(0) == 0)
    def _():
        copy_att(parts, w_refs, w_scr, sem, 4, n_i)

    hat, _ = normalise(x_ref[0].astype(F32))
    n1 = (hat * g_ref[...] + c_ref[...]).astype(BF)
    n1_ref[...] = n1
    for t in range(3):
        cols = pl.ds(t * n_i * he, n_i * he)
        res = (mm(n1, w_scr[:, cols]) + bias_ref[:, cols]).astype(BF)
        for i in range(n_i):
            qkv_ref[t * n_i + i] = res[:, i * he : (i + 1) * he]
    bias = jnp.where(valid_ref[0] > 0.5, 0.0, masked_score)
    lane = lax.broadcasted_iota(jnp.int32, (1, he), 1)
    low_half = lane < HEAD
    for i in range(n_i):
        q2, k2, v2 = qkv_ref[i], qkv_ref[n_i + i], qkv_ref[2 * n_i + i]
        outs = []
        for h in range(2):
            qm = jnp.where(low_half if h == 0 else ~low_half, q2, jnp.zeros_like(q2))
            s = mm(qm, k2, NT) * factor + bias
            top = jnp.max(s, axis=-1, keepdims=True)
            p = jnp.exp(s - top)
            w = (p / jnp.sum(p, axis=-1, keepdims=True)).astype(BF)
            outs.append(mm(w, v2))
        mixed = jnp.where(low_half, outs[0], outs[1]).astype(BF)
        m_scr[:, i * he : (i + 1) * he] = mixed
    mix_ref[...] = m_scr[...]
    part_ref[...] = mm(m_scr[...], w_scr[:, 3 * n_i * he :], NT).astype(BF)


def att_forward(x, gain, shift, bias, valid, parts, arrays, cost=True):
    images, slots, width = x.shape
    n_i = 4
    he = 2 * HEAD
    rows = images * slots
    row_block = lambda last: pl.BlockSpec((slots, last), lambda a: (a, 0))
    whole = lambda *shape: pl.BlockSpec(shape, lambda a: (0,) * len(shape))
    return pl.pallas_call(
        functools.partial(att_fwd_kernel, parts, n_i),
        grid=(images,),
        in_specs=[
            pl.BlockSpec((1, slots, width), lambda a: (a, 0, 0)),
            whole(1, width),
            whole(1, width),
            whole(1, 3 * n_i * he),
            pl.BlockSpec((1, 1, slots), lambda a: (a, 0, 0)),
        ]
        + [ANY_SPEC] * len(arrays),
        out_specs=[
            row_block(width),
            pl.BlockSpec((3 * n_i, slots, he), lambda a: (0, a, 0)),
            row_block(n_i * he),
            row_block(width),
        ],
        out_shape=[
            jax.ShapeDtypeStruct((rows, width), BF),
            jax.ShapeDtypeStruct((3 * n_i, rows, he), BF),
            jax.ShapeDtypeStruct((rows, n_i * he), BF),
            jax.ShapeDtypeStruct((rows, width), BF),
        ],
        scratch_shapes=[
            pltpu.VMEM((width, 4 * n_i * he), BF),
            pltpu.VMEM((slots, n_i * he), BF),
            pltpu.SemaphoreType.DMA,
        ],
        compiler_params=pltpu.CompilerParams(vmem_limit_bytes=32 * MIB),
        cost_estimate=pl.CostEstimate(flops=8_000_000_000, bytes_accessed=20_000_000, transcendentals=2_500_000),
        name="att_forward",
    )(x, gain, shift, bias, valid, *arrays)


def ffn_kernel(
    parts, n_i, last, x_ref, pa_ref, pb_ref, b_ref, g_ref, c_ref, go_ref, upb_ref, *rest
):
    w_refs = rest[: len(parts)]
    hidden_ref, branch_ref, gn2_ref, grads_ref, upg_ref = rest[len(parts) : len(parts) + 5]
    n2, n2t, got, acc_b, acc_g, wbuf, gbuf, act_s, pre_s, wsem, gsem = rest[len(parts) + 5 :]
    rows, width = x_ref.shape
    fh = last
    n_j, _, _, wq, _ = grads_ref.shape

    def fetch(i, slot):
        for (j0, i0), ref in zip(parts, w_refs):
            nj, ni = ref.shape[:2]
            if not i0 <= i < i0 + ni:
                continue

            def one(jj, ref=ref, j0=j0, i0=i0):
                start = (j0 + jj) * wq
                rws = pl.ds(start if isinstance(jj, int) else pl.multiple_of(start, wq), wq)
                for kind in range(2):
                    pltpu.make_async_copy(
                        ref.at[jj, i - i0, kind], wbuf.at[slot, kind, rws], wsem.at[slot]
                    ).start()

            for_each(nj, one)

    def fetched(slot):
        pltpu.make_async_copy(wbuf.at[slot], wbuf.at[slot], wsem.at[slot]).wait()

    def put(i, slot):
        def one(jj):
            start = jj * wq
            rws = pl.ds(start if isinstance(jj, int) else pl.multiple_of(start, wq), wq)
            for kind in range(2):
                pltpu.make_async_copy(
                    gbuf.at[slot, kind, rws], grads_ref.at[jj, i, kind], gsem.at[slot]
                ).start()

        for_each(n_j, one)

    def stored(slot):
        pltpu.make_async_copy(gbuf.at[slot], gbuf.at[slot], gsem.at[slot]).wait()

    fetch(0, 0)
    block = 192

    @pl.loop(0, rows // block)
    def _(r):
        rw = pl.ds(pl.multiple_of(r * block, block), block)
        h = (
            x_ref[rw, :].astype(F32)
            + (pa_ref[rw, :].astype(F32) + pb_ref[rw, :].astype(F32))
            + b_ref[...]
        )
        hidden_ref[rw, :] = h
        hat, _ = normalise(h)
        n2[rw, :] = (hat * g_ref[...] + c_ref[...]).astype(BF)

    n2t[...] = n2[...].T
    got[...] = go_ref[...].T
    rb = rows // 3
    for i in range(n_i):
        slot = i % 2
        if i + 1 < n_i:
            fetch(i + 1, 1 - slot)
        fetched(slot)

        @pl.loop(0, 3)
        def _(r, i=i, slot=slot):
            rw = pl.ds(pl.multiple_of(r * rb, rb), rb)
            u, w = wbuf[slot, 0], wbuf[slot, 1]
            up = mm(n2[rw, :], u) + upb_ref[i : i + 1, :]
            act, slope = gelu_parts(up)
            act = act.astype(BF)
            act_s[rw, :] = act
            pre = (mm(go_ref[rw, :], w) * slope).astype(BF)
            pre_s[rw, :] = pre
            down = mm(act, w, NT)
            back = mm(pre, u, NT)
            if i == 0:
                acc_b[rw, :] = down
                acc_g[rw, :] = back
            elif i < n_i - 1:
                acc_b[rw, :] += down
                acc_g[rw, :] += back
            else:
                branch_ref[rw, :] = (acc_b[rw, :] + down).astype(BF)
                gn2_ref[rw, :] = (acc_g[rw, :] + back).astype(BF)

        upg_ref[i : i + 1, :] = jnp.sum(pre_s[...].astype(F32), axis=0, keepdims=True)
        if i >= 2:
            stored(slot)
        gbuf[slot, 0] = mm(n2t[...], pre_s[...]).astype(BF)
        gbuf[slot, 1] = mm(got[...], act_s[...]).astype(BF)
        put(i, slot)
    stored((n_i - 2) % 2)
    stored((n_i - 1) % 2)


def ffn(x, pa, pb, b0, gain, shift, go, upb, n_j, parts, arrays):
    rows, width = x.shape
    n_i, fh = upb.shape
    wq = width // n_j
    return pl.pallas_call(
        functools.partial(ffn_kernel, parts, n_i, fh),
        in_specs=[VMEM_SPEC] * 8 + [ANY_SPEC] * len(arrays),
        out_specs=[VMEM_SPEC] * 3 + [ANY_SPEC, VMEM_SPEC],
        out_shape=[
            jax.ShapeDtypeStruct((rows, width), F32),
            jax.ShapeDtypeStruct((rows, width), BF),
            jax.ShapeDtypeStruct((rows, width), BF),
            jax.ShapeDtypeStruct((n_j, n_i, 2, wq, fh), BF),
            jax.ShapeDtypeStruct((n_i, fh), F32),
        ],
        scratch_shapes=[
            pltpu.VMEM((rows, width), BF),
            pltpu.VMEM((width, rows), BF),
            pltpu.VMEM((width, rows), BF),
            pltpu.VMEM((rows, width), F32),
            pltpu.VMEM((rows, width), F32),
            pltpu.VMEM((2, 2, width, fh), BF),
            pltpu.VMEM((2, 2, width, fh), BF),
            pltpu.VMEM((rows, fh), BF),
            pltpu.VMEM((rows, fh), BF),
            pltpu.SemaphoreType.DMA((2,)),
            pltpu.SemaphoreType.DMA((2,)),
        ],
        compiler_params=pltpu.CompilerParams(vmem_limit_bytes=56 * MIB),
        cost_estimate=pl.CostEstimate(flops=36_000_000_000, bytes_accessed=30_000_000, transcendentals=4_000_000),
        name="ffn",
    )(x, pa, pb, b0, gain, shift, go, upb, *arrays)


def att_bwd_kernel(
    parts, n_i, hid_ref, ga_ref, gb_ref, g_ref, go_ref, n1_ref, qkv_ref, mix_ref, valid_ref, *rest
):
    w_refs = rest[: len(parts)]
    gh_ref, gn1_ref, grads_ref, bias_ref, sums_ref = rest[len(parts) : len(parts) + 5]
    ghb, gmix, gq, w_scr, gbuf, sem, gsem = rest[len(parts) + 5 :]
    rows, width = hid_ref.shape
    he = 2 * HEAD
    images = valid_ref.shape[0]
    slots = rows // images
    n_j, _, _, wq, _ = grads_ref.shape
    copy_att(parts, w_refs, w_scr, sem, 4, n_i)
    block = 192
    proj_cols = pl.ds(3 * n_i * he, n_i * he)
    sums_ref[...] = jnp.zeros_like(sums_ref)

    @pl.loop(0, rows // block)
    def _(r):
        rw = pl.ds(pl.multiple_of(r * block, block), block)
        hat, inv = normalise(hid_ref[rw, :])
        grad = ga_ref[rw, :].astype(F32) + gb_ref[rw, :].astype(F32)
        gout = go_ref[rw, :].astype(F32)
        gh = gout + norm_back(hat, inv, g_ref[...], grad)
        gh_ref[rw, :] = gh
        low = gh.astype(BF)
        ghb[rw, :] = low
        sums_ref[0:1, :] += jnp.sum(grad * hat, axis=0, keepdims=True)
        sums_ref[1:2, :] += jnp.sum(grad, axis=0, keepdims=True)
        sums_ref[2:3, :] += jnp.sum(gh, axis=0, keepdims=True)
        sums_ref[3:4, :] += jnp.sum(gout, axis=0, keepdims=True)
        res = mm(low, w_scr[:, proj_cols]).astype(BF)
        for i in range(n_i):
            gmix[i, rw, :] = res[:, i * he : (i + 1) * he]

    def put(kind):
        def one(jj):
            start = jj * wq
            rws = pl.ds(start if isinstance(jj, int) else pl.multiple_of(start, wq), wq)
            for i in range(n_i):
                pltpu.make_async_copy(
                    gbuf.at[kind, rws, pl.ds(i * he, he)], grads_ref.at[jj, i, kind], gsem.at[kind]
                ).start()

        for_each(n_j, one)

    gbuf[3] = mm(ghb[...].T, mix_ref[...]).astype(BF)
    put(3)
    lane = lax.broadcasted_iota(jnp.int32, (1, he), 1)
    low_half = lane < HEAD

    @pl.loop(0, images)
    def _(a):
        rw = pl.ds(pl.multiple_of(a * slots, slots), slots)
        bias = jnp.where(valid_ref[a] > 0.5, 0.0, masked_score)
        for i in range(n_i):
            q2, k2, v2 = qkv_ref[i, rw, :], qkv_ref[n_i + i, rw, :], qkv_ref[2 * n_i + i, rw, :]
            g2 = gmix[i, rw, :]
            dq, dk, dv = [], [], []
            for h in range(2):
                here = low_half if h == 0 else ~low_half
                qm = jnp.where(here, q2, jnp.zeros_like(q2))
                gm = jnp.where(here, g2, jnp.zeros_like(g2))
                st = mm(k2, qm, NT) * factor + bias
                top = jnp.max(st, axis=0, keepdims=True)
                p = jnp.exp(st - top)
                p = p / jnp.sum(p, axis=0, keepdims=True)
                dpt = mm(v2, gm, NT)
                dot = jnp.sum(p * dpt, axis=0, keepdims=True)
                ds = (p * (dpt - dot)).astype(BF)
                dk.append(mm(ds, q2))
                dv.append(mm(p.astype(BF), g2))
                dq.append(mm(ds, k2, TN))
            gq[rw, i * he : (i + 1) * he] = (jnp.where(low_half, dq[0], dq[1]) * factor).astype(BF)
            gq[rw, (n_i + i) * he : (n_i + i + 1) * he] = (
                jnp.where(low_half, dk[0], dk[1]) * factor
            ).astype(BF)
            gq[rw, (2 * n_i + i) * he : (2 * n_i + i + 1) * he] = jnp.where(
                low_half, dv[0], dv[1]
            ).astype(BF)

    n1t = n1_ref[...].T
    for t in range(3):
        cols = pl.ds(t * n_i * he, n_i * he)
        gbuf[t] = mm(n1t, gq[:, cols]).astype(BF)
        put(t)
    bias_ref[...] = jnp.sum(gq[...].astype(F32), axis=0, keepdims=True)
    rb = rows // 3

    @pl.loop(0, 3)
    def _(r):
        rw = pl.ds(pl.multiple_of(r * rb, rb), rb)
        gn1_ref[rw, :] = mm(gq[rw, :], w_scr[:, : 3 * n_i * he], NT).astype(BF)

    for kind in range(4):
        pltpu.make_async_copy(gbuf.at[kind], gbuf.at[kind], gsem.at[kind]).wait()


def att_backward(hidden, ga, gb, gain, go, n1, qkv, mix, valid_t, n_j, parts, arrays):
    rows, width = hidden.shape
    n_i, he = 4, 2 * HEAD
    wq = width // n_j
    return pl.pallas_call(
        functools.partial(att_bwd_kernel, parts, n_i),
        in_specs=[VMEM_SPEC] * 9 + [ANY_SPEC] * len(arrays),
        out_specs=[VMEM_SPEC] * 2 + [ANY_SPEC] + [VMEM_SPEC] * 2,
        out_shape=[
            jax.ShapeDtypeStruct((rows, width), F32),
            jax.ShapeDtypeStruct((rows, width), BF),
            jax.ShapeDtypeStruct((n_j, n_i, 4, wq, he), BF),
            jax.ShapeDtypeStruct((1, 3 * n_i * he), F32),
            jax.ShapeDtypeStruct((8, width), F32),
        ],
        scratch_shapes=[
            pltpu.VMEM((rows, width), BF),
            pltpu.VMEM((n_i, rows, he), BF),
            pltpu.VMEM((rows, 3 * n_i * he), BF),
            pltpu.VMEM((width, 4 * n_i * he), BF),
            pltpu.VMEM((4, width, n_i * he), BF),
            pltpu.SemaphoreType.DMA,
            pltpu.SemaphoreType.DMA((4,)),
        ],
        compiler_params=pltpu.CompilerParams(vmem_limit_bytes=56 * MIB),
        cost_estimate=pl.CostEstimate(flops=20_000_000_000, bytes_accessed=40_000_000, transcendentals=2_500_000),
        name="att_backward",
    )(hidden, ga, gb, gain, go, n1, qkv, mix, valid_t, *arrays)


def swap(x, axis, bits):
    n = lax.axis_size(axis)
    return lax.ppermute(x, axis, [(i, i ^ bits) for i in range(n)])


def gather_q(own):
    n_q = lax.axis_size("dp") // 2
    if n_q != 4:
        blocks = own[None]
        bit = 1
        while bit < n_q:
            blocks = jnp.concatenate([blocks, swap(blocks, "dp", 2 * bit)])
            bit *= 2
        return [(0, 0)], [blocks]
    half = own.shape[0] // 2
    one = swap(own, "dp", 2)
    two = swap(own, "dp", 4)
    three_a = swap(one[:half], "dp", 4)
    three_b = swap(two[half:], "dp", 2)
    places = [(0, 0), (1, 0), (2, 0), (3, 0), (3, half)]
    return places, [v[None] for v in (own, one, two, three_a, three_b)]


def add(*parts):
    total = parts[0].astype(F32)
    for part in parts[1:]:
        total = total + part.astype(F32)
    return total.astype(parts[0].dtype)


def scatter_q(parts):
    n_q = lax.axis_size("dp") // 2
    if n_q != 4:
        bit = n_q // 2
        while bit >= 1:
            parts = add(parts[:bit], swap(parts[bit:], "dp", 2 * bit))
            bit //= 2
        return parts[0]
    half = parts.shape[1] // 2
    into_one = swap(parts[3, :half], "dp", 4)
    into_two = swap(parts[3, half:], "dp", 2)
    one = jnp.concatenate([add(parts[1, :half], into_one), parts[1, half:]])
    two = jnp.concatenate([parts[2, :half], add(parts[2, half:], into_two)])
    return add(parts[0], swap(one, "dp", 2), swap(two, "dp", 4))


def gather_z(own):
    two = swap(own, "mp", 2)
    one = swap(own, "mp", 1)
    three = swap(two, "mp", 1)
    return jnp.stack([own, one, two, three])


def scatter_z(parts):
    into_two = swap(parts[3], "mp", 1)
    return add(parts[0], swap(parts[1], "mp", 1), swap(add(parts[2], into_two), "mp", 2))


def ordered_pair(own, other, core, axis=0):
    return jnp.stack(
        [jnp.where(core == 0, own, other), jnp.where(core == 0, other, own)], axis
    )


def image_routes(n_dp, n_mp, odd):
    pairs = []
    for plane in range(n_dp // 2):
        for core in range(2):
            for z in range(n_mp):
                shift = 2 * core + odd
                worker = (plane * 2 + core) * n_mp + z
                holder = (plane * 2 + (z >> 1)) * n_mp + (z ^ shift)
                pairs.append((holder, worker))
    return pairs


def to_images(x, z):
    n_dp, n_mp = lax.axis_size("dp"), lax.axis_size("mp")
    slots, images, width = x.shape
    groups = jnp.transpose(x, (1, 0, 2)).reshape(2, images // 2, slots, width)
    got = []
    for odd in (0, 1):
        send = lax.dynamic_index_in_dim(groups, (z ^ odd) & 1, 0, False)
        got.append(lax.ppermute(send, ("dp", "mp"), image_routes(n_dp, n_mp, odd)))
    return jnp.stack(got, 1)


def from_images(y, z):
    n_dp, n_mp = lax.axis_size("dp"), lax.axis_size("mp")
    back = []
    for odd in (0, 1):
        routes = [(b, a) for a, b in image_routes(n_dp, n_mp, odd)]
        back.append(lax.ppermute(y[:, odd], ("dp", "mp"), routes))
    flip = (z & 1) == 1
    groups = jnp.concatenate([jnp.where(flip, back[1], back[0]), jnp.where(flip, back[0], back[1])])
    return jnp.transpose(groups, (1, 0, 2))


def local(
    tokens,
    counts,
    norm_gains,
    norm_shifts,
    qkv_weight,
    qkv_bias,
    proj_weight,
    out_biases,
    up_weight,
    up_bias,
    down_weight,
    cotangent,
):
    slots, images, width = tokens.shape
    n_dp, n_mp = lax.axis_size("dp"), lax.axis_size("mp")
    n_q = n_dp // 2
    wq = width // n_q
    dp, z = lax.axis_index("dp"), lax.axis_index("mp")
    q, core = dp >> 1, dp & 1
    own_images = images // 2
    all_slots = slots * n_mp
    rows = own_images * all_slots

    def rel(v):
        blocks = [lax.dynamic_slice_in_dim(v, (q ^ j) * wq, wq, v.ndim - 1) for j in range(n_q)]
        return jnp.concatenate(blocks, -1)

    def half_of(v, which, axis):
        size = v.shape[axis] // 2
        return lax.dynamic_slice_in_dim(v, which * size, size, axis)

    att = jnp.concatenate([qkv_weight, jnp.transpose(proj_weight)[None]])
    ffn_w = jnp.stack([up_weight, jnp.transpose(down_weight)])

    def paired(v):
        got = swap(half_of(v, 1 - core, 2), "dp", 1)
        both = ordered_pair(half_of(v, core, 2), got, core, 1)
        return both.reshape(v.shape[0], wq, -1)

    att_own, ffn_own = paired(att), paired(ffn_w)
    he, fh = att_own.shape[-1], ffn_own.shape[-1]
    bias_own = jnp.concatenate(
        [half_of(qkv_bias, core, 1), half_of(up_bias, core, 0).reshape(-1, he)]
    )
    bias_all = gather_z(bias_own)
    att_places, att_parts = gather_q(gather_z(att_own))

    def whole_rows(v):
        got = to_images(rel(v), z)
        return ordered_pair(got, swap(got, "dp", 1), core, 1).reshape(rows, width)

    other_counts = swap(counts, "dp", 1)
    counts_here = jnp.where((z >> 1) == core, counts, other_counts)
    counts_here = lax.dynamic_slice_in_dim(counts_here, (z & 1) * own_images, own_images, 0)
    slot_ids = jnp.arange(slots, dtype=jnp.int32)
    slot_of = (z ^ jnp.arange(n_mp, dtype=jnp.int32))[:, None] * slots + slot_ids
    valid = (slot_of.reshape(1, -1) < BUF + counts_here[:, None]).astype(F32)
    keep_mine = ((z * slots + slot_ids)[:, None] < BUF + counts[None, :])[:, :, None]

    x = whole_rows(tokens)
    gains, shifts, out_b = rel(norm_gains), rel(norm_shifts), rel(out_biases)
    n_i = n_mp
    bias_rows = jnp.concatenate(
        [bias_all[:, 0].reshape(1, -1), jnp.zeros((1, n_i * he), F32), bias_all[:, 1].reshape(1, -1)], 1
    )
    n1, qkv, mix, part = att_forward(
        x.reshape(own_images, all_slots, width),
        gains[0:1],
        shifts[0:1],
        bias_rows,
        valid[:, None],
        att_places,
        att_parts,
    )

    ffn_z = gather_z(ffn_own)
    ffn_places, ffn_parts = [], []
    for i0 in (0, 2):
        places, arrays = gather_q(ffn_z[i0 : i0 + 2])
        ffn_places += [(j, i + i0) for j, i in places]
        ffn_parts += arrays
    go = whole_rows(jnp.where(keep_mine, cotangent, jnp.zeros_like(cotangent)))
    hidden, branch, gn2, ffn_g, upg = ffn(
        x,
        part,
        swap(part, "dp", 1),
        out_b[0:1],
        gains[1:2],
        shifts[1:2],
        go,
        bias_all[:, 2:].reshape(n_i, fh),
        n_q,
        ffn_places,
        ffn_parts,
    )
    gn2_other = swap(gn2, "dp", 1)
    gh, gn1, att_g, bias_sum, sums = att_backward(
        hidden,
        gn2,
        gn2_other,
        gains[1:2],
        go,
        n1,
        qkv,
        mix,
        valid[:, :, None],
        n_q,
        att_places,
        att_parts,
    )
    ffn_grad = scatter_z(
        jnp.concatenate([scatter_q(ffn_g[:, :2]), scatter_q(ffn_g[:, 2:])])
    )

    row_half = lambda v, which: half_of(v.reshape(own_images, n_mp, slots, width), which, 1)
    theirs = swap(row_half(branch, 1 - core), "dp", 1).astype(F32)
    out_half = row_half(hidden, core) + row_half(branch, core).astype(F32) + theirs + out_b[1]
    block_out = from_images(rel(out_half.astype(BF)), z)
    block_out = jnp.where(keep_mine, block_out, jnp.zeros_like(block_out))

    att_grad = scatter_z(scatter_q(att_g))
    gn1 = row_half(gn1, core).astype(F32) + swap(row_half(gn1, 1 - core), "dp", 1).astype(F32)
    hat1, inv1 = normalise(row_half(x, core).astype(F32))
    input_half = row_half(gh, core) + norm_back(hat1, inv1, gains[0], gn1)
    gain_one, shift_one = jnp.sum(gn1 * hat1, (0, 1, 2)), jnp.sum(gn1, (0, 1, 2))
    input_grad = from_images(rel(input_half.astype(BF)), z)

    def own_shard(grad):
        kinds, _, last = grad.shape
        pair = grad.reshape(kinds, 2, wq // 2, last)
        keep = lax.dynamic_index_in_dim(pair, core, 1, False)
        got = swap(lax.dynamic_index_in_dim(pair, 1 - core, 1, False), "dp", 1)
        return ordered_pair(keep, got, core, 2).reshape(kinds, wq // 2, 2 * last).astype(F32)

    att_shard, ffn_shard = own_shard(att_grad), own_shard(ffn_grad)
    qkv_owned, proj_owned = att_shard[:3], jnp.transpose(att_shard[3])
    up_owned, down_owned = ffn_shard[0], jnp.transpose(ffn_shard[1])

    wide_up = jnp.zeros((n_mp, 2, fh), F32)
    wide_bias = jnp.zeros((2, n_mp, 2, he), F32)
    biases = bias_sum.reshape(3, n_i, he)[0::2]
    for i in range(n_i):
        wide_up = lax.dynamic_update_slice(wide_up, upg[i][None, None], (z ^ i, core, 0))
        wide_bias = lax.dynamic_update_slice(wide_bias, biases[:, i][:, None, None], (0, z ^ i, core, 0))
    small = rel(
        jnp.concatenate(
            [gain_one[None], sums[0:1] * 0.5, shift_one[None], sums[1:2] * 0.5, sums[2:4] * 0.5]
        )
    )
    small, wide_bias, wide_up = lax.psum((small, wide_bias, wide_up), ("dp", "mp"))
    bias_grad = lax.dynamic_index_in_dim(wide_bias, z, 1, False).reshape(2, -1)
    upbias_grad = lax.dynamic_index_in_dim(wide_up, z, 0, False).reshape(-1)
    return (
        block_out,
        input_grad,
        small[0:2],
        small[2:4],
        qkv_owned,
        bias_grad,
        proj_owned,
        small[4:6],
        up_owned,
        upbias_grad,
        down_owned,
    )


def solution(mesh):
    split = P("mp", "dp", None)
    return jax.shard_map(
        local,
        mesh=mesh,
        in_specs=(
            split,
            P("dp"),
            P(),
            P(),
            P(None, "dp", "mp"),
            P(None, "mp"),
            P("mp", "dp"),
            P(),
            P("dp", "mp"),
            P("mp"),
            P("mp", "dp"),
            split,
        ),
        out_specs=(
            split,
            split,
            P(),
            P(),
            P(None, "dp", "mp"),
            P(None, "mp"),
            P("mp", "dp"),
            P(),
            P("dp", "mp"),
            P("mp"),
            P("mp", "dp"),
        ),
        check_vma=False,
    )
```

time: 687 us -> 525 us (0.76)
  local copies, waits for them, and re-layouts: 166 us -> 43.7 us
  matrix products: 102 us -> 0 us
  Pallas kernels: 0 us -> 98.5 us
  starting transfers between devices: 86.8 us -> 54.6 us
  other arithmetic: 71.8 us -> 52.8 us
  waiting for transfers between devices: 205 us -> 222 us
    pallas_call x0 -> x3, Pallas kernels: none -> 98.5 us  [the longest x1 40.4 us: ffn(): pl.pallas_call(functools.partial(ffn_kernel, parts, n_i, fh), in_specs=[V...]
    dot_general x23 -> x0, matrix products: 91.6 us -> none  [the longest x2 11.3 us: local(): grad_act = jnp.einsum('rd,df->rf', go, w[1], preferred_element_type=F32)]
    another operation x19 -> x6, local copies, waits for them, and re-layouts: 41.5 us -> 2.22 us  [the longest x4 2.21 us: ordered_pair(): jnp.stack([jnp.where(core == 0, own, other), jnp.where(core == 0, other,...]
    ppermute x50, waiting for transfers between devices: 187 us -> 217 us  [swap(): return lax.ppermute(x, axis, [(i, i ^ bits) for i in range(n)])]
    ppermute x50, starting transfers between devices: 74.8 us -> 45 us  [swap(): return lax.ppermute(x, axis, [(i, i ^ bits) for i in range(n)])]
    unnamed x176 -> x104, local copies, waits for them, and re-layouts: 35.2 us -> 9.16 us
    slice x27 -> x10, local copies, waits for them, and re-layouts: 28.2 us -> 7.27 us  [the longest x3 3.23 us: gather_q(): three_b = swap(two[half:], 'dp', 2)]
    concatenate x4 -> x2, local copies, waits for them, and re-layouts: 12.6 us -> 0.05 us  [the longest x1 0.04 us: local(): jnp.concatenate([gain_one[None], sums[0:1] * 0.5, shift_one[None], sums[1...]
  transfers between devices with their start and end apart: 58 -> 58, of which waited for: 25 -> 26; matrix products, arithmetic and copies ran while one was open for 37% -> 17% of each run, Pallas kernels for 0% -> 11%
where the time goes in v2:
time: 525 us; the launch traced here: 520 us
  waiting for transfers between devices  222 us (42%)
  Pallas kernels  98.5 us (19%)
  starting transfers between devices  54.6 us (10%)
  other arithmetic  52.8 us (10%)
  blocking collectives  46.2 us (9%)
  local copies, waits for them, and re-layouts  43.7 us (8%)
    ppermute x50, waiting for transfers between devices, swap(): return lax.ppermute(x, axis, [(i, i ^ bits) for i in range(n)])  217 us
    psum x1, blocking collectives, local(): lax.psum((small, wide_bias, wide_up), ('dp', 'mp'))  46.2 us
    ppermute x50, starting transfers between devices, swap(): return lax.ppermute(x, axis, [(i, i ^ bits) for i in range(n)])  45 us
    pallas_call x1, Pallas kernels, ffn(): pl.pallas_call(functools.partial(ffn_kernel, parts, n_i, fh), in_specs=[V...  40.4 us
    pallas_call x1, Pallas kernels, att_backward(): pl.pallas_call(functools.partial(att_bwd_kernel, parts, n_i), in_specs=[V...  38.8 us
    pallas_call x1, Pallas kernels, att_forward(): pl.pallas_call(functools.partial(att_fwd_kernel, parts, n_i), grid=(image...  19.4 us
    convert_element_type x8, other arithmetic, add(): return total.astype(parts[0].dtype)  13.9 us
  transfers between devices with their start and end apart: 58, of which 26 were waited for; matrix products, arithmetic and copies ran while one was open for 17% of the time, Pallas kernels for 11%

profile of v2, /device:TPU:0, one launch (start us, length us, event | category | flops | bytes accessed | tf_op | source)
XLA Modules:
  0.0 519.6 jit_solution(15170317927331038440)
XLA Ops:
  4.7 3.9 collective-permute-start.4
  17.6 1.9 collective-permute-start.1
  20.6 13.5 %collective-permute-done.9 = bf16[4,256,128]{2,1,0:T(8,128)(2,1)} collective-permute-done((bf16[4,256,128]{2,1,0:T(8,128)(2,1)S(1)}, bf16[4,256,128]{2,1,0:T(8,128)(2,1)}, u32[]{:S(2)}, u32[]{:S(2)}) %collective-permute-start.9) | collective-permute-done | bytes 262176 | tf_op jit(solution)/shard_map/ppermute | solution.py:413
  35.0 13.3 %collective-permute-done.8 = bf16[4,256,128]{2,1,0:T(8,128)(2,1)S(1)} collective-permute-done((bf16[4,256,128]{2,1,0:T(8,128)(2,1)S(1)}, bf16[4,256,128]{2,1,0:T(8,128)(2,1)S(1)}, u32[]{:S(2)}, u32[]{:S(2)}) %collective-permute-start.8) | collective-permute-done | bytes 262176 | tf_op jit(solution)/shard_map/ppermute | solution.py:413
  48.3 4.8 collective-permute-done.10
  53.0 2.2 pad_maximum_fusion.2
  55.2 1.8 collective-permute-start.11
  61.6 2.1 collective-permute-start.5
  63.7 10.8 %collective-permute-done.5 = f32[6,128]{1,0:T(8,128)S(1)} collective-permute-done((f32[6,128]{1,0:T(8,128)}, f32[6,128]{1,0:T(8,128)S(1)}, u32[]{:S(2)}, u32[]{:S(2)}) %collective-permute-start.5) | collective-permute-done | bytes 3104 | tf_op jit(solution)/shard_map/ppermute | solution.py:413
  76.0 5.1 collective-permute-done.11
  81.1 3.3 collective-permute-start.25
  90.2 2.1 collective-permute-start.17
  95.1 25.0 %collective-permute-done.25 = bf16[2,256,512]{2,1,0:T(8,128)(2,1)S(1)} collective-permute-done((bf16[2,256,512]{2,1,0:T(8,128)(2,1)S(1)}, bf16[2,256,512]{2,1,0:T(8,128)(2,1)S(1)}, u32[]{:S(2)}, u32[]{:S(2)}) %collective-permute-start.25) | collective-permute-done | bytes 524320 | tf_op jit(solution)/shard_map/ppermute | solution.py:413
  120.7 19.4 %att_forward.1 = (bf16[960,1024]{1,0:T(8,128)(2,1)S(1)}, bf16[12,960,128]{2,1,0:T(8,128)(2,1)S(1)}, bf16[960,512]{1,0:T(8,128)(2,1)S(1)}, bf16[960,1024]{1,0:T(8,128)(2,1)}) custom-call(bf16[3,320,1024]{2,1,0:T(8,128)(2,1)S(1)} %bitcast.266, f32[1,1024]{1,0:T(1,128)S(1)} %get-tuple-element.142.g_ref, f32[1,1024]{1,0:T(1,128)S(1)} %get-tuple-element.140.c_ref, ...), custom_call_target="tpu_custom_call" | custom-call | flops 8000000000 | bytes 20000000 | tf_op jit(solution)/shard_map/att_forward/pallas_call | solution.py:117
  148.8 18.7 %collective-permute-done.22 = bf16[2,2,256,512]{3,2,1,0:T(8,128)(2,1)} collective-permute-done((bf16[2,2,256,512]{3,2,1,0:T(8,128)(2,1)}, bf16[2,2,256,512]{3,2,1,0:T(8,128)(2,1)}, u32[]{:S(2)}, u32[]{:S(2)}) %collective-permute-start.22) | collective-permute-done | bytes 1048608 | tf_op jit(solution)/shard_map/ppermute | solution.py:413
  171.7 18.2 %collective-permute-done.28 = bf16[2,2,256,512]{3,2,1,0:T(8,128)(2,1)} collective-permute-done((bf16[2,2,256,512]{3,2,1,0:T(8,128)(2,1)S(1)}, bf16[2,2,256,512]{3,2,1,0:T(8,128)(2,1)}, u32[]{:S(2)}, u32[]{:S(2)}) %collective-permute-start.28) | collective-permute-done | bytes 1048608 | tf_op jit(solution)/shard_map/ppermute | solution.py:413
  197.1 3.9 collective-permute-done.23
  201.1 10.8 %collective-permute-done.29 = bf16[1,2,256,512]{3,2,1,0:T(8,128)(2,1)S(1)} collective-permute-done((bf16[1,2,256,512]{3,2,1,0:T(8,128)(2,1)S(1)}, bf16[1,2,256,512]{3,2,1,0:T(8,128)(2,1)S(1)}, u32[]{:S(2)}, u32[]{:S(2)}) %collective-permute-start.29) | collective-permute-done | bytes 524320 | tf_op jit(solution)/shard_map/ppermute | solution.py:413
  212.8 40.4 %ffn.1 = (f32[960,1024]{1,0:T(8,128)}, bf16[960,1024]{1,0:T(8,128)(2,1)}, bf16[960,1024]{1,0:T(8,128)(2,1)}, bf16[4,4,2,256,512]{4,3,2,1,0:T(8,128)(2,1)}, f32[4,512]{1,0:T(4,128)}) custom-call(bf16[960,1024]{1,0:T(8,128)(2,1)} %bitcast.267, bf16[960,1024]{1,0:T(8,128)(2,1)} %get-tuple-element.25.pa_ref, bf16[960,1024]{1,0:T(8,128)(2,1)} %collective-permute-done.15.pb_ref, ...), custom_call_target="tpu_custom_call" | custom-call | flops 35999997952 | bytes 30000000 | tf_op jit(solution)/shard_map/ffn/pallas_call | solution.py:254
  255.9 4.0 slice_bitcast_fusion.11
  264.9 1.8 copy.64
  267.0 8.0 %collective-permute-done.46 = bf16[1,2,256,512]{3,2,1,0:T(8,128)(2,1)} collective-permute-done((bf16[1,2,256,512]{3,2,1,0:T(8,128)(2,1)}, bf16[1,2,256,512]{3,2,1,0:T(8,128)(2,1)}, u32[]{:S(2)}, u32[]{:S(2)}) %collective-permute-start.46) | collective-permute-done | bytes 524320 | tf_op jit(solution)/shard_map/ppermute | solution.py:413
  275.5 10.3 %collective-permute-done.51 = bf16[1,2,256,512]{3,2,1,0:T(8,128)(2,1)} collective-permute-done((bf16[1,2,256,512]{3,2,1,0:T(8,128)(2,1)}, bf16[1,2,256,512]{3,2,1,0:T(8,128)(2,1)}, u32[]{:S(2)}, u32[]{:S(2)}) %collective-permute-start.51) | collective-permute-done | bytes 524320 | tf_op jit(solution)/shard_map/ppermute | solution.py:413
  286.1 2.8 fusion.30
  288.8 1.8 fusion.20
  291.0 2.0 collective-permute-start.32
  301.0 4.3 collective-permute-done.32
  311.6 9.2 %collective-permute-done.52 = bf16[2,2,256,512]{3,2,1,0:T(8,128)(2,1)} collective-permute-done((bf16[2,2,256,512]{3,2,1,0:T(8,128)(2,1)S(1)}, bf16[2,2,256,512]{3,2,1,0:T(8,128)(2,1)}, u32[]{:S(2)}, u32[]{:S(2)}) %collective-permute-start.52) | collective-permute-done | bytes 1048608 | tf_op jit(solution)/shard_map/ppermute | solution.py:413
  320.8 2.7 collective-permute-done.54
  323.5 19.6 %collective-permute-done.47 = bf16[2,2,256,512]{3,2,1,0:T(8,128)(2,1)} collective-permute-done((bf16[2,2,256,512]{3,2,1,0:T(8,128)(2,1)}, bf16[2,2,256,512]{3,2,1,0:T(8,128)(2,1)}, u32[]{:S(2)}, u32[]{:S(2)}) %collective-permute-start.47) | collective-permute-done | bytes 1048608 | tf_op jit(solution)/shard_map/ppermute | solution.py:413
  343.2 2.5 collective-permute-done.49
  345.7 3.7 fusion.8
  350.5 1.9 collective-permute-start.50
  352.4 38.8 %att_backward.1 = (f32[960,1024]{1,0:T(8,128)}, bf16[960,1024]{1,0:T(8,128)(2,1)}, bf16[4,4,4,256,128]{4,3,2,1,0:T(8,128)(2,1)}, f32[1,1536]{1,0:T(1,128)}, f32[8,1024]{1,0:T(8,128)}) custom-call(f32[960,1024]{1,0:T(8,128)} %get-tuple-element.26.hid_ref, bf16[960,1024]{1,0:T(8,128)(2,1)} %get-tuple-element.28.ga_ref, ...), custom_call_target="tpu_custom_call" | custom-call | flops 20000000000 | bytes 40000000 | tf_op jit(solution)/shard_map/att_backward/pallas_call | solution.py:385
  391.2 3.0 slice_bitcast_fusion.15
  401.2 6.4 %collective-permute-done.38 = bf16[2,4,256,128]{3,2,1,0:T(8,128)(2,1)} collective-permute-done((bf16[2,4,256,128]{3,2,1,0:T(8,128)(2,1)}, bf16[2,4,256,128]{3,2,1,0:T(8,128)(2,1)}, u32[]{:S(2)}, u32[]{:S(2)}) %collective-permute-start.38) | collective-permute-done | bytes 524320 | tf_op jit(solution)/shard_map/ppermute | solution.py:413
  408.9 2.6 fusion.32
  411.5 14.3 %collective-permute-done.56 = bf16[2,256,512]{2,1,0:T(8,128)(2,1)} collective-permute-done((bf16[2,256,512]{2,1,0:T(8,128)(2,1)}, bf16[2,256,512]{2,1,0:T(8,128)(2,1)}, u32[]{:S(2)}, u32[]{:S(2)}) %collective-permute-start.56) | collective-permute-done | bytes 524320 | tf_op jit(solution)/shard_map/ppermute | solution.py:413
  428.1 1.8 copy.72
  429.9 2.3 pad_maximum_fusion.5
  439.4 2.4 fusion.16
  441.8 2.7 fusion.15
  445.8 46.2 %all-reduce = (f32[6,1024]{1,0:T(8,128)S(1)}, f32[2,4,2,128]{3,2,0,1:T(2,128)S(1)}, f32[4,2,512]{2,1,0:T(2,128)S(1)}) all-reduce(f32[6,1024]{1,0:T(8,128)S(1)} %pad_maximum_fusion.19, f32[2,4,2,128]{3,2,0,1:T(2,128)S(1)} %dynamic_update_slice.27, f32[4,2,512]{2,1,0:T(2,128)S(1)} %copy-done.33), channel_id=1, replica_groups=mesh['dp'=8,'mp'=4] {'dp','mp'}, use_global_device_ids=true, to_apply=%region_6.7 | all-reduce | flops 12288 | bytes 98304 | tf_op jit(solution)/shard_map/psum | solution.py:659
  492.1 2.3 fusion.10
  496.3 2.0 collective-permute-start.42
  498.3 8.2 %collective-permute-done.43 = bf16[4,256,128]{2,1,0:T(8,128)(2,1)S(1)} collective-permute-done((bf16[4,256,128]{2,1,0:T(8,128)(2,1)S(1)}, bf16[4,256,128]{2,1,0:T(8,128)(2,1)S(1)}, u32[]{:S(2)}, u32[]{:S(2)}) %collective-permute-start.43) | collective-permute-done | bytes 262176 | tf_op jit(solution)/shard_map/ppermute | solution.py:413
  506.7 3.4 collective-permute-done.42
  510.2 6.0 %collective-permute-done.44 = bf16[4,256,128]{2,1,0:T(8,128)(2,1)S(1)} collective-permute-done((bf16[4,256,128]{2,1,0:T(8,128)(2,1)S(1)}, bf16[4,256,128]{2,1,0:T(8,128)(2,1)S(1)}, u32[]{:S(2)}, u32[]{:S(2)}) %collective-permute-start.44) | collective-permute-done | bytes 262176 | tf_op jit(solution)/shard_map/ppermute | solution.py:413
  (305 shorter events, 99.2 us)
Async XLA Ops:
  4.7 55.4 %collective-permute-start.4 = (f32[6,128]{1,0:T(8,128)}, f32[6,128]{1,0:T(8,128)}, u32[]{:S(2)}, u32[]{:S(2)}) collective-permute-start(f32[6,128]{1,0:T(8,128)} %get-tuple-element.160), channel_id=1, source_target_pairs={{0,2},{1,3},{2,0},{3,1},{4,6},{5,7},{6,4},{7,5},{8,10},{9,11},{10,... | collective-permute-start | bytes 9224 | tf_op jit(solution)/shard_map/ppermute | solution.py:413
  15.9 18.3 %collective-permute-start.9 = (bf16[4,256,128]{2,1,0:T(8,128)(2,1)S(1)}, bf16[4,256,128]{2,1,0:T(8,128)(2,1)}, u32[]{:S(2)}, u32[]{:S(2)}) collective-permute-start(bf16[4,256,128]{2,1,0:T(8,128)(2,1)S(1)} %bitcast.301), channel_id=1, source_target_pairs={{0,2},{1,3},{2,0},{3,1},{4,6},{5,7},{6,4},{7,5},{8,10},{9,11},{10,... | collective-permute-start | bytes 786440 | tf_op jit(solution)/shard_map/ppermute | solution.py:413
  16.9 38.3 %collective-permute-start = (bf16[3,80,1024]{2,1,0:T(8,128)(2,1)S(1)}, bf16[3,80,1024]{2,1,0:T(8,128)(2,1)S(1)}, u32[]{:S(2)}, u32[]{:S(2)}) collective-permute-start(bf16[3,80,1024]{2,1,0:T(8,128)(2,1)S(1)} %get-tuple-element.106), channel_id=1, source_target_pairs={{0,0},{1,1},{6,2},{7,3},{2,4},{3,5},{4,6},{5,7},{8,8},{9,9},{14,10... | collective-permute-start | bytes 1474568 | tf_op jit(solution)/shard_map/ppermute | solution.py:494
  17.6 39.4 %collective-permute-start.1 = (bf16[3,80,1024]{2,1,0:T(8,128)(2,1)}, bf16[3,80,1024]{2,1,0:T(8,128)(2,1)S(1)}, u32[]{:S(2)}, u32[]{:S(2)}) collective-permute-start(bf16[3,80,1024]{2,1,0:T(8,128)(2,1)} %get-tuple-element.107), channel_id=1, source_target_pairs={{1,0},{0,1},{7,2},{6,3},{3,4},{2,5},{5,6},{4,7},{9,8},{8,9},{15,10... | collective-permute-start | bytes 1474568 | tf_op jit(solution)/shard_map/ppermute | solution.py:494
  20.4 27.9 %collective-permute-start.8 = (bf16[4,256,128]{2,1,0:T(8,128)(2,1)S(1)}, bf16[4,256,128]{2,1,0:T(8,128)(2,1)S(1)}, u32[]{:S(2)}, u32[]{:S(2)}) collective-permute-start(bf16[4,256,128]{2,1,0:T(8,128)(2,1)S(1)} %bitcast.302), channel_id=1, source_target_pairs={{0,1},{1,0},{2,3},{3,2},{4,5},{5,4},{6,7},{7,6},{8,9},{9,8},{10,11... | collective-permute-start | bytes 786440 | tf_op jit(solution)/shard_map/ppermute | solution.py:413
  34.1 18.9 %collective-permute-start.10 = (bf16[4,256,128]{2,1,0:T(8,128)(2,1)}, bf16[4,256,128]{2,1,0:T(8,128)(2,1)S(1)}, u32[]{:S(2)}, u32[]{:S(2)}) collective-permute-start(bf16[4,256,128]{2,1,0:T(8,128)(2,1)} %collective-permute-done.9), channel_id=1, source_target_pairs={{0,1},{1,0},{2,3},{3,2},{4,5},{5,4},{6,7},{7,6},{8,9},{9,8},{10,11... | collective-permute-start | bytes 786440 | tf_op jit(solution)/shard_map/ppermute | solution.py:413
  55.2 25.9 %collective-permute-start.11 = (bf16[4,4,256,128]{3,2,1,0:T(8,128)(2,1)}, bf16[4,4,256,128]{3,2,1,0:T(8,128)(2,1)S(1)}, u32[]{:S(2)}, u32[]{:S(2)}) collective-permute-start(bf16[4,4,256,128]{3,2,1,0:T(8,128)(2,1)} %get-tuple-element.82), channel_id=1, source_target_pairs={{0,8},{4,12},{8,0},{12,4},{16,24},{20,28},{24,16},{28,20},{1,9},{5... | collective-permute-start | bytes 3145736 | tf_op jit(solution)/shard_map/ppermute | solution.py:413
  57.1 27.4 %collective-permute-start.12 = (bf16[4,4,256,128]{3,2,1,0:T(8,128)(2,1)}, bf16[4,4,256,128]{3,2,1,0:T(8,128)(2,1)}, u32[]{:S(2)}, u32[]{:S(2)}) collective-permute-start(bf16[4,4,256,128]{3,2,1,0:T(8,128)(2,1)} %get-tuple-element.82), channel_id=1, source_target_pairs={{0,16},{4,20},{8,24},{12,28},{16,0},{20,4},{24,8},{28,12},{1,17},{... | collective-permute-start | bytes 3145736 | tf_op jit(solution)/shard_map/ppermute | solution.py:413
  59.6 30.6 %collective-permute-start.2 = (bf16[3,2,80,1024]{3,2,1,0:T(8,128)(2,1)}, bf16[3,2,80,1024]{3,2,1,0:T(8,128)(2,1)}, u32[]{:S(2)}, u32[]{:S(2)}) collective-permute-start(bf16[3,2,80,1024]{3,2,1,0:T(8,128)(2,1)} %pad_maximum_fusion.12), channel_id=1, source_target_pairs={{0,4},{4,0},{8,12},{12,8},{16,20},{20,16},{24,28},{28,24},{1,5},{5... | collective-permute-start | bytes 2949128 | tf_op jit(solution)/shard_map/ppermute | solution.py:413
  60.1 27.1 %collective-permute-start.20 = (bf16[2,256,512]{2,1,0:T(8,128)(2,1)S(1)}, bf16[2,256,512]{2,1,0:T(8,128)(2,1)S(1)}, u32[]{:S(2)}, u32[]{:S(2)}) collective-permute-start(bf16[2,256,512]{2,1,0:T(8,128)(2,1)S(1)} %bitcast.285), channel_id=1, source_target_pairs={{0,1},{1,0},{2,3},{3,2},{4,5},{5,4},{6,7},{7,6},{8,9},{9,8},{10,11... | collective-permute-start | bytes 1572872 | tf_op jit(solution)/shard_map/ppermute | solution.py:413
  74.5 68.3 %collective-permute-start.16 = (bf16[3,80,1024]{2,1,0:T(8,128)(2,1)S(1)}, bf16[3,80,1024]{2,1,0:T(8,128)(2,1)S(1)}, u32[]{:S(2)}, u32[]{:S(2)}) collective-permute-start(bf16[3,80,1024]{2,1,0:T(8,128)(2,1)S(1)} %get-tuple-element.100), channel_id=1, source_target_pairs={{0,0},{1,1},{6,2},{7,3},{2,4},{3,5},{4,6},{5,7},{8,8},{9,9},{14,10... | collective-permute-start | bytes 1474568 | tf_op jit(solution)/shard_map/ppermute | solution.py:494
  81.1 39.1 %collective-permute-start.25 = (bf16[2,256,512]{2,1,0:T(8,128)(2,1)S(1)}, bf16[2,256,512]{2,1,0:T(8,128)(2,1)S(1)}, u32[]{:S(2)}, u32[]{:S(2)}) collective-permute-start(bf16[2,256,512]{2,1,0:T(8,128)(2,1)S(1)} %bitcast.286), channel_id=1, source_target_pairs={{0,2},{1,3},{2,0},{3,1},{4,6},{5,7},{6,4},{7,5},{8,10},{9,11},{10,... | collective-permute-start | bytes 1572872 | tf_op jit(solution)/shard_map/ppermute | solution.py:413
  84.5 36.2 %collective-permute-start.13 = (bf16[2,4,256,128]{3,2,1,0:T(8,128)(2,1)S(1)}, bf16[2,4,256,128]{3,2,1,0:T(8,128)(2,1)S(1)}, u32[]{:S(2)}, u32[]{:S(2)}) collective-permute-start(bf16[2,4,256,128]{3,2,1,0:T(8,128)(2,1)S(1)} %slice.299), channel_id=1, source_target_pairs={{0,16},{4,20},{8,24},{12,28},{16,0},{20,4},{24,8},{28,12},{1,17},{... | collective-permute-start | bytes 1572872 | tf_op jit(solution)/shard_map/ppermute | solution.py:413
  87.2 33.5 %collective-permute-start.14 = (bf16[2,4,256,128]{3,2,1,0:T(8,128)(2,1)S(1)}, bf16[2,4,256,128]{3,2,1,0:T(8,128)(2,1)S(1)}, u32[]{:S(2)}, u32[]{:S(2)}) collective-permute-start(bf16[2,4,256,128]{3,2,1,0:T(8,128)(2,1)S(1)} %slice.300), channel_id=1, source_target_pairs={{0,8},{4,12},{8,0},{12,4},{16,24},{20,28},{24,16},{28,20},{1,9},{5... | collective-permute-start | bytes 1572872 | tf_op jit(solution)/shard_map/ppermute | solution.py:413
  90.2 54.2 %collective-permute-start.17 = (bf16[3,80,1024]{2,1,0:T(8,128)(2,1)S(1)}, bf16[3,80,1024]{2,1,0:T(8,128)(2,1)S(1)}, u32[]{:S(2)}, u32[]{:S(2)}) collective-permute-start(bf16[3,80,1024]{2,1,0:T(8,128)(2,1)S(1)} %get-tuple-element.101), channel_id=1, source_target_pairs={{1,0},{0,1},{7,2},{6,3},{3,4},{2,5},{5,6},{4,7},{9,8},{8,9},{15,10... | collective-permute-start | bytes 1474568 | tf_op jit(solution)/shard_map/ppermute | solution.py:494
  120.2 25.8 %collective-permute-start.21 = (bf16[2,2,256,512]{3,2,1,0:T(8,128)(2,1)}, bf16[2,2,256,512]{3,2,1,0:T(8,128)(2,1)S(1)}, u32[]{:S(2)}, u32[]{:S(2)}) collective-permute-start(bf16[2,2,256,512]{3,2,1,0:T(8,128)(2,1)} %get-tuple-element.80), channel_id=1, source_target_pairs={{0,8},{4,12},{8,0},{12,4},{16,24},{20,28},{24,16},{28,20},{1,9},{5... | collective-permute-start | bytes 3145736 | tf_op jit(solution)/shard_map/ppermute | solution.py:413
  120.7 20.4 %collective-permute-start.26 = (bf16[2,256,512]{2,1,0:T(8,128)(2,1)S(1)}, bf16[2,256,512]{2,1,0:T(8,128)(2,1)S(1)}, u32[]{:S(2)}, u32[]{:S(2)}) collective-permute-start(bf16[2,256,512]{2,1,0:T(8,128)(2,1)S(1)} %collective-permute-done.25), channel_id=1, source_target_pairs={{0,1},{1,0},{2,3},{3,2},{4,5},{5,4},{6,7},{7,6},{8,9},{9,8},{10,11... | collective-permute-start | bytes 1572872 | tf_op jit(solution)/shard_map/ppermute | solution.py:413
  141.1 70.7 %collective-permute-start.15 = (bf16[960,1024]{1,0:T(8,128)(2,1)}, bf16[960,1024]{1,0:T(8,128)(2,1)}, u32[]{:S(2)}, u32[]{:S(2)}) collective-permute-start(bf16[960,1024]{1,0:T(8,128)(2,1)} %get-tuple-element.25.pa_ref), channel_id=1, source_target_pairs={{0,4},{4,0},{8,12},{12,8},{16,20},{20,16},{24,28},{28,24},{1,5},{5... | collective-permute-start | bytes 5898248 | tf_op jit(solution)/shard_map/ppermute | solution.py:413
  141.1 26.3 %collective-permute-start.22 = (bf16[2,2,256,512]{3,2,1,0:T(8,128)(2,1)}, bf16[2,2,256,512]{3,2,1,0:T(8,128)(2,1)}, u32[]{:S(2)}, u32[]{:S(2)}) collective-permute-start(bf16[2,2,256,512]{3,2,1,0:T(8,128)(2,1)} %get-tuple-element.80), channel_id=1, source_target_pairs={{0,16},{4,20},{8,24},{12,28},{16,0},{20,4},{24,8},{28,12},{1,17},{... | collective-permute-start | bytes 3145736 | tf_op jit(solution)/shard_map/ppermute | solution.py:413
  142.8 26.2 %collective-permute-start.27 = (bf16[2,2,256,512]{3,2,1,0:T(8,128)(2,1)S(1)}, bf16[2,2,256,512]{3,2,1,0:T(8,128)(2,1)}, u32[]{:S(2)}, u32[]{:S(2)}) collective-permute-start(bf16[2,2,256,512]{3,2,1,0:T(8,128)(2,1)S(1)} %get-tuple-element.78), channel_id=1, source_target_pairs={{0,8},{4,12},{8,0},{12,4},{16,24},{20,28},{24,16},{28,20},{1,9},{5... | collective-permute-start | bytes 3145736 | tf_op jit(solution)/shard_map/ppermute | solution.py:413
  144.3 45.6 %collective-permute-start.28 = (bf16[2,2,256,512]{3,2,1,0:T(8,128)(2,1)S(1)}, bf16[2,2,256,512]{3,2,1,0:T(8,128)(2,1)}, u32[]{:S(2)}, u32[]{:S(2)}) collective-permute-start(bf16[2,2,256,512]{3,2,1,0:T(8,128)(2,1)S(1)} %get-tuple-element.78), channel_id=1, source_target_pairs={{0,16},{4,20},{8,24},{12,28},{16,0},{20,4},{24,8},{28,12},{1,17},{... | collective-permute-start | bytes 3145736 | tf_op jit(solution)/shard_map/ppermute | solution.py:413
  147.0 44.6 %collective-permute-start.18 = (bf16[3,2,80,1024]{3,2,1,0:T(8,128)(2,1)S(1)}, bf16[3,2,80,1024]{3,2,1,0:T(8,128)(2,1)}, u32[]{:S(2)}, u32[]{:S(2)}) collective-permute-start(bf16[3,2,80,1024]{3,2,1,0:T(8,128)(2,1)S(1)} %pad_maximum_fusion.14), channel_id=1, source_target_pairs={{0,4},{4,0},{8,12},{12,8},{16,20},{20,16},{24,28},{28,24},{1,5},{5... | collective-permute-start | bytes 2949128 | tf_op jit(solution)/shard_map/ppermute | solution.py:413
  167.5 33.6 %collective-permute-start.23 = (bf16[1,2,256,512]{3,2,1,0:T(8,128)(2,1)S(1)}, bf16[1,2,256,512]{3,2,1,0:T(8,128)(2,1)S(1)}, u32[]{:S(2)}, u32[]{:S(2)}) collective-permute-start(bf16[1,2,256,512]{3,2,1,0:T(8,128)(2,1)S(1)} %slice.304), channel_id=1, source_target_pairs={{0,16},{4,20},{8,24},{12,28},{16,0},{20,4},{24,8},{28,12},{1,17},{... | collective-permute-start | bytes 1572872 | tf_op jit(solution)/shard_map/ppermute | solution.py:413
  169.1 32.0 %collective-permute-start.24 = (bf16[1,2,256,512]{3,2,1,0:T(8,128)(2,1)S(1)}, bf16[1,2,256,512]{3,2,1,0:T(8,128)(2,1)S(1)}, u32[]{:S(2)}, u32[]{:S(2)}) collective-permute-start(bf16[1,2,256,512]{3,2,1,0:T(8,128)(2,1)S(1)} %slice.305), channel_id=1, source_target_pairs={{0,8},{4,12},{8,0},{12,4},{16,24},{20,28},{24,16},{28,20},{1,9},{5... | collective-permute-start | bytes 1572872 | tf_op jit(solution)/shard_map/ppermute | solution.py:413
  189.9 21.9 %collective-permute-start.29 = (bf16[1,2,256,512]{3,2,1,0:T(8,128)(2,1)S(1)}, bf16[1,2,256,512]{3,2,1,0:T(8,128)(2,1)S(1)}, u32[]{:S(2)}, u32[]{:S(2)}) collective-permute-start(bf16[1,2,256,512]{3,2,1,0:T(8,128)(2,1)S(1)} %slice.306), channel_id=1, source_target_pairs={{0,16},{4,20},{8,24},{12,28},{16,0},{20,4},{24,8},{28,12},{1,17},{... | collective-permute-start | bytes 1572872 | tf_op jit(solution)/shard_map/ppermute | solution.py:413
  191.5 20.3 %collective-permute-start.30 = (bf16[1,2,256,512]{3,2,1,0:T(8,128)(2,1)S(1)}, bf16[1,2,256,512]{3,2,1,0:T(8,128)(2,1)S(1)}, u32[]{:S(2)}, u32[]{:S(2)}) collective-permute-start(bf16[1,2,256,512]{3,2,1,0:T(8,128)(2,1)S(1)} %slice.307), channel_id=1, source_target_pairs={{0,8},{4,12},{8,0},{12,4},{16,24},{20,28},{24,16},{28,20},{1,9},{5... | collective-permute-start | bytes 1572872 | tf_op jit(solution)/shard_map/ppermute | solution.py:413
  255.9 32.9 %collective-permute-start.31 = (bf16[3,2,80,1024]{3,2,0,1:T(8,128)(2,1)}, bf16[3,2,80,1024]{3,2,0,1:T(8,128)(2,1)}, u32[]{:S(2)}, u32[]{:S(2)}) collective-permute-start(bf16[3,2,80,1024]{3,2,0,1:T(8,128)(2,1)} %copy.77), channel_id=1, source_target_pairs={{0,4},{4,0},{8,12},{12,8},{16,20},{20,16},{24,28},{28,24},{1,5},{5... | collective-permute-start | bytes 2949128 | tf_op jit(solution)/shard_map/ppermute | solution.py:413
  259.9 15.0 %collective-permute-start.46 = (bf16[1,2,256,512]{3,2,1,0:T(8,128)(2,1)}, bf16[1,2,256,512]{3,2,1,0:T(8,128)(2,1)}, u32[]{:S(2)}, u32[]{:S(2)}) collective-permute-start(bf16[1,2,256,512]{3,2,1,0:T(8,128)(2,1)} %get-tuple-element.52), channel_id=1, source_target_pairs={{0,16},{4,20},{8,24},{12,28},{16,0},{20,4},{24,8},{28,12},{1,17},{... | collective-permute-start | bytes 1572872 | tf_op jit(solution)/shard_map/ppermute | solution.py:413
  260.4 15.1 %collective-permute-start.48 = (bf16[1,2,256,512]{3,2,1,0:T(8,128)(2,1)}, bf16[1,2,256,512]{3,2,1,0:T(8,128)(2,1)}, u32[]{:S(2)}, u32[]{:S(2)}) collective-permute-start(bf16[1,2,256,512]{3,2,1,0:T(8,128)(2,1)} %get-tuple-element.57), channel_id=1, source_target_pairs={{0,8},{4,12},{8,0},{12,4},{16,24},{20,28},{24,16},{28,20},{1,9},{5... | collective-permute-start | bytes 1572872 | tf_op jit(solution)/shard_map/ppermute | solution.py:413
  261.9 23.9 %collective-permute-start.51 = (bf16[1,2,256,512]{3,2,1,0:T(8,128)(2,1)}, bf16[1,2,256,512]{3,2,1,0:T(8,128)(2,1)}, u32[]{:S(2)}, u32[]{:S(2)}) collective-permute-start(bf16[1,2,256,512]{3,2,1,0:T(8,128)(2,1)} %get-tuple-element.56), channel_id=1, source_target_pairs={{0,16},{4,20},{8,24},{12,28},{16,0},{20,4},{24,8},{28,12},{1,17},{... | collective-permute-start | bytes 1572872 | tf_op jit(solution)/shard_map/ppermute | solution.py:413
  263.5 22.6 %collective-permute-start.53 = (bf16[1,2,256,512]{3,2,1,0:T(8,128)(2,1)}, bf16[1,2,256,512]{3,2,1,0:T(8,128)(2,1)}, u32[]{:S(2)}, u32[]{:S(2)}) collective-permute-start(bf16[1,2,256,512]{3,2,1,0:T(8,128)(2,1)} %get-tuple-element.53), channel_id=1, source_target_pairs={{0,8},{4,12},{8,0},{12,4},{16,24},{20,28},{24,16},{28,20},{1,9},{5... | collective-permute-start | bytes 1572872 | tf_op jit(solution)/shard_map/ppermute | solution.py:413
  275.0 77.4 %collective-permute-start.34 = (bf16[960,1024]{1,0:T(8,128)(2,1)}, bf16[960,1024]{1,0:T(8,128)(2,1)}, u32[]{:S(2)}, u32[]{:S(2)}) collective-permute-start(bf16[960,1024]{1,0:T(8,128)(2,1)} %get-tuple-element.28.ga_ref), channel_id=1, source_target_pairs={{0,4},{4,0},{8,12},{12,8},{16,20},{20,16},{24,28},{28,24},{1,5},{5... | collective-permute-start | bytes 5898248 | tf_op jit(solution)/shard_map/ppermute | solution.py:413
  291.0 14.3 %collective-permute-start.32 = (bf16[3,80,1024]{2,1,0:T(8,128)(2,1)S(1)}, bf16[3,80,1024]{2,1,0:T(8,128)(2,1)}, u32[]{:S(2)}, u32[]{:S(2)}) collective-permute-start(bf16[3,80,1024]{2,1,0:T(8,128)(2,1)S(1)} %get-tuple-element.94), channel_id=1, source_target_pairs={{0,1},{1,0},{2,7},{3,6},{4,3},{5,2},{6,5},{7,4},{8,9},{9,8},{10,15... | collective-permute-start | bytes 1474568 | tf_op jit(solution)/shard_map/ppermute | solution.py:503
  293.0 13.7 %collective-permute-start.33 = (bf16[3,80,1024]{2,1,0:T(8,128)(2,1)S(1)}, bf16[3,80,1024]{2,1,0:T(8,128)(2,1)}, u32[]{:S(2)}, u32[]{:S(2)}) collective-permute-start(bf16[3,80,1024]{2,1,0:T(8,128)(2,1)S(1)} %get-tuple-element.95), channel_id=1, source_target_pairs={{0,0},{1,1},{2,6},{3,7},{4,2},{5,3},{6,4},{7,5},{8,8},{9,9},{10,14... | collective-permute-start | bytes 1474568 | tf_op jit(solution)/shard_map/ppermute | solution.py:503
  294.6 26.2 %collective-permute-start.52 = (bf16[2,2,256,512]{3,2,1,0:T(8,128)(2,1)S(1)}, bf16[2,2,256,512]{3,2,1,0:T(8,128)(2,1)}, u32[]{:S(2)}, u32[]{:S(2)}) collective-permute-start(bf16[2,2,256,512]{3,2,1,0:T(8,128)(2,1)S(1)} %pad_maximum_fusion.9), channel_id=1, source_target_pairs={{0,8},{4,12},{8,0},{12,4},{16,24},{20,28},{24,16},{28,20},{1,9},{5... | collective-permute-start | bytes 3145736 | tf_op jit(solution)/shard_map/ppermute | solution.py:413
  297.3 26.3 %collective-permute-start.54 = (bf16[2,2,256,512]{3,2,1,0:T(8,128)(2,1)}, bf16[2,2,256,512]{3,2,1,0:T(8,128)(2,1)}, u32[]{:S(2)}, u32[]{:S(2)}) collective-permute-start(bf16[2,2,256,512]{3,2,1,0:T(8,128)(2,1)} %pad_maximum_fusion.10), channel_id=1, source_target_pairs={{0,16},{4,20},{8,24},{12,28},{16,0},{20,4},{24,8},{28,12},{1,17},{... | collective-permute-start | bytes 3145736 | tf_op jit(solution)/shard_map/ppermute | solution.py:413
  305.3 37.8 %collective-permute-start.47 = (bf16[2,2,256,512]{3,2,1,0:T(8,128)(2,1)}, bf16[2,2,256,512]{3,2,1,0:T(8,128)(2,1)}, u32[]{:S(2)}, u32[]{:S(2)}) collective-permute-start(bf16[2,2,256,512]{3,2,1,0:T(8,128)(2,1)} %pad_maximum_fusion.7), channel_id=1, source_target_pairs={{0,8},{4,12},{8,0},{12,4},{16,24},{20,28},{24,16},{28,20},{1,9},{5... | collective-permute-start | bytes 3145736 | tf_op jit(solution)/shard_map/ppermute | solution.py:413
  306.8 38.9 %collective-permute-start.49 = (bf16[2,2,256,512]{3,2,1,0:T(8,128)(2,1)}, bf16[2,2,256,512]{3,2,1,0:T(8,128)(2,1)}, u32[]{:S(2)}, u32[]{:S(2)}) collective-permute-start(bf16[2,2,256,512]{3,2,1,0:T(8,128)(2,1)} %pad_maximum_fusion.8), channel_id=1, source_target_pairs={{0,16},{4,20},{8,24},{12,28},{16,0},{20,4},{24,8},{28,12},{1,17},{... | collective-permute-start | bytes 3145736 | tf_op jit(solution)/shard_map/ppermute | solution.py:413
  349.4 49.0 %collective-permute-start.55 = (bf16[2,256,512]{2,1,0:T(8,128)(2,1)S(1)}, bf16[2,256,512]{2,1,0:T(8,128)(2,1)S(1)}, u32[]{:S(2)}, u32[]{:S(2)}) collective-permute-start(bf16[2,256,512]{2,1,0:T(8,128)(2,1)S(1)} %slice_bitcast_fusion), channel_id=1, source_target_pairs={{0,1},{1,0},{2,3},{3,2},{4,5},{5,4},{6,7},{7,6},{8,9},{9,8},{10,11... | collective-permute-start | bytes 1572872 | tf_op jit(solution)/shard_map/ppermute | solution.py:413
  350.5 61.0 %collective-permute-start.50 = (bf16[2,256,512]{2,1,0:T(8,128)(2,1)}, bf16[2,256,512]{2,1,0:T(8,128)(2,1)}, u32[]{:S(2)}, u32[]{:S(2)}) collective-permute-start(bf16[2,256,512]{2,1,0:T(8,128)(2,1)} %slice_bitcast_fusion.2), channel_id=1, source_target_pairs={{0,1},{1,0},{2,3},{3,2},{4,5},{5,4},{6,7},{7,6},{8,9},{9,8},{10,11... | collective-permute-start | bytes 1572872 | tf_op jit(solution)/shard_map/ppermute | solution.py:413
  394.2 13.4 %collective-permute-start.38 = (bf16[2,4,256,128]{3,2,1,0:T(8,128)(2,1)}, bf16[2,4,256,128]{3,2,1,0:T(8,128)(2,1)}, u32[]{:S(2)}, u32[]{:S(2)}) collective-permute-start(bf16[2,4,256,128]{3,2,1,0:T(8,128)(2,1)} %get-tuple-element.62), channel_id=1, source_target_pairs={{0,16},{4,20},{8,24},{12,28},{16,0},{20,4},{24,8},{28,12},{1,17},{... | collective-permute-start | bytes 1572872 | tf_op jit(solution)/shard_map/ppermute | solution.py:413
  397.6 41.8 %collective-permute-start.35 = (bf16[3,2,80,1024]{3,2,0,1:T(8,128)(2,1)}, bf16[3,2,80,1024]{3,2,0,1:T(8,128)(2,1)}, u32[]{:S(2)}, u32[]{:S(2)}) collective-permute-start(bf16[3,2,80,1024]{3,2,0,1:T(8,128)(2,1)} %copy.80), channel_id=1, source_target_pairs={{0,4},{4,0},{8,12},{12,8},{16,20},{20,16},{24,28},{28,24},{1,5},{5... | collective-permute-start | bytes 2949128 | tf_op jit(solution)/shard_map/ppermute | solution.py:413
  399.4 26.4 %collective-permute-start.56 = (bf16[2,256,512]{2,1,0:T(8,128)(2,1)}, bf16[2,256,512]{2,1,0:T(8,128)(2,1)}, u32[]{:S(2)}, u32[]{:S(2)}) collective-permute-start(bf16[2,256,512]{2,1,0:T(8,128)(2,1)} %fusion.24), channel_id=1, source_target_pairs={{0,2},{1,3},{2,0},{3,1},{4,6},{5,7},{6,4},{7,5},{8,10},{9,11},{10,... | collective-permute-start | bytes 1572872 | tf_op jit(solution)/shard_map/ppermute | solution.py:413
  432.2 59.9 %collective-permute-start.39 = (bf16[4,4,256,128]{3,2,1,0:T(8,128)(2,1)}, bf16[4,4,256,128]{3,2,1,0:T(8,128)(2,1)}, u32[]{:S(2)}, u32[]{:S(2)}) collective-permute-start(bf16[4,4,256,128]{3,2,1,0:T(8,128)(2,1)} %pad_maximum_fusion.5), channel_id=1, source_target_pairs={{0,8},{4,12},{8,0},{12,4},{16,24},{20,28},{24,16},{28,20},{1,9},{5... | collective-permute-start | bytes 3145736 | tf_op jit(solution)/shard_map/ppermute | solution.py:413
  434.8 57.3 %collective-permute-start.41 = (bf16[4,4,256,128]{3,2,1,0:T(8,128)(2,1)}, bf16[4,4,256,128]{3,2,1,0:T(8,128)(2,1)}, u32[]{:S(2)}, u32[]{:S(2)}) collective-permute-start(bf16[4,4,256,128]{3,2,1,0:T(8,128)(2,1)} %pad_maximum_fusion.6), channel_id=1, source_target_pairs={{0,16},{4,20},{8,24},{12,28},{16,0},{20,4},{24,8},{28,12},{1,17},{... | collective-permute-start | bytes 3145736 | tf_op jit(solution)/shard_map/ppermute | solution.py:413
  444.9 61.7 %collective-permute-start.36 = (bf16[3,80,1024]{2,1,0:T(8,128)(2,1)S(1)}, bf16[3,80,1024]{2,1,0:T(8,128)(2,1)S(1)}, u32[]{:S(2)}, u32[]{:S(2)}) collective-permute-start(bf16[3,80,1024]{2,1,0:T(8,128)(2,1)S(1)} %get-tuple-element.86), channel_id=1, source_target_pairs={{0,1},{1,0},{2,7},{3,6},{4,3},{5,2},{6,5},{7,4},{8,9},{9,8},{10,15... | collective-permute-start | bytes 1474568 | tf_op jit(solution)/shard_map/ppermute | solution.py:503
  445.0 61.6 %collective-permute-start.37 = (bf16[3,80,1024]{2,1,0:T(8,128)(2,1)S(1)}, bf16[3,80,1024]{2,1,0:T(8,128)(2,1)S(1)}, u32[]{:S(2)}, u32[]{:S(2)}) collective-permute-start(bf16[3,80,1024]{2,1,0:T(8,128)(2,1)S(1)} %get-tuple-element.87), channel_id=1, source_target_pairs={{0,0},{1,1},{2,6},{3,7},{4,2},{5,3},{6,4},{7,5},{8,8},{9,9},{10,14... | collective-permute-start | bytes 1474568 | tf_op jit(solution)/shard_map/ppermute | solution.py:503
  496.3 13.8 %collective-permute-start.42 = (bf16[4,256,128]{2,1,0:T(8,128)(2,1)S(1)}, bf16[4,256,128]{2,1,0:T(8,128)(2,1)S(1)}, u32[]{:S(2)}, u32[]{:S(2)}) collective-permute-start(bf16[4,256,128]{2,1,0:T(8,128)(2,1)S(1)} %get-tuple-element.76), channel_id=1, source_target_pairs={{0,1},{1,0},{2,3},{3,2},{4,5},{5,4},{6,7},{7,6},{8,9},{9,8},{10,11... | collective-permute-start | bytes 786440 | tf_op jit(solution)/shard_map/ppermute | solution.py:413
  (58 other events, 625.1 us)

commit v3 on v2

--- a/solution.py
+++ b/solution.py
@@ -55,23 +55,34 @@
         pl.loop(0, count)(step)
 
 
+def valid_slots(meta_ref, image, slots, axis):
+    shape = (slots, 1) if axis == 0 else (1, slots)
+    row = lax.broadcasted_iota(jnp.int32, shape, axis)
+    n = slots // 4
+    k = (row >= n).astype(jnp.int32) + (row >= 2 * n) + (row >= 3 * n)
+    slot = (k ^ meta_ref[3]) * n + (row - k * n)
+    return slot < BUF + meta_ref[image]
+
+
 def copy_att(parts, refs, w_scr, sem, kinds, n_i):
+    n_j = parts[-1][0] + refs[-1].shape[0]
+    wq = w_scr.shape[0] // n_j
     for (j0, i0), ref in zip(parts, refs):
-        nj, ni, _, wq, he = ref.shape
+        nj, ni, _, he = ref.shape
 
         def one(jj, ref=ref, j0=j0, i0=i0, ni=ni, wq=wq, he=he):
             rows = pl.ds(pl.multiple_of((j0 + jj) * wq, wq), wq) if not isinstance(jj, int) else pl.ds((j0 + jj) * wq, wq)
             for ii in range(ni):
                 for t in range(kinds):
                     pltpu.make_async_copy(
-                        ref.at[jj, ii, t], w_scr.at[rows, pl.ds((t * n_i + i0 + ii) * he, he)], sem
+                        ref.at[jj, ii, pl.ds(t * wq, wq)], w_scr.at[rows, pl.ds((t * n_i + i0 + ii) * he, he)], sem
                     ).start()
 
         for_each(nj, one)
     pltpu.make_async_copy(w_scr, w_scr, sem).wait()
 
 
-def att_fwd_kernel(parts, n_i, x_ref, g_ref, c_ref, bias_ref, valid_ref, *rest):
+def att_fwd_kernel(parts, n_i, x_ref, g_ref, c_ref, bias_ref, meta_ref, *rest):
     w_refs = rest[: len(parts)]
     n1_ref, qkv_ref, mix_ref, part_ref, w_scr, m_scr, sem = rest[len(parts) :]
     he = 2 * HEAD
@@ -88,7 +99,8 @@
         res = (mm(n1, w_scr[:, cols]) + bias_ref[:, cols]).astype(BF)
         for i in range(n_i):
             qkv_ref[t * n_i + i] = res[:, i * he : (i + 1) * he]
-    bias = jnp.where(valid_ref[0] > 0.5, 0.0, masked_score)
+    image = pl.program_id(0)
+    bias = jnp.where(valid_slots(meta_ref, image, x_ref.shape[1], 1), 0.0, masked_score)
     lane = lax.broadcasted_iota(jnp.int32, (1, he), 1)
     low_half = lane < HEAD
     for i in range(n_i):
@@ -107,7 +119,7 @@
     part_ref[...] = mm(m_scr[...], w_scr[:, 3 * n_i * he :], NT).astype(BF)
 
 
-def att_forward(x, gain, shift, bias, valid, parts, arrays, cost=True):
+def att_forward(x, gain, shift, bias, meta, parts, arrays):
     images, slots, width = x.shape
     n_i = 4
     he = 2 * HEAD
@@ -122,7 +134,7 @@
             whole(1, width),
             whole(1, width),
             whole(1, 3 * n_i * he),
-            pl.BlockSpec((1, 1, slots), lambda a: (a, 0, 0)),
+            pl.BlockSpec(memory_space=pltpu.SMEM),
         ]
         + [ANY_SPEC] * len(arrays),
         out_specs=[
@@ -145,17 +157,24 @@
         compiler_params=pltpu.CompilerParams(vmem_limit_bytes=32 * MIB),
         cost_estimate=pl.CostEstimate(flops=8_000_000_000, bytes_accessed=20_000_000, transcendentals=2_500_000),
         name="att_forward",
-    )(x, gain, shift, bias, valid, *arrays)
-
-
-def ffn_kernel(
-    parts, n_i, last, x_ref, pa_ref, pb_ref, b_ref, g_ref, c_ref, go_ref, upb_ref, *rest
-):
-    w_refs = rest[: len(parts)]
-    hidden_ref, branch_ref, gn2_ref, grads_ref, upg_ref = rest[len(parts) : len(parts) + 5]
-    n2, n2t, got, acc_b, acc_g, wbuf, gbuf, act_s, pre_s, wsem, gsem = rest[len(parts) + 5 :]
-    rows, width = x_ref.shape
-    fh = last
+    )(x, gain, shift, bias, meta, *arrays)
+
+
+def ffn_kernel(parts, n_i, first, last, *refs):
+    if first:
+        x_ref, pa_ref, pb_ref, b_ref, g_ref, c_ref = refs[:6]
+        refs = refs[6:]
+    else:
+        n2, n2t, got, acc_b, acc_g = refs[:5]
+        refs = refs[5:]
+    go_ref, upb_ref = refs[:2]
+    w_refs, refs = refs[2 : 2 + len(parts)], refs[2 + len(parts) :]
+    if first:
+        hidden_ref, n2, n2t, got = refs[:4]
+        refs = refs[4:]
+    sum_b, sum_g, grads_ref, upg_ref, wbuf, gbuf, act_s, pre_s, wsem, gsem = refs[:10]
+    run_b, run_g = refs[10:] if last else (sum_b, sum_g)
+    rows, width = go_ref.shape
     n_j, _, _, wq, _ = grads_ref.shape
 
     def fetch(i, slot):
@@ -192,22 +211,23 @@
         pltpu.make_async_copy(gbuf.at[slot], gbuf.at[slot], gsem.at[slot]).wait()
 
     fetch(0, 0)
-    block = 192
-
-    @pl.loop(0, rows // block)
-    def _(r):
-        rw = pl.ds(pl.multiple_of(r * block, block), block)
-        h = (
-            x_ref[rw, :].astype(F32)
-            + (pa_ref[rw, :].astype(F32) + pb_ref[rw, :].astype(F32))
-            + b_ref[...]
-        )
-        hidden_ref[rw, :] = h
-        hat, _ = normalise(h)
-        n2[rw, :] = (hat * g_ref[...] + c_ref[...]).astype(BF)
-
-    n2t[...] = n2[...].T
-    got[...] = go_ref[...].T
+    if first:
+        block = 192
+
+        @pl.loop(0, rows // block)
+        def _(r):
+            rw = pl.ds(pl.multiple_of(r * block, block), block)
+            h = (
+                x_ref[rw, :].astype(F32)
+                + (pa_ref[rw, :].astype(F32) + pb_ref[rw, :].astype(F32))
+                + b_ref[...]
+            )
+            hidden_ref[rw, :] = h
+            hat, _ = normalise(h)
+            n2[rw, :] = (hat * g_ref[...] + c_ref[...]).astype(BF)
+
+        n2t[...] = n2[...].T
+        got[...] = go_ref[...].T
     rb = rows // 3
     for i in range(n_i):
         slot = i % 2
@@ -227,15 +247,18 @@
             pre_s[rw, :] = pre
             down = mm(act, w, NT)
             back = mm(pre, u, NT)
-            if i == 0:
-                acc_b[rw, :] = down
-                acc_g[rw, :] = back
-            elif i < n_i - 1:
-                acc_b[rw, :] += down
-                acc_g[rw, :] += back
+            if i > 0:
+                down += run_b[rw, :]
+                back += run_g[rw, :]
+            elif not first:
+                down += acc_b[rw, :]
+                back += acc_g[rw, :]
+            if i < n_i - 1:
+                run_b[rw, :] = down
+                run_g[rw, :] = back
             else:
-                branch_ref[rw, :] = (acc_b[rw, :] + down).astype(BF)
-                gn2_ref[rw, :] = (acc_g[rw, :] + back).astype(BF)
+                sum_b[rw, :] = down.astype(sum_b.dtype)
+                sum_g[rw, :] = back.astype(sum_g.dtype)
 
         upg_ref[i : i + 1, :] = jnp.sum(pre_s[...].astype(F32), axis=0, keepdims=True)
         if i >= 2:
@@ -243,53 +266,62 @@
         gbuf[slot, 0] = mm(n2t[...], pre_s[...]).astype(BF)
         gbuf[slot, 1] = mm(got[...], act_s[...]).astype(BF)
         put(i, slot)
-    stored((n_i - 2) % 2)
-    stored((n_i - 1) % 2)
-
-
-def ffn(x, pa, pb, b0, gain, shift, go, upb, n_j, parts, arrays):
-    rows, width = x.shape
-    n_i, fh = upb.shape
+    for i in range(max(n_i - 2, 0), n_i):
+        stored(i % 2)
+
+
+def ffn_call(ins, n_j, n_i, fh, parts, arrays, first, last):
+    go = ins[-2]
+    rows, width = go.shape
     wq = width // n_j
-    return pl.pallas_call(
-        functools.partial(ffn_kernel, parts, n_i, fh),
-        in_specs=[VMEM_SPEC] * 8 + [ANY_SPEC] * len(arrays),
-        out_specs=[VMEM_SPEC] * 3 + [ANY_SPEC, VMEM_SPEC],
-        out_shape=[
+    made = (
+        [
             jax.ShapeDtypeStruct((rows, width), F32),
             jax.ShapeDtypeStruct((rows, width), BF),
-            jax.ShapeDtypeStruct((rows, width), BF),
+            jax.ShapeDtypeStruct((width, rows), BF),
+            jax.ShapeDtypeStruct((width, rows), BF),
+        ]
+        if first
+        else []
+    )
+    sums = BF if last else F32
+    return pl.pallas_call(
+        functools.partial(ffn_kernel, parts, n_i, first, last),
+        in_specs=[VMEM_SPEC] * len(ins) + [ANY_SPEC] * len(arrays),
+        out_specs=[VMEM_SPEC] * (len(made) + 2) + [ANY_SPEC, VMEM_SPEC],
+        out_shape=made
+        + [
+            jax.ShapeDtypeStruct((rows, width), sums),
+            jax.ShapeDtypeStruct((rows, width), sums),
             jax.ShapeDtypeStruct((n_j, n_i, 2, wq, fh), BF),
             jax.ShapeDtypeStruct((n_i, fh), F32),
         ],
         scratch_shapes=[
-            pltpu.VMEM((rows, width), BF),
-            pltpu.VMEM((width, rows), BF),
-            pltpu.VMEM((width, rows), BF),
-            pltpu.VMEM((rows, width), F32),
-            pltpu.VMEM((rows, width), F32),
             pltpu.VMEM((2, 2, width, fh), BF),
             pltpu.VMEM((2, 2, width, fh), BF),
             pltpu.VMEM((rows, fh), BF),
             pltpu.VMEM((rows, fh), BF),
             pltpu.SemaphoreType.DMA((2,)),
             pltpu.SemaphoreType.DMA((2,)),
-        ],
-        compiler_params=pltpu.CompilerParams(vmem_limit_bytes=56 * MIB),
-        cost_estimate=pl.CostEstimate(flops=36_000_000_000, bytes_accessed=30_000_000, transcendentals=4_000_000),
-        name="ffn",
-    )(x, pa, pb, b0, gain, shift, go, upb, *arrays)
+        ]
+        + [pltpu.VMEM((rows, width), F32)] * (2 if last else 0),
+        compiler_params=pltpu.CompilerParams(vmem_limit_bytes=58 * MIB),
+        cost_estimate=pl.CostEstimate(
+            flops=9_000_000_000 * n_i, bytes_accessed=30_000_000, transcendentals=1_000_000 * n_i
+        ),
+        name="ffn_first" if first else "ffn_last",
+    )(*ins, *arrays)
 
 
 def att_bwd_kernel(
-    parts, n_i, hid_ref, ga_ref, gb_ref, g_ref, go_ref, n1_ref, qkv_ref, mix_ref, valid_ref, *rest
+    parts, n_i, meta_ref, x_ref, hid_ref, ga_ref, gb_ref, g_ref, go_ref, n1_ref, qkv_ref, mix_ref, *rest
 ):
     w_refs = rest[: len(parts)]
     gh_ref, gn1_ref, grads_ref, bias_ref, sums_ref = rest[len(parts) : len(parts) + 5]
     ghb, gmix, gq, w_scr, gbuf, sem, gsem = rest[len(parts) + 5 :]
     rows, width = hid_ref.shape
     he = 2 * HEAD
-    images = valid_ref.shape[0]
+    images = 3
     slots = rows // images
     n_j, _, _, wq, _ = grads_ref.shape
     copy_att(parts, w_refs, w_scr, sem, 4, n_i)
@@ -334,7 +366,7 @@
     @pl.loop(0, images)
     def _(a):
         rw = pl.ds(pl.multiple_of(a * slots, slots), slots)
-        bias = jnp.where(valid_ref[a] > 0.5, 0.0, masked_score)
+        bias = jnp.where(valid_slots(meta_ref, a, slots, 0), 0.0, masked_score)
         for i in range(n_i):
             q2, k2, v2 = qkv_ref[i, rw, :], qkv_ref[n_i + i, rw, :], qkv_ref[2 * n_i + i, rw, :]
             g2 = gmix[i, rw, :]
@@ -372,19 +404,23 @@
     @pl.loop(0, 3)
     def _(r):
         rw = pl.ds(pl.multiple_of(r * rb, rb), rb)
-        gn1_ref[rw, :] = mm(gq[rw, :], w_scr[:, : 3 * n_i * he], NT).astype(BF)
+        grad = mm(gq[rw, :], w_scr[:, : 3 * n_i * he], NT)
+        gn1_ref[rw, :] = grad.astype(BF)
+        hat, _ = normalise(x_ref[rw, :].astype(F32))
+        sums_ref[4:5, :] += jnp.sum(grad * hat, axis=0, keepdims=True)
+        sums_ref[5:6, :] += jnp.sum(grad, axis=0, keepdims=True)
 
     for kind in range(4):
         pltpu.make_async_copy(gbuf.at[kind], gbuf.at[kind], gsem.at[kind]).wait()
 
 
-def att_backward(hidden, ga, gb, gain, go, n1, qkv, mix, valid_t, n_j, parts, arrays):
+def att_backward(meta, x, hidden, ga, gb, gain, go, n1, qkv, mix, n_j, parts, arrays):
     rows, width = hidden.shape
     n_i, he = 4, 2 * HEAD
     wq = width // n_j
     return pl.pallas_call(
         functools.partial(att_bwd_kernel, parts, n_i),
-        in_specs=[VMEM_SPEC] * 9 + [ANY_SPEC] * len(arrays),
+        in_specs=[pl.BlockSpec(memory_space=pltpu.SMEM)] + [VMEM_SPEC] * 9 + [ANY_SPEC] * len(arrays),
         out_specs=[VMEM_SPEC] * 2 + [ANY_SPEC] + [VMEM_SPEC] * 2,
         out_shape=[
             jax.ShapeDtypeStruct((rows, width), F32),
@@ -405,28 +441,29 @@
         compiler_params=pltpu.CompilerParams(vmem_limit_bytes=56 * MIB),
         cost_estimate=pl.CostEstimate(flops=20_000_000_000, bytes_accessed=40_000_000, transcendentals=2_500_000),
         name="att_backward",
-    )(hidden, ga, gb, gain, go, n1, qkv, mix, valid_t, *arrays)
-
-
-def swap(x, axis, bits):
+    )(meta, x, hidden, ga, gb, gain, go, n1, qkv, mix, *arrays)
+
+
+def swap(x, axis, bits, what):
     n = lax.axis_size(axis)
-    return lax.ppermute(x, axis, [(i, i ^ bits) for i in range(n)])
-
-
-def gather_q(own):
+    with jax.named_scope(what):
+        return lax.ppermute(x, axis, [(i, i ^ bits) for i in range(n)])
+
+
+def gather_q(own, what):
     n_q = lax.axis_size("dp") // 2
     if n_q != 4:
         blocks = own[None]
         bit = 1
         while bit < n_q:
-            blocks = jnp.concatenate([blocks, swap(blocks, "dp", 2 * bit)])
+            blocks = jnp.concatenate([blocks, swap(blocks, "dp", 2 * bit, what)])
             bit *= 2
         return [(0, 0)], [blocks]
     half = own.shape[0] // 2
-    one = swap(own, "dp", 2)
-    two = swap(own, "dp", 4)
-    three_a = swap(one[:half], "dp", 4)
-    three_b = swap(two[half:], "dp", 2)
+    one = swap(own, "dp", 2, what + "_x1")
+    two = swap(own, "dp", 4, what + "_y1")
+    three_a = swap(one[:half], "dp", 4, what + "_y2")
+    three_b = swap(two[half:], "dp", 2, what + "_x2")
     places = [(0, 0), (1, 0), (2, 0), (3, 0), (3, half)]
     return places, [v[None] for v in (own, one, two, three_a, three_b)]
 
@@ -438,32 +475,32 @@
     return total.astype(parts[0].dtype)
 
 
-def scatter_q(parts):
+def scatter_q(parts, what):
     n_q = lax.axis_size("dp") // 2
     if n_q != 4:
         bit = n_q // 2
         while bit >= 1:
-            parts = add(parts[:bit], swap(parts[bit:], "dp", 2 * bit))
+            parts = add(parts[:bit], swap(parts[bit:], "dp", 2 * bit, what))
             bit //= 2
         return parts[0]
     half = parts.shape[1] // 2
-    into_one = swap(parts[3, :half], "dp", 4)
-    into_two = swap(parts[3, half:], "dp", 2)
+    into_one = swap(parts[3, :half], "dp", 4, what + "_y1")
+    into_two = swap(parts[3, half:], "dp", 2, what + "_x1")
     one = jnp.concatenate([add(parts[1, :half], into_one), parts[1, half:]])
     two = jnp.concatenate([parts[2, :half], add(parts[2, half:], into_two)])
-    return add(parts[0], swap(one, "dp", 2), swap(two, "dp", 4))
-
-
-def gather_z(own):
-    two = swap(own, "mp", 2)
-    one = swap(own, "mp", 1)
-    three = swap(two, "mp", 1)
+    return add(parts[0], swap(one, "dp", 2, what + "_x2"), swap(two, "dp", 4, what + "_y2"))
+
+
+def gather_z(own, what):
+    two = swap(own, "mp", 2, what + "_z2")
+    one = swap(own, "mp", 1, what + "_z1")
+    three = swap(two, "mp", 1, what + "_z3")
     return jnp.stack([own, one, two, three])
 
 
-def scatter_z(parts):
-    into_two = swap(parts[3], "mp", 1)
-    return add(parts[0], swap(parts[1], "mp", 1), swap(add(parts[2], into_two), "mp", 2))
+def scatter_z(parts, what):
+    into_two = swap(parts[3], "mp", 1, what + "_z3")
+    return add(parts[0], swap(parts[1], "mp", 1, what + "_z1"), swap(add(parts[2], into_two), "mp", 2, what + "_z2"))
 
 
 def ordered_pair(own, other, core, axis=0):
@@ -484,23 +521,25 @@
     return pairs
 
 
-def to_images(x, z):
+def to_images(x, z, what):
     n_dp, n_mp = lax.axis_size("dp"), lax.axis_size("mp")
     slots, images, width = x.shape
     groups = jnp.transpose(x, (1, 0, 2)).reshape(2, images // 2, slots, width)
     got = []
     for odd in (0, 1):
         send = lax.dynamic_index_in_dim(groups, (z ^ odd) & 1, 0, False)
-        got.append(lax.ppermute(send, ("dp", "mp"), image_routes(n_dp, n_mp, odd)))
+        with jax.named_scope(what + "_route" + str(odd)):
+            got.append(lax.ppermute(send, ("dp", "mp"), image_routes(n_dp, n_mp, odd)))
     return jnp.stack(got, 1)
 
 
-def from_images(y, z):
+def from_images(y, z, what):
     n_dp, n_mp = lax.axis_size("dp"), lax.axis_size("mp")
     back = []
     for odd in (0, 1):
         routes = [(b, a) for a, b in image_routes(n_dp, n_mp, odd)]
-        back.append(lax.ppermute(y[:, odd], ("dp", "mp"), routes))
+        with jax.named_scope(what + "_route" + str(odd)):
+            back.append(lax.ppermute(y[:, odd], ("dp", "mp"), routes))
     flip = (z & 1) == 1
     groups = jnp.concatenate([jnp.where(flip, back[1], back[0]), jnp.where(flip, back[0], back[1])])
     return jnp.transpose(groups, (1, 0, 2))
@@ -540,70 +579,78 @@
 
     att = jnp.concatenate([qkv_weight, jnp.transpose(proj_weight)[None]])
     ffn_w = jnp.stack([up_weight, jnp.transpose(down_weight)])
-
-    def paired(v):
-        got = swap(half_of(v, 1 - core, 2), "dp", 1)
-        both = ordered_pair(half_of(v, core, 2), got, core, 1)
-        return both.reshape(v.shape[0], wq, -1)
-
-    att_own, ffn_own = paired(att), paired(ffn_w)
-    he, fh = att_own.shape[-1], ffn_own.shape[-1]
-    bias_own = jnp.concatenate(
+    he, fh = att.shape[-1] // 2, ffn_w.shape[-1] // 2
+
+    count_rows = jnp.pad(counts.astype(BF)[None], ((0, 15), (0, he - images)))
+    sent = jnp.concatenate([half_of(att, 1 - core, 2).reshape(-1, he), count_rows])
+    got = swap(sent, "dp", 1, "att_w_core")
+    other_counts = got[-16, :images].astype(jnp.int32)
+    got = got[:-16].reshape(4, wq // 2, he)
+    att_own = ordered_pair(half_of(att, core, 2), got, core, 1).reshape(-1, he)
+    got = swap(half_of(ffn_w, 1 - core, 2), "dp", 1, "ffn_w_core")
+    ffn_own = ordered_pair(half_of(ffn_w, core, 2), got, core, 1).reshape(2, wq, fh)
+    left = jnp.concatenate(
         [half_of(qkv_bias, core, 1), half_of(up_bias, core, 0).reshape(-1, he)]
     )
-    bias_all = gather_z(bias_own)
-    att_places, att_parts = gather_q(gather_z(att_own))
-
-    def whole_rows(v):
-        got = to_images(rel(v), z)
-        return ordered_pair(got, swap(got, "dp", 1), core, 1).reshape(rows, width)
-
-    other_counts = swap(counts, "dp", 1)
+    n_bias = left.shape[0]
+    terms = []
+    for _ in range(3):
+        term = lax.reduce_precision(left, 8, 7)
+        terms.append(term.astype(BF))
+        left = left - term
+    bias_pad = -(-3 * n_bias // 16) * 16
+    bias_terms = jnp.pad(jnp.concatenate(terms), ((0, bias_pad - 3 * n_bias), (0, 0)))
+
     counts_here = jnp.where((z >> 1) == core, counts, other_counts)
     counts_here = lax.dynamic_slice_in_dim(counts_here, (z & 1) * own_images, own_images, 0)
+    meta = jnp.concatenate([counts_here, z[None]])
     slot_ids = jnp.arange(slots, dtype=jnp.int32)
-    slot_of = (z ^ jnp.arange(n_mp, dtype=jnp.int32))[:, None] * slots + slot_ids
-    valid = (slot_of.reshape(1, -1) < BUF + counts_here[:, None]).astype(F32)
     keep_mine = ((z * slots + slot_ids)[:, None] < BUF + counts[None, :])[:, :, None]
 
-    x = whole_rows(tokens)
+    def whole_rows(got, what):
+        return ordered_pair(got, swap(got, "dp", 1, what), core, 1).reshape(rows, width)
+
+    n_i = n_mp
     gains, shifts, out_b = rel(norm_gains), rel(norm_shifts), rel(out_biases)
-    n_i = n_mp
+    token_rows = to_images(rel(tokens), z, "tokens")
+    att_z = gather_z(jnp.concatenate([att_own, bias_terms]), "att_w")
+    bias_all = att_z[:, 4 * wq : 4 * wq + 3 * n_bias].astype(F32).reshape(n_i, 3, n_bias, he)
+    bias_all = bias_all[:, 0] + (bias_all[:, 1] + bias_all[:, 2])
     bias_rows = jnp.concatenate(
         [bias_all[:, 0].reshape(1, -1), jnp.zeros((1, n_i * he), F32), bias_all[:, 1].reshape(1, -1)], 1
     )
+    x = whole_rows(token_rows, "tokens_core")
+    att_places, att_parts = gather_q(att_z, "att_w")
     n1, qkv, mix, part = att_forward(
         x.reshape(own_images, all_slots, width),
         gains[0:1],
         shifts[0:1],
         bias_rows,
-        valid[:, None],
+        meta,
         att_places,
         att_parts,
     )
 
-    ffn_z = gather_z(ffn_own)
-    ffn_places, ffn_parts = [], []
-    for i0 in (0, 2):
-        places, arrays = gather_q(ffn_z[i0 : i0 + 2])
-        ffn_places += [(j, i + i0) for j, i in places]
-        ffn_parts += arrays
-    go = whole_rows(jnp.where(keep_mine, cotangent, jnp.zeros_like(cotangent)))
-    hidden, branch, gn2, ffn_g, upg = ffn(
+    ffn_z = gather_z(ffn_own, "ffn_w")
+    cot_rows = to_images(
+        rel(jnp.where(keep_mine, cotangent, jnp.zeros_like(cotangent))), z, "cotangent"
+    )
+    go = whole_rows(cot_rows, "cotangent_core")
+    up_rows = bias_all[:, 2:].reshape(n_i, fh)
+    places0, parts0 = gather_q(ffn_z[:2], "ffn_w0")
+    hidden, n2, n2t, got, sum_b, sum_g, ffn_g0, upg0 = ffn_call(
+        [x, part, swap(part, "dp", 1, "attended"), out_b[0:1], gains[1:2], shifts[1:2], go, up_rows[:2]],
+        n_q, 2, fh, places0, parts0, True, False,
+    )
+    places1, parts1 = gather_q(ffn_z[2:], "ffn_w2")
+    branch, gn2, ffn_g1, upg1 = ffn_call(
+        [n2, n2t, got, sum_b, sum_g, go, up_rows[2:]], n_q, 2, fh, places1, parts1, False, True
+    )
+    upg = jnp.concatenate([upg0, upg1])
+    gn2_other = swap(gn2, "dp", 1, "grad_norm_two")
+    gh, gn1, att_g, bias_sum, sums = att_backward(
+        meta,
         x,
-        part,
-        swap(part, "dp", 1),
-        out_b[0:1],
-        gains[1:2],
-        shifts[1:2],
-        go,
-        bias_all[:, 2:].reshape(n_i, fh),
-        n_q,
-        ffn_places,
-        ffn_parts,
-    )
-    gn2_other = swap(gn2, "dp", 1)
-    gh, gn1, att_g, bias_sum, sums = att_backward(
         hidden,
         gn2,
         gn2_other,
@@ -612,36 +659,34 @@
         n1,
         qkv,
         mix,
-        valid[:, :, None],
         n_q,
         att_places,
         att_parts,
     )
     ffn_grad = scatter_z(
-        jnp.concatenate([scatter_q(ffn_g[:, :2]), scatter_q(ffn_g[:, 2:])])
+        jnp.concatenate([scatter_q(ffn_g0, "ffn_g0"), scatter_q(ffn_g1, "ffn_g2")]), "ffn_g"
     )
 
     row_half = lambda v, which: half_of(v.reshape(own_images, n_mp, slots, width), which, 1)
-    theirs = swap(row_half(branch, 1 - core), "dp", 1).astype(F32)
+    theirs = swap(row_half(branch, 1 - core), "dp", 1, "branch").astype(F32)
     out_half = row_half(hidden, core) + row_half(branch, core).astype(F32) + theirs + out_b[1]
-    block_out = from_images(rel(out_half.astype(BF)), z)
+    block_out = from_images(rel(out_half.astype(BF)), z, "block_out")
     block_out = jnp.where(keep_mine, block_out, jnp.zeros_like(block_out))
 
-    att_grad = scatter_z(scatter_q(att_g))
-    gn1 = row_half(gn1, core).astype(F32) + swap(row_half(gn1, 1 - core), "dp", 1).astype(F32)
+    att_grad = scatter_z(scatter_q(att_g, "att_g"), "att_g")
+    gn1 = row_half(gn1, core).astype(F32) + swap(row_half(gn1, 1 - core), "dp", 1, "grad_norm_one").astype(F32)
     hat1, inv1 = normalise(row_half(x, core).astype(F32))
     input_half = row_half(gh, core) + norm_back(hat1, inv1, gains[0], gn1)
-    gain_one, shift_one = jnp.sum(gn1 * hat1, (0, 1, 2)), jnp.sum(gn1, (0, 1, 2))
-    input_grad = from_images(rel(input_half.astype(BF)), z)
-
-    def own_shard(grad):
+    input_grad = from_images(rel(input_half.astype(BF)), z, "input_grad")
+
+    def own_shard(grad, what):
         kinds, _, last = grad.shape
         pair = grad.reshape(kinds, 2, wq // 2, last)
         keep = lax.dynamic_index_in_dim(pair, core, 1, False)
-        got = swap(lax.dynamic_index_in_dim(pair, 1 - core, 1, False), "dp", 1)
+        got = swap(lax.dynamic_index_in_dim(pair, 1 - core, 1, False), "dp", 1, what)
         return ordered_pair(keep, got, core, 2).reshape(kinds, wq // 2, 2 * last).astype(F32)
 
-    att_shard, ffn_shard = own_shard(att_grad), own_shard(ffn_grad)
+    att_shard, ffn_shard = own_shard(att_grad, "att_g_core"), own_shard(ffn_grad, "ffn_g_core")
     qkv_owned, proj_owned = att_shard[:3], jnp.transpose(att_shard[3])
     up_owned, down_owned = ffn_shard[0], jnp.transpose(ffn_shard[1])
 
@@ -651,23 +696,33 @@
     for i in range(n_i):
         wide_up = lax.dynamic_update_slice(wide_up, upg[i][None, None], (z ^ i, core, 0))
         wide_bias = lax.dynamic_update_slice(wide_bias, biases[:, i][:, None, None], (0, z ^ i, core, 0))
-    small = rel(
-        jnp.concatenate(
-            [gain_one[None], sums[0:1] * 0.5, shift_one[None], sums[1:2] * 0.5, sums[2:4] * 0.5]
-        )
-    )
-    small, wide_bias, wide_up = lax.psum((small, wide_bias, wide_up), ("dp", "mp"))
+    small = rel(sums)
+    vector = jnp.concatenate([small.reshape(-1), wide_bias.reshape(-1), wide_up.reshape(-1)])
+    vector = vector.reshape(-1, 128)
+    for axis, size in (("mp", n_mp), ("dp", n_dp)):
+        bit = size // 2
+        while bit >= 1:
+            vector = vector + swap(vector, axis, bit, "sums_" + axis + str(bit))
+            bit //= 2
+    vector = vector.reshape(-1)
+    n_small, n_wide = small.size, wide_bias.size
+    small = vector[:n_small].reshape(small.shape)
+    wide_bias = vector[n_small : n_small + n_wide].reshape(wide_bias.shape)
+    wide_up = vector[n_small + n_wide :].reshape(wide_up.shape)
+    small = jnp.concatenate([small[:4] * 0.5, small[4:]])
+    gains_grad = jnp.stack([small[4], small[0]])
+    shifts_grad = jnp.stack([small[5], small[1]])
     bias_grad = lax.dynamic_index_in_dim(wide_bias, z, 1, False).reshape(2, -1)
     upbias_grad = lax.dynamic_index_in_dim(wide_up, z, 0, False).reshape(-1)
     return (
         block_out,
         input_grad,
-        small[0:2],
-        small[2:4],
+        gains_grad,
+        shifts_grad,
         qkv_owned,
         bias_grad,
         proj_owned,
-        small[4:6],
+        small[2:4],
         up_owned,
         upbias_grad,
         down_owned,

time: 525 us -> 447 us (0.85)
  waiting for transfers between devices: 222 us -> 170 us
  blocking collectives: 46.2 us -> 0 us
  Pallas kernels: 98.5 us -> 112 us
  starting transfers between devices: 54.6 us -> 67.4 us
    ppermute x50 -> x51, waiting for transfers between devices: 217 us -> 149 us  [swap(): return lax.ppermute(x, axis, [(i, i ^ bits) for i in range(n)])]
    psum x1 -> x0, blocking collectives: 46.2 us -> none  [local(): lax.psum((small, wide_bias, wide_up), ('dp', 'mp'))]
    ppermute x4, waiting for transfers between devices: 0.01 us -> 13.9 us  [to_images(): got.append(lax.ppermute(send, ('dp', 'mp'), image_routes(n_dp, n_mp, odd)))]
    pallas_call x2 -> x3, Pallas kernels: 79.2 us -> 92.4 us  [the longest x2 53 us: ffn_call(): pl.pallas_call(functools.partial(ffn_kernel, parts, n_i, first, last), in...]
    ppermute x50 -> x51, starting transfers between devices: 45 us -> 58 us  [swap(): return lax.ppermute(x, axis, [(i, i ^ bits) for i in range(n)])]
    unnamed x104 -> x99, local copies, waits for them, and re-layouts: 9.16 us -> 13.5 us
    convert_element_type x8 -> x10, other arithmetic: 13.9 us -> 15.6 us  [add(): return total.astype(parts[0].dtype)]
  transfers between devices with their start and end apart: 58 -> 59, of which waited for: 26 -> 27; matrix products, arithmetic and copies ran while one was open for 17% -> 17% of each run, Pallas kernels for 11% -> 25%
where the time goes in v3:
time: 447 us; the launch traced here: 442 us
  waiting for transfers between devices  170 us (38%)
  Pallas kernels  112 us (25%)
  starting transfers between devices  67.4 us (15%)
  other arithmetic  49.7 us (11%)
  local copies, waits for them, and re-layouts  40.4 us (9%)
    ppermute x51, waiting for transfers between devices, swap(): return lax.ppermute(x, axis, [(i, i ^ bits) for i in range(n)])  149 us
    ppermute x51, starting transfers between devices, swap(): return lax.ppermute(x, axis, [(i, i ^ bits) for i in range(n)])  58 us
    pallas_call x2, Pallas kernels, ffn_call(): pl.pallas_call(functools.partial(ffn_kernel, parts, n_i, first, last), in...  53 us
    pallas_call x1, Pallas kernels, att_backward(): pl.pallas_call(functools.partial(att_bwd_kernel, parts, n_i), in_specs=[p...  39.4 us
    pallas_call x1, Pallas kernels, att_forward(): pl.pallas_call(functools.partial(att_fwd_kernel, parts, n_i), grid=(image...  19.8 us
    convert_element_type x10, other arithmetic, add(): return total.astype(parts[0].dtype)  15.6 us
    ppermute x4, waiting for transfers between devices, to_images(): got.append(lax.ppermute(send, ('dp', 'mp'), image_routes(n_dp, n_mp, odd)))  13.9 us
    unnamed x99, local copies, waits for them, and re-layouts  13.5 us
  transfers between devices with their start and end apart: 59, of which 27 were waited for; matrix products, arithmetic and copies ran while one was open for 17% of the time, Pallas kernels for 25%

profile of v3, /device:TPU:0, one launch (start us, length us, event | category | flops | bytes accessed | tf_op | source)
XLA Modules:
  0.0 441.7 jit_solution(8210577504213616207)
XLA Ops:
  7.8 4.1 collective-permute-start.5
  15.6 8.9 %collective-permute-done.5 = bf16[1056,128]{1,0:T(8,128)(2,1)S(1)} collective-permute-done((bf16[1056,128]{1,0:T(8,128)(2,1)S(1)}, bf16[1056,128]{1,0:T(8,128)(2,1)S(1)}, u32[]{:S(2)}, u32[]{:S(2)}) %collective-permute-start.5) | collective-permute-done | bytes 270368 | tf_op jit(solution)/shard_map/att_w_z2/ppermute | solution.py:450
  26.9 5.4 %collective-permute-start.12 = (bf16[3,80,1024]{2,1,0:T(8,128)(2,1)}, bf16[3,80,1024]{2,1,0:T(8,128)(2,1)}, u32[]{:S(2)}, u32[]{:S(2)}) collective-permute-start(bf16[3,80,1024]{2,1,0:T(8,128)(2,1)} %get-tuple-element.107), channel_id=1, source_target_pairs={{0,0},{1,1},{6,2},{7,3},{2,4},{3,5},{4,6},{5,7},{8,8},{9,9},{14,10... | collective-permute-start | bytes 1474568 | tf_op jit(solution)/shard_map/cotangent_route0/ppermute | solution.py:532
  33.2 7.4 %collective-permute-done.6 = bf16[1056,128]{1,0:T(8,128)(2,1)S(1)} collective-permute-done((bf16[1056,128]{1,0:T(8,128)(2,1)S(1)}, bf16[1056,128]{1,0:T(8,128)(2,1)S(1)}, u32[]{:S(2)}, u32[]{:S(2)}) %collective-permute-start.6) | collective-permute-done | bytes 270368 | tf_op jit(solution)/shard_map/att_w_z3/ppermute | solution.py:450
  44.7 13.9 %collective-permute-done.1 = bf16[3,80,1024]{2,1,0:T(8,128)(2,1)} collective-permute-done((bf16[3,80,1024]{2,1,0:T(8,128)(2,1)}, bf16[3,80,1024]{2,1,0:T(8,128)(2,1)}, u32[]{:S(2)}, u32[]{:S(2)}) %collective-permute-start.1) | collective-permute-done | bytes 491552 | tf_op jit(solution)/shard_map/tokens_route1/ppermute | solution.py:532
  59.9 10.7 %collective-permute-start.21 = (bf16[2,256,512]{2,1,0:T(8,128)(2,1)S(1)}, bf16[2,256,512]{2,1,0:T(8,128)(2,1)S(1)}, u32[]{:S(2)}, u32[]{:S(2)}) collective-permute-start(bf16[2,256,512]{2,1,0:T(8,128)(2,1)S(1)} %bitcast.319), channel_id=1, source_target_pairs={{0,2},{1,3},{2,0},{3,1},{4,6},{5,7},{6,4},{7,5},{8,10},{9,11},{10,... | collective-permute-start | bytes 1572872 | tf_op jit(solution)/shard_map/ffn_w_z2/ppermute | solution.py:450
  70.6 2.3 pad_maximum_fusion.14
  80.7 7.7 %collective-permute-done.9 = bf16[2,1056,128]{2,1,0:T(8,128)(2,1)S(1)} collective-permute-done((bf16[2,1056,128]{2,1,0:T(8,128)(2,1)S(1)}, bf16[2,1056,128]{2,1,0:T(8,128)(2,1)S(1)}, u32[]{:S(2)}, u32[]{:S(2)}) %collective-permute-start.9) | collective-permute-done | bytes 540704 | tf_op jit(solution)/shard_map/att_w_y2/ppermute | solution.py:450
  88.4 2.4 collective-permute-done.10
  90.8 19.8 %att_forward.1 = (bf16[960,1024]{1,0:T(8,128)(2,1)S(1)}, bf16[12,960,128]{2,1,0:T(8,128)(2,1)S(1)}, bf16[960,512]{1,0:T(8,128)(2,1)S(1)}, bf16[960,1024]{1,0:T(8,128)(2,1)}) custom-call(bf16[3,320,1024]{2,1,0:T(8,128)(2,1)S(1)} %bitcast.298, f32[1,1024]{1,0:T(1,128)S(1)} %get-tuple-element.150.g_ref, f32[1,1024]{1,0:T(1,128)S(1)} %get-tuple-element.148.c_ref, ...), custom_call_target="tpu_custom_call" | custom-call | flops 8000000000 | bytes 20000000 | tf_op jit(solution)/shard_map/att_forward/pallas_call | solution.py:129
  115.8 2.2 pad_maximum_fusion.3
  121.2 7.7 %collective-permute-done.22 = bf16[2,256,512]{2,1,0:T(8,128)(2,1)S(1)} collective-permute-done((bf16[2,256,512]{2,1,0:T(8,128)(2,1)S(1)}, bf16[2,256,512]{2,1,0:T(8,128)(2,1)S(1)}, u32[]{:S(2)}, u32[]{:S(2)}) %collective-permute-start.22) | collective-permute-done | bytes 524320 | tf_op jit(solution)/shard_map/ffn_w_z3/ppermute | solution.py:450
  134.2 9.8 %collective-permute-done.17 = bf16[2,2,256,512]{3,2,1,0:T(8,128)(2,1)S(1)} collective-permute-done((bf16[2,2,256,512]{3,2,1,0:T(8,128)(2,1)S(1)}, bf16[2,2,256,512]{3,2,1,0:T(8,128)(2,1)S(1)}, u32[]{:S(2)}, u32[]{:S(2)}) %collective-permute-start.17) | collective-permute-done | bytes 1048608 | tf_op jit(solution)/shard_map/ffn_w0_x1/ppermute | solution.py:450
  148.1 18.3 %collective-permute-done.23 = bf16[2,2,256,512]{3,2,1,0:T(8,128)(2,1)S(1)} collective-permute-done((bf16[2,2,256,512]{3,2,1,0:T(8,128)(2,1)S(1)}, bf16[2,2,256,512]{3,2,1,0:T(8,128)(2,1)S(1)}, u32[]{:S(2)}, u32[]{:S(2)}) %collective-permute-start.23) | collective-permute-done | bytes 1048608 | tf_op jit(solution)/shard_map/ffn_w2_x1/ppermute | solution.py:450
  168.7 10.5 %collective-permute-done.19 = bf16[1,2,256,512]{3,2,1,0:T(8,128)(2,1)S(1)} collective-permute-done((bf16[1,2,256,512]{3,2,1,0:T(8,128)(2,1)S(1)}, bf16[1,2,256,512]{3,2,1,0:T(8,128)(2,1)S(1)}, u32[]{:S(2)}, u32[]{:S(2)}) %collective-permute-start.19) | collective-permute-done | bytes 524320 | tf_op jit(solution)/shard_map/ffn_w0_y2/ppermute | solution.py:450
  180.8 28.5 %ffn_first.1 = (f32[960,1024]{1,0:T(8,128)}, bf16[960,1024]{1,0:T(8,128)(2,1)}, bf16[1024,960]{1,0:T(8,128)(2,1)}, bf16[1024,960]{1,0:T(8,128)(2,1)}, f32[960,10...) custom-call(bf16[960,1024]{1,0:T(8,128)(2,1)} %bitcast.299, ...), custom_call_target="tpu_custom_call" | custom-call | flops 17999998976 | bytes 30000000 | tf_op jit(solution)/shard_map/ffn_first/pallas_call | solution.py:288
  209.3 2.9 slice_bitcast_fusion.11
  213.3 24.5 %ffn_last.1 = (bf16[960,1024]{1,0:T(8,128)(2,1)}, bf16[960,1024]{1,0:T(8,128)(2,1)}, bf16[4,2,2,256,512]{4,3,2,1,0:T(8,128)(2,1)}, f32[2,512]{1,0:T(2,128)}) custom-call(bf16[960,1024]{1,0:T(8,128)(2,1)} %get-tuple-element.34.refs_0_, bf16[1024,960]{1,0:T(8,128)(2,1)} %get-tuple-element.35.refs_1_, bf16[1024,960]{1,0:T(8,128)(2,1)} %get-tuple-element.36.refs_2_, ...), custom_call_target="tpu_custom_call" | custom-call | flops 17999998976 | bytes 30000000 | tf_op jit(solution)/shard_map/ffn_last/pallas_call | solution.py:288
  237.8 2.8 slice_bitcast_fusion.7
  245.7 1.8 fusion.26
  249.6 1.8 fusion.18
  251.8 1.9 collective-permute-done.52
  254.5 2.0 collective-permute-done.54
  257.6 1.8 fusion.22
  261.7 6.8 %collective-permute-done.28 = bf16[3,80,1024]{2,1,0:T(8,128)(2,1)S(1)} collective-permute-done((bf16[3,80,1024]{2,1,0:T(8,128)(2,1)S(1)}, bf16[3,80,1024]{2,1,0:T(8,128)(2,1)S(1)}, u32[]{:S(2)}, u32[]{:S(2)}) %collective-permute-start.28) | collective-permute-done | bytes 491552 | tf_op jit(solution)/shard_map/block_out_route1/ppermute | solution.py:542
  272.2 6.7 %collective-permute-done.48 = bf16[2,2,256,512]{3,2,1,0:T(8,128)(2,1)S(1)} collective-permute-done((bf16[2,2,256,512]{3,2,1,0:T(8,128)(2,1)S(1)}, bf16[2,2,256,512]{3,2,1,0:T(8,128)(2,1)S(1)}, u32[]{:S(2)}, u32[]{:S(2)}) %collective-permute-start.48) | collective-permute-done | bytes 1048608 | tf_op jit(solution)/shard_map/ffn_g0_x2/ppermute | solution.py:450
  278.9 1.6 fusion.7
  283.1 39.4 %att_backward.1 = (f32[960,1024]{1,0:T(8,128)}, bf16[960,1024]{1,0:T(8,128)(2,1)}, bf16[4,4,4,256,128]{4,3,2,1,0:T(8,128)(2,1)}, f32[1,1536]{1,0:T(1,128)}, f32[8,1024]{1,0:T(8,128)}) custom-call(s32[4]{0:T(128)} %copy-done.8, bf16[960,1024]{1,0:T(8,128)(2,1)} %bitcast.300, f32[960,1024]{1,0:T(8,128)} %get-tuple-element.33.hid_ref, ...), custom_call_target="tpu_custom_call" | custom-call | flops 20000000000 | bytes 40000000 | tf_op jit(solution)/shard_map/att_backward/pallas_call | solution.py:421
  324.4 3.6 collective-permute-start.34
  327.9 2.0 fusion.5
  330.9 2.0 collective-permute-start.56
  332.9 2.7 collective-permute-done.35
  337.1 2.0 collective-permute-start.39
  343.0 6.7 %collective-permute-done.37 = f32[112,128]{1,0:T(8,128)S(1)} collective-permute-done((f32[112,128]{1,0:T(8,128)S(1)}, f32[112,128]{1,0:T(8,128)S(1)}, u32[]{:S(2)}, u32[]{:S(2)}) %collective-permute-start.37) | collective-permute-done | bytes 57376 | tf_op jit(solution)/shard_map/sums_dp2/ppermute | solution.py:450
  351.9 2.1 collective-permute-start.57
  357.9 2.6 fusion.28
  360.5 18.1 %collective-permute-done.57 = bf16[2,256,512]{2,1,0:T(8,128)(2,1)} collective-permute-done((bf16[2,256,512]{2,1,0:T(8,128)(2,1)}, bf16[2,256,512]{2,1,0:T(8,128)(2,1)}, u32[]{:S(2)}, u32[]{:S(2)}) %collective-permute-start.57) | collective-permute-done | bytes 524320 | tf_op jit(solution)/shard_map/ffn_g_z2/ppermute | solution.py:450
  380.8 1.8 copy.68
  382.6 2.3 pad_maximum_fusion.5
  390.0 2.2 fusion.19
  392.3 2.1 fusion.14
  395.6 15.2 %collective-permute-done.40 = bf16[4,4,256,128]{3,2,1,0:T(8,128)(2,1)} collective-permute-done((bf16[4,4,256,128]{3,2,1,0:T(8,128)(2,1)}, bf16[4,4,256,128]{3,2,1,0:T(8,128)(2,1)}, u32[]{:S(2)}, u32[]{:S(2)}) %collective-permute-start.40) | collective-permute-done | bytes 1048608 | tf_op jit(solution)/shard_map/att_g_x2/ppermute | solution.py:450
  410.8 2.3 collective-permute-done.42
  413.0 2.3 fusion.9
  418.0 2.0 collective-permute-start.43
  420.0 5.7 %collective-permute-done.44 = bf16[4,256,128]{2,1,0:T(8,128)(2,1)} collective-permute-done((bf16[4,256,128]{2,1,0:T(8,128)(2,1)}, bf16[4,256,128]{2,1,0:T(8,128)(2,1)}, u32[]{:S(2)}, u32[]{:S(2)}) %collective-permute-start.44) | collective-permute-done | bytes 262176 | tf_op jit(solution)/shard_map/att_g_z3/ppermute | solution.py:450
  427.1 4.8 %collective-permute-done.43 = bf16[4,256,128]{2,1,0:T(8,128)(2,1)S(1)} collective-permute-done((bf16[4,256,128]{2,1,0:T(8,128)(2,1)}, bf16[4,256,128]{2,1,0:T(8,128)(2,1)S(1)}, u32[]{:S(2)}, u32[]{:S(2)}) %collective-permute-start.43) | collective-permute-done | bytes 262176 | tf_op jit(solution)/shard_map/att_g_z1/ppermute | solution.py:450
  431.9 6.4 %collective-permute-done.45 = bf16[4,256,128]{2,1,0:T(8,128)(2,1)S(1)} collective-permute-done((bf16[4,256,128]{2,1,0:T(8,128)(2,1)S(1)}, bf16[4,256,128]{2,1,0:T(8,128)(2,1)S(1)}, u32[]{:S(2)}, u32[]{:S(2)}) %collective-permute-start.45) | collective-permute-done | bytes 262176 | tf_op jit(solution)/shard_map/att_g_z2/ppermute | solution.py:450
  (321 shorter events, 97.3 us)
Async XLA Ops:
  6.0 35.8 %collective-permute-start.15 = (bf16[2,128,512]{1,2,0:T(8,128)(2,1)S(1)}, bf16[2,128,512]{1,2,0:T(8,128)(2,1)S(1)}, u32[]{:S(2)}, u32[]{:S(2)}) collective-permute-start(bf16[2,128,512]{1,2,0:T(8,128)(2,1)S(1)} %fusion.34), channel_id=1, source_target_pairs={{0,4},{4,0},{8,12},{12,8},{16,20},{20,16},{24,28},{28,24},{1,5},{5... | collective-permute-start | bytes 786440 | tf_op jit(solution)/shard_map/ffn_w_core/ppermute | solution.py:450
  7.8 16.7 %collective-permute-start.5 = (bf16[1056,128]{1,0:T(8,128)(2,1)S(1)}, bf16[1056,128]{1,0:T(8,128)(2,1)S(1)}, u32[]{:S(2)}, u32[]{:S(2)}) collective-permute-start(bf16[1056,128]{1,0:T(8,128)(2,1)S(1)} %get-tuple-element.130), channel_id=1, source_target_pairs={{0,2},{1,3},{2,0},{3,1},{4,6},{5,7},{6,4},{7,5},{8,10},{9,11},{10,... | collective-permute-start | bytes 811016 | tf_op jit(solution)/shard_map/att_w_z2/ppermute | solution.py:450
  11.9 20.6 %collective-permute-start.4 = (bf16[1056,128]{1,0:T(8,128)(2,1)S(1)}, bf16[1056,128]{1,0:T(8,128)(2,1)S(1)}, u32[]{:S(2)}, u32[]{:S(2)}) collective-permute-start(bf16[1056,128]{1,0:T(8,128)(2,1)S(1)} %get-tuple-element.130), channel_id=1, source_target_pairs={{0,1},{1,0},{2,3},{3,2},{4,5},{5,4},{6,7},{7,6},{8,9},{9,8},{10,11... | collective-permute-start | bytes 811016 | tf_op jit(solution)/shard_map/att_w_z1/ppermute | solution.py:450
  14.9 27.8 %collective-permute-start = (bf16[3,80,1024]{2,1,0:T(8,128)(2,1)S(1)}, bf16[3,80,1024]{2,1,0:T(8,128)(2,1)S(1)}, u32[]{:S(2)}, u32[]{:S(2)}) collective-permute-start(bf16[3,80,1024]{2,1,0:T(8,128)(2,1)S(1)} %get-tuple-element.113), channel_id=1, source_target_pairs={{0,0},{1,1},{6,2},{7,3},{2,4},{3,5},{4,6},{5,7},{8,8},{9,9},{14,10... | collective-permute-start | bytes 1474568 | tf_op jit(solution)/shard_map/tokens_route0/ppermute | solution.py:532
  24.5 16.1 %collective-permute-start.6 = (bf16[1056,128]{1,0:T(8,128)(2,1)S(1)}, bf16[1056,128]{1,0:T(8,128)(2,1)S(1)}, u32[]{:S(2)}, u32[]{:S(2)}) collective-permute-start(bf16[1056,128]{1,0:T(8,128)(2,1)S(1)} %collective-permute-done.5), channel_id=1, source_target_pairs={{0,1},{1,0},{2,3},{3,2},{4,5},{5,4},{6,7},{7,6},{8,9},{9,8},{10,11... | collective-permute-start | bytes 811016 | tf_op jit(solution)/shard_map/att_w_z3/ppermute | solution.py:450
  26.9 32.9 %collective-permute-start.12 = (bf16[3,80,1024]{2,1,0:T(8,128)(2,1)}, bf16[3,80,1024]{2,1,0:T(8,128)(2,1)}, u32[]{:S(2)}, u32[]{:S(2)}) collective-permute-start(bf16[3,80,1024]{2,1,0:T(8,128)(2,1)} %get-tuple-element.107), channel_id=1, source_target_pairs={{0,0},{1,1},{6,2},{7,3},{2,4},{3,5},{4,6},{5,7},{8,8},{9,9},{14,10... | collective-permute-start | bytes 1474568 | tf_op jit(solution)/shard_map/cotangent_route0/ppermute | solution.py:532
  32.5 38.1 %collective-permute-start.13 = (bf16[3,80,1024]{2,1,0:T(8,128)(2,1)}, bf16[3,80,1024]{2,1,0:T(8,128)(2,1)}, u32[]{:S(2)}, u32[]{:S(2)}) collective-permute-start(bf16[3,80,1024]{2,1,0:T(8,128)(2,1)} %get-tuple-element.108), channel_id=1, source_target_pairs={{1,0},{0,1},{7,2},{6,3},{3,4},{2,5},{5,6},{4,7},{9,8},{8,9},{15,10... | collective-permute-start | bytes 1474568 | tf_op jit(solution)/shard_map/cotangent_route1/ppermute | solution.py:532
  40.6 18.0 %collective-permute-start.1 = (bf16[3,80,1024]{2,1,0:T(8,128)(2,1)}, bf16[3,80,1024]{2,1,0:T(8,128)(2,1)}, u32[]{:S(2)}, u32[]{:S(2)}) collective-permute-start(bf16[3,80,1024]{2,1,0:T(8,128)(2,1)} %get-tuple-element.114), channel_id=1, source_target_pairs={{1,0},{0,1},{7,2},{6,3},{3,4},{2,5},{5,6},{4,7},{9,8},{8,9},{15,10... | collective-permute-start | bytes 1474568 | tf_op jit(solution)/shard_map/tokens_route1/ppermute | solution.py:532
  41.8 31.9 %collective-permute-start.7 = (bf16[4,1056,128]{2,1,0:T(8,128)(2,1)}, bf16[4,1056,128]{2,1,0:T(8,128)(2,1)S(1)}, u32[]{:S(2)}, u32[]{:S(2)}) collective-permute-start(bf16[4,1056,128]{2,1,0:T(8,128)(2,1)} %get-tuple-element.82), channel_id=1, source_target_pairs={{0,8},{4,12},{8,0},{12,4},{16,24},{20,28},{24,16},{28,20},{1,9},{5... | collective-permute-start | bytes 3244040 | tf_op jit(solution)/shard_map/att_w_x1/ppermute | solution.py:450
  42.7 32.6 %collective-permute-start.8 = (bf16[4,1056,128]{2,1,0:T(8,128)(2,1)}, bf16[4,1056,128]{2,1,0:T(8,128)(2,1)}, u32[]{:S(2)}, u32[]{:S(2)}) collective-permute-start(bf16[4,1056,128]{2,1,0:T(8,128)(2,1)} %get-tuple-element.82), channel_id=1, source_target_pairs={{0,16},{4,20},{8,24},{12,28},{16,0},{20,4},{24,8},{28,12},{1,17},{... | collective-permute-start | bytes 3244040 | tf_op jit(solution)/shard_map/att_w_y1/ppermute | solution.py:450
  58.6 57.3 %collective-permute-start.16 = (bf16[2,256,512]{2,1,0:T(8,128)(2,1)S(1)}, bf16[2,256,512]{2,1,0:T(8,128)(2,1)}, u32[]{:S(2)}, u32[]{:S(2)}) collective-permute-start(bf16[2,256,512]{2,1,0:T(8,128)(2,1)S(1)} %bitcast.318), channel_id=1, source_target_pairs={{0,1},{1,0},{2,3},{3,2},{4,5},{5,4},{6,7},{7,6},{8,9},{9,8},{10,11... | collective-permute-start | bytes 1572872 | tf_op jit(solution)/shard_map/ffn_w_z1/ppermute | solution.py:450
  59.9 54.7 %collective-permute-start.21 = (bf16[2,256,512]{2,1,0:T(8,128)(2,1)S(1)}, bf16[2,256,512]{2,1,0:T(8,128)(2,1)S(1)}, u32[]{:S(2)}, u32[]{:S(2)}) collective-permute-start(bf16[2,256,512]{2,1,0:T(8,128)(2,1)S(1)} %bitcast.319), channel_id=1, source_target_pairs={{0,2},{1,3},{2,0},{3,1},{4,6},{5,7},{6,4},{7,5},{8,10},{9,11},{10,... | collective-permute-start | bytes 1572872 | tf_op jit(solution)/shard_map/ffn_w_z2/ppermute | solution.py:450
  73.7 14.7 %collective-permute-start.9 = (bf16[2,1056,128]{2,1,0:T(8,128)(2,1)S(1)}, bf16[2,1056,128]{2,1,0:T(8,128)(2,1)S(1)}, u32[]{:S(2)}, u32[]{:S(2)}) collective-permute-start(bf16[2,1056,128]{2,1,0:T(8,128)(2,1)S(1)} %slice.369), channel_id=1, source_target_pairs={{0,16},{4,20},{8,24},{12,28},{16,0},{20,4},{24,8},{28,12},{1,17},{... | collective-permute-start | bytes 1622024 | tf_op jit(solution)/shard_map/att_w_y2/ppermute | solution.py:450
  76.4 14.5 %collective-permute-start.10 = (bf16[2,1056,128]{2,1,0:T(8,128)(2,1)S(1)}, bf16[2,1056,128]{2,1,0:T(8,128)(2,1)S(1)}, u32[]{:S(2)}, u32[]{:S(2)}) collective-permute-start(bf16[2,1056,128]{2,1,0:T(8,128)(2,1)S(1)} %slice.370), channel_id=1, source_target_pairs={{0,8},{4,12},{8,0},{12,4},{16,24},{20,28},{24,16},{28,20},{1,9},{5... | collective-permute-start | bytes 1622024 | tf_op jit(solution)/shard_map/att_w_x2/ppermute | solution.py:450
  77.9 54.0 %collective-permute-start.14 = (bf16[3,2,80,1024]{3,2,1,0:T(8,128)(2,1)}, bf16[3,2,80,1024]{3,2,1,0:T(8,128)(2,1)}, u32[]{:S(2)}, u32[]{:S(2)}) collective-permute-start(bf16[3,2,80,1024]{3,2,1,0:T(8,128)(2,1)} %pad_maximum_fusion.14), channel_id=1, source_target_pairs={{0,4},{4,0},{8,12},{12,8},{16,20},{20,16},{24,28},{28,24},{1,5},{5... | collective-permute-start | bytes 2949128 | tf_op jit(solution)/shard_map/cotangent_core/ppermute | solution.py:450
  114.6 65.5 %collective-permute-start.11 = (bf16[960,1024]{1,0:T(8,128)(2,1)}, bf16[960,1024]{1,0:T(8,128)(2,1)}, u32[]{:S(2)}, u32[]{:S(2)}) collective-permute-start(bf16[960,1024]{1,0:T(8,128)(2,1)} %get-tuple-element.32.refs_1_), channel_id=1, source_target_pairs={{0,4},{4,0},{8,12},{12,8},{16,20},{20,16},{24,28},{28,24},{1,5},{5... | collective-permute-start | bytes 5898248 | tf_op jit(solution)/shard_map/attended/ppermute | solution.py:450
  114.6 14.4 %collective-permute-start.22 = (bf16[2,256,512]{2,1,0:T(8,128)(2,1)S(1)}, bf16[2,256,512]{2,1,0:T(8,128)(2,1)S(1)}, u32[]{:S(2)}, u32[]{:S(2)}) collective-permute-start(bf16[2,256,512]{2,1,0:T(8,128)(2,1)S(1)} %collective-permute-done.21), channel_id=1, source_target_pairs={{0,1},{1,0},{2,3},{3,2},{4,5},{5,4},{6,7},{7,6},{8,9},{9,8},{10,11... | collective-permute-start | bytes 1572872 | tf_op jit(solution)/shard_map/ffn_w_z3/ppermute | solution.py:450
  118.0 26.0 %collective-permute-start.17 = (bf16[2,2,256,512]{3,2,1,0:T(8,128)(2,1)S(1)}, bf16[2,2,256,512]{3,2,1,0:T(8,128)(2,1)S(1)}, u32[]{:S(2)}, u32[]{:S(2)}) collective-permute-start(bf16[2,2,256,512]{3,2,1,0:T(8,128)(2,1)S(1)} %get-tuple-element.89), channel_id=1, source_target_pairs={{0,8},{4,12},{8,0},{12,4},{16,24},{20,28},{24,16},{28,20},{1,9},{5... | collective-permute-start | bytes 3145736 | tf_op jit(solution)/shard_map/ffn_w0_x1/ppermute | solution.py:450
  119.5 26.0 %collective-permute-start.18 = (bf16[2,2,256,512]{3,2,1,0:T(8,128)(2,1)S(1)}, bf16[2,2,256,512]{3,2,1,0:T(8,128)(2,1)S(1)}, u32[]{:S(2)}, u32[]{:S(2)}) collective-permute-start(bf16[2,2,256,512]{3,2,1,0:T(8,128)(2,1)S(1)} %get-tuple-element.89), channel_id=1, source_target_pairs={{0,16},{4,20},{8,24},{12,28},{16,0},{20,4},{24,8},{28,12},{1,17},{... | collective-permute-start | bytes 3145736 | tf_op jit(solution)/shard_map/ffn_w0_y1/ppermute | solution.py:450
  130.1 36.4 %collective-permute-start.23 = (bf16[2,2,256,512]{3,2,1,0:T(8,128)(2,1)S(1)}, bf16[2,2,256,512]{3,2,1,0:T(8,128)(2,1)S(1)}, u32[]{:S(2)}, u32[]{:S(2)}) collective-permute-start(bf16[2,2,256,512]{3,2,1,0:T(8,128)(2,1)S(1)} %get-tuple-element.87), channel_id=1, source_target_pairs={{0,8},{4,12},{8,0},{12,4},{16,24},{20,28},{24,16},{28,20},{1,9},{5... | collective-permute-start | bytes 3145736 | tf_op jit(solution)/shard_map/ffn_w2_x1/ppermute | solution.py:450
  132.0 36.0 %collective-permute-start.24 = (bf16[2,2,256,512]{3,2,1,0:T(8,128)(2,1)S(1)}, bf16[2,2,256,512]{3,2,1,0:T(8,128)(2,1)S(1)}, u32[]{:S(2)}, u32[]{:S(2)}) collective-permute-start(bf16[2,2,256,512]{3,2,1,0:T(8,128)(2,1)S(1)} %get-tuple-element.87), channel_id=1, source_target_pairs={{0,16},{4,20},{8,24},{12,28},{16,0},{20,4},{24,8},{28,12},{1,17},{... | collective-permute-start | bytes 3145736 | tf_op jit(solution)/shard_map/ffn_w2_y1/ppermute | solution.py:450
  144.0 35.2 %collective-permute-start.19 = (bf16[1,2,256,512]{3,2,1,0:T(8,128)(2,1)S(1)}, bf16[1,2,256,512]{3,2,1,0:T(8,128)(2,1)S(1)}, u32[]{:S(2)}, u32[]{:S(2)}) collective-permute-start(bf16[1,2,256,512]{3,2,1,0:T(8,128)(2,1)S(1)} %slice.375), channel_id=1, source_target_pairs={{0,16},{4,20},{8,24},{12,28},{16,0},{20,4},{24,8},{28,12},{1,17},{... | collective-permute-start | bytes 1572872 | tf_op jit(solution)/shard_map/ffn_w0_y2/ppermute | solution.py:450
  145.6 33.7 %collective-permute-start.20 = (bf16[1,2,256,512]{3,2,1,0:T(8,128)(2,1)S(1)}, bf16[1,2,256,512]{3,2,1,0:T(8,128)(2,1)S(1)}, u32[]{:S(2)}, u32[]{:S(2)}) collective-permute-start(bf16[1,2,256,512]{3,2,1,0:T(8,128)(2,1)S(1)} %slice.376), channel_id=1, source_target_pairs={{0,8},{4,12},{8,0},{12,4},{16,24},{20,28},{24,16},{28,20},{1,9},{5... | collective-permute-start | bytes 1572872 | tf_op jit(solution)/shard_map/ffn_w0_x2/ppermute | solution.py:450
  166.5 46.8 %collective-permute-start.25 = (bf16[1,2,256,512]{3,2,1,0:T(8,128)(2,1)S(1)}, bf16[1,2,256,512]{3,2,1,0:T(8,128)(2,1)}, u32[]{:S(2)}, u32[]{:S(2)}) collective-permute-start(bf16[1,2,256,512]{3,2,1,0:T(8,128)(2,1)S(1)} %slice.378), channel_id=1, source_target_pairs={{0,16},{4,20},{8,24},{12,28},{16,0},{20,4},{24,8},{28,12},{1,17},{... | collective-permute-start | bytes 1572872 | tf_op jit(solution)/shard_map/ffn_w2_y2/ppermute | solution.py:450
  168.0 45.3 %collective-permute-start.26 = (bf16[1,2,256,512]{3,2,1,0:T(8,128)(2,1)S(1)}, bf16[1,2,256,512]{3,2,1,0:T(8,128)(2,1)}, u32[]{:S(2)}, u32[]{:S(2)}) collective-permute-start(bf16[1,2,256,512]{3,2,1,0:T(8,128)(2,1)S(1)} %slice.379), channel_id=1, source_target_pairs={{0,8},{4,12},{8,0},{12,4},{16,24},{20,28},{24,16},{28,20},{1,9},{5... | collective-permute-start | bytes 1572872 | tf_op jit(solution)/shard_map/ffn_w2_x2/ppermute | solution.py:450
  212.2 32.9 %collective-permute-start.47 = (bf16[1,2,256,512]{3,2,1,0:T(8,128)(2,1)}, bf16[1,2,256,512]{3,2,1,0:T(8,128)(2,1)}, u32[]{:S(2)}, u32[]{:S(2)}) collective-permute-start(bf16[1,2,256,512]{3,2,1,0:T(8,128)(2,1)} %get-tuple-element.57), channel_id=1, source_target_pairs={{0,16},{4,20},{8,24},{12,28},{16,0},{20,4},{24,8},{28,12},{1,17},{... | collective-permute-start | bytes 1572872 | tf_op jit(solution)/shard_map/ffn_g0_y1/ppermute | solution.py:450
  212.8 32.9 %collective-permute-start.49 = (bf16[1,2,256,512]{3,2,1,0:T(8,128)(2,1)}, bf16[1,2,256,512]{3,2,1,0:T(8,128)(2,1)}, u32[]{:S(2)}, u32[]{:S(2)}) collective-permute-start(bf16[1,2,256,512]{3,2,1,0:T(8,128)(2,1)} %get-tuple-element.58), channel_id=1, source_target_pairs={{0,8},{4,12},{8,0},{12,4},{16,24},{20,28},{24,16},{28,20},{1,9},{5... | collective-permute-start | bytes 1572872 | tf_op jit(solution)/shard_map/ffn_g0_x1/ppermute | solution.py:450
  240.7 13.0 %collective-permute-start.52 = (bf16[1,2,256,512]{3,2,1,0:T(8,128)(2,1)}, bf16[1,2,256,512]{3,2,1,0:T(8,128)(2,1)}, u32[]{:S(2)}, u32[]{:S(2)}) collective-permute-start(bf16[1,2,256,512]{3,2,1,0:T(8,128)(2,1)} %get-tuple-element.63), channel_id=1, source_target_pairs={{0,16},{4,20},{8,24},{12,28},{16,0},{20,4},{24,8},{28,12},{1,17},{... | collective-permute-start | bytes 1572872 | tf_op jit(solution)/shard_map/ffn_g2_y1/ppermute | solution.py:450
  242.1 14.3 %collective-permute-start.54 = (bf16[1,2,256,512]{3,2,1,0:T(8,128)(2,1)}, bf16[1,2,256,512]{3,2,1,0:T(8,128)(2,1)}, u32[]{:S(2)}, u32[]{:S(2)}) collective-permute-start(bf16[1,2,256,512]{3,2,1,0:T(8,128)(2,1)} %get-tuple-element.64), channel_id=1, source_target_pairs={{0,8},{4,12},{8,0},{12,4},{16,24},{20,28},{24,16},{28,20},{1,9},{5... | collective-permute-start | bytes 1572872 | tf_op jit(solution)/shard_map/ffn_g2_x1/ppermute | solution.py:450
  245.1 38.0 %collective-permute-start.30 = (bf16[960,1024]{1,0:T(8,128)(2,1)}, bf16[960,1024]{1,0:T(8,128)(2,1)}, u32[]{:S(2)}, u32[]{:S(2)}) collective-permute-start(bf16[960,1024]{1,0:T(8,128)(2,1)} %get-tuple-element.40.ga_ref), channel_id=1, source_target_pairs={{0,4},{4,0},{8,12},{12,8},{16,20},{20,16},{24,28},{28,24},{1,5},{5... | collective-permute-start | bytes 5898248 | tf_op jit(solution)/shard_map/grad_norm_two/ppermute | solution.py:450
  247.6 31.2 %collective-permute-start.48 = (bf16[2,2,256,512]{3,2,1,0:T(8,128)(2,1)S(1)}, bf16[2,2,256,512]{3,2,1,0:T(8,128)(2,1)S(1)}, u32[]{:S(2)}, u32[]{:S(2)}) collective-permute-start(bf16[2,2,256,512]{3,2,1,0:T(8,128)(2,1)S(1)} %pad_maximum_fusion.7), channel_id=1, source_target_pairs={{0,8},{4,12},{8,0},{12,4},{16,24},{20,28},{24,16},{28,20},{1,9},{5... | collective-permute-start | bytes 3145736 | tf_op jit(solution)/shard_map/ffn_g0_x2/ppermute | solution.py:450
  248.3 30.5 %collective-permute-start.50 = (bf16[2,2,256,512]{3,2,1,0:T(8,128)(2,1)S(1)}, bf16[2,2,256,512]{3,2,1,0:T(8,128)(2,1)S(1)}, u32[]{:S(2)}, u32[]{:S(2)}) collective-permute-start(bf16[2,2,256,512]{3,2,1,0:T(8,128)(2,1)S(1)} %pad_maximum_fusion.8), channel_id=1, source_target_pairs={{0,16},{4,20},{8,24},{12,28},{16,0},{20,4},{24,8},{28,12},{1,17},{... | collective-permute-start | bytes 3145736 | tf_op jit(solution)/shard_map/ffn_g0_y2/ppermute | solution.py:450
  253.6 14.8 %collective-permute-start.28 = (bf16[3,80,1024]{2,1,0:T(8,128)(2,1)S(1)}, bf16[3,80,1024]{2,1,0:T(8,128)(2,1)S(1)}, u32[]{:S(2)}, u32[]{:S(2)}) collective-permute-start(bf16[3,80,1024]{2,1,0:T(8,128)(2,1)S(1)} %get-tuple-element.101), channel_id=1, source_target_pairs={{0,1},{1,0},{2,7},{3,6},{4,3},{5,2},{6,5},{7,4},{8,9},{9,8},{10,15... | collective-permute-start | bytes 1474568 | tf_op jit(solution)/shard_map/block_out_route1/ppermute | solution.py:542
  256.5 13.1 %collective-permute-start.29 = (bf16[3,80,1024]{2,1,0:T(8,128)(2,1)S(1)}, bf16[3,80,1024]{2,1,0:T(8,128)(2,1)S(1)}, u32[]{:S(2)}, u32[]{:S(2)}) collective-permute-start(bf16[3,80,1024]{2,1,0:T(8,128)(2,1)S(1)} %get-tuple-element.102), channel_id=1, source_target_pairs={{0,0},{1,1},{2,6},{3,7},{4,2},{5,3},{6,4},{7,5},{8,8},{9,9},{10,14... | collective-permute-start | bytes 1474568 | tf_op jit(solution)/shard_map/block_out_route0/ppermute | solution.py:542
  268.5 59.5 %collective-permute-start.53 = (bf16[2,2,256,512]{3,2,1,0:T(8,128)(2,1)}, bf16[2,2,256,512]{3,2,1,0:T(8,128)(2,1)S(1)}, u32[]{:S(2)}, u32[]{:S(2)}) collective-permute-start(bf16[2,2,256,512]{3,2,1,0:T(8,128)(2,1)} %pad_maximum_fusion.9), channel_id=1, source_target_pairs={{0,8},{4,12},{8,0},{12,4},{16,24},{20,28},{24,16},{28,20},{1,9},{5... | collective-permute-start | bytes 3145736 | tf_op jit(solution)/shard_map/ffn_g2_x2/ppermute | solution.py:450
  269.6 58.3 %collective-permute-start.55 = (bf16[2,2,256,512]{3,2,1,0:T(8,128)(2,1)}, bf16[2,2,256,512]{3,2,1,0:T(8,128)(2,1)}, u32[]{:S(2)}, u32[]{:S(2)}) collective-permute-start(bf16[2,2,256,512]{3,2,1,0:T(8,128)(2,1)} %pad_maximum_fusion.10), channel_id=1, source_target_pairs={{0,16},{4,20},{8,24},{12,28},{16,0},{20,4},{24,8},{28,12},{1,17},{... | collective-permute-start | bytes 3145736 | tf_op jit(solution)/shard_map/ffn_g2_y2/ppermute | solution.py:450
  282.3 78.2 %collective-permute-start.51 = (bf16[2,256,512]{2,1,0:T(8,128)(2,1)}, bf16[2,256,512]{2,1,0:T(8,128)(2,1)}, u32[]{:S(2)}, u32[]{:S(2)}) collective-permute-start(bf16[2,256,512]{2,1,0:T(8,128)(2,1)} %slice_bitcast_fusion.2), channel_id=1, source_target_pairs={{0,1},{1,0},{2,3},{3,2},{4,5},{5,4},{6,7},{7,6},{8,9},{9,8},{10,11... | collective-permute-start | bytes 1572872 | tf_op jit(solution)/shard_map/ffn_g_z1/ppermute | solution.py:450
  330.9 18.7 %collective-permute-start.56 = (bf16[2,256,512]{2,1,0:T(8,128)(2,1)S(1)}, bf16[2,256,512]{2,1,0:T(8,128)(2,1)S(1)}, u32[]{:S(2)}, u32[]{:S(2)}) collective-permute-start(bf16[2,256,512]{2,1,0:T(8,128)(2,1)S(1)} %slice_bitcast_fusion), channel_id=1, source_target_pairs={{0,1},{1,0},{2,3},{3,2},{4,5},{5,4},{6,7},{7,6},{8,9},{9,8},{10,11... | collective-permute-start | bytes 1572872 | tf_op jit(solution)/shard_map/ffn_g_z3/ppermute | solution.py:450
  337.1 20.0 %collective-permute-start.39 = (bf16[2,4,256,128]{3,2,1,0:T(8,128)(2,1)}, bf16[2,4,256,128]{3,2,1,0:T(8,128)(2,1)S(1)}, u32[]{:S(2)}, u32[]{:S(2)}) collective-permute-start(bf16[2,4,256,128]{3,2,1,0:T(8,128)(2,1)} %get-tuple-element.69), channel_id=1, source_target_pairs={{0,16},{4,20},{8,24},{12,28},{16,0},{20,4},{24,8},{28,12},{1,17},{... | collective-permute-start | bytes 1572872 | tf_op jit(solution)/shard_map/att_g_y1/ppermute | solution.py:450
  339.1 18.8 %collective-permute-start.41 = (bf16[2,4,256,128]{3,2,1,0:T(8,128)(2,1)}, bf16[2,4,256,128]{3,2,1,0:T(8,128)(2,1)}, u32[]{:S(2)}, u32[]{:S(2)}) collective-permute-start(bf16[2,4,256,128]{3,2,1,0:T(8,128)(2,1)} %get-tuple-element.70), channel_id=1, source_target_pairs={{0,8},{4,12},{8,0},{12,4},{16,24},{20,28},{24,16},{28,20},{1,9},{5... | collective-permute-start | bytes 1572872 | tf_op jit(solution)/shard_map/att_g_x1/ppermute | solution.py:450
  349.7 40.4 %collective-permute-start.31 = (bf16[3,2,80,1024]{3,2,0,1:T(8,128)(2,1)}, bf16[3,2,80,1024]{3,2,0,1:T(8,128)(2,1)}, u32[]{:S(2)}, u32[]{:S(2)}) collective-permute-start(bf16[3,2,80,1024]{3,2,0,1:T(8,128)(2,1)} %copy.76), channel_id=1, source_target_pairs={{0,4},{4,0},{8,12},{12,8},{16,20},{20,16},{24,28},{28,24},{1,5},{5... | collective-permute-start | bytes 2949128 | tf_op jit(solution)/shard_map/grad_norm_one/ppermute | solution.py:450
  351.9 26.7 %collective-permute-start.57 = (bf16[2,256,512]{2,1,0:T(8,128)(2,1)}, bf16[2,256,512]{2,1,0:T(8,128)(2,1)}, u32[]{:S(2)}, u32[]{:S(2)}) collective-permute-start(bf16[2,256,512]{2,1,0:T(8,128)(2,1)} %fusion.20), channel_id=1, source_target_pairs={{0,2},{1,3},{2,0},{3,1},{4,6},{5,7},{6,4},{7,5},{8,10},{9,11},{10,... | collective-permute-start | bytes 1572872 | tf_op jit(solution)/shard_map/ffn_g_z2/ppermute | solution.py:450
  385.0 25.8 %collective-permute-start.40 = (bf16[4,4,256,128]{3,2,1,0:T(8,128)(2,1)}, bf16[4,4,256,128]{3,2,1,0:T(8,128)(2,1)}, u32[]{:S(2)}, u32[]{:S(2)}) collective-permute-start(bf16[4,4,256,128]{3,2,1,0:T(8,128)(2,1)} %pad_maximum_fusion.5), channel_id=1, source_target_pairs={{0,8},{4,12},{8,0},{12,4},{16,24},{20,28},{24,16},{28,20},{1,9},{5... | collective-permute-start | bytes 3145736 | tf_op jit(solution)/shard_map/att_g_x2/ppermute | solution.py:450
  387.5 25.5 %collective-permute-start.42 = (bf16[4,4,256,128]{3,2,1,0:T(8,128)(2,1)}, bf16[4,4,256,128]{3,2,1,0:T(8,128)(2,1)}, u32[]{:S(2)}, u32[]{:S(2)}) collective-permute-start(bf16[4,4,256,128]{3,2,1,0:T(8,128)(2,1)} %pad_maximum_fusion.6), channel_id=1, source_target_pairs={{0,16},{4,20},{8,24},{12,28},{16,0},{20,4},{24,8},{28,12},{1,17},{... | collective-permute-start | bytes 3145736 | tf_op jit(solution)/shard_map/att_g_y2/ppermute | solution.py:450
  394.8 32.2 %collective-permute-start.32 = (bf16[3,80,1024]{2,1,0:T(8,128)(2,1)S(1)}, bf16[3,80,1024]{2,1,0:T(8,128)(2,1)S(1)}, u32[]{:S(2)}, u32[]{:S(2)}) collective-permute-start(bf16[3,80,1024]{2,1,0:T(8,128)(2,1)S(1)} %get-tuple-element.93), channel_id=1, source_target_pairs={{0,1},{1,0},{2,7},{3,6},{4,3},{5,2},{6,5},{7,4},{8,9},{9,8},{10,15... | collective-permute-start | bytes 1474568 | tf_op jit(solution)/shard_map/input_grad_route1/ppermute | solution.py:542
  394.9 32.1 %collective-permute-start.33 = (bf16[3,80,1024]{2,1,0:T(8,128)(2,1)S(1)}, bf16[3,80,1024]{2,1,0:T(8,128)(2,1)S(1)}, u32[]{:S(2)}, u32[]{:S(2)}) collective-permute-start(bf16[3,80,1024]{2,1,0:T(8,128)(2,1)S(1)} %get-tuple-element.94), channel_id=1, source_target_pairs={{0,0},{1,1},{2,6},{3,7},{4,2},{5,3},{6,4},{7,5},{8,8},{9,9},{10,14... | collective-permute-start | bytes 1474568 | tf_op jit(solution)/shard_map/input_grad_route0/ppermute | solution.py:542
  418.0 13.9 %collective-permute-start.43 = (bf16[4,256,128]{2,1,0:T(8,128)(2,1)}, bf16[4,256,128]{2,1,0:T(8,128)(2,1)S(1)}, u32[]{:S(2)}, u32[]{:S(2)}) collective-permute-start(bf16[4,256,128]{2,1,0:T(8,128)(2,1)} %get-tuple-element.85), channel_id=1, source_target_pairs={{0,1},{1,0},{2,3},{3,2},{4,5},{5,4},{6,7},{7,6},{8,9},{9,8},{10,11... | collective-permute-start | bytes 786440 | tf_op jit(solution)/shard_map/att_g_z1/ppermute | solution.py:450
  426.8 11.6 %collective-permute-start.45 = (bf16[4,256,128]{2,1,0:T(8,128)(2,1)S(1)}, bf16[4,256,128]{2,1,0:T(8,128)(2,1)S(1)}, u32[]{:S(2)}, u32[]{:S(2)}) collective-permute-start(bf16[4,256,128]{2,1,0:T(8,128)(2,1)S(1)} %fusion.30), channel_id=1, source_target_pairs={{0,2},{1,3},{2,0},{3,1},{4,6},{5,7},{6,4},{7,5},{8,10},{9,11},{10,... | collective-permute-start | bytes 786440 | tf_op jit(solution)/shard_map/att_g_z2/ppermute | solution.py:450
  (56 other events, 529.6 us)
